TPU v7x, 32 devices: a whole 2x2x4 slice. The times are simulated.
32 devices in a mesh: rep: 4 (over y, x), shard: 8 (over z, core).
Axes of the slice: x: 2, y: 2, z: 4, core: 2. Of those that a mesh axis runs over, the one named last changes fastest.
Arguments:
- hidden_in: bfloat16 [8192, 2048], P(('rep', 'shard')), may hold values from -6 to 6
- layer_vectors: bfloat16 [8192, 256], P(('rep', 'shard')), may hold values from -6 to 6
- positions: int32 [8192], P(('rep', 'shard')), may hold values from 0 to 2047, as said below
- cotangent: bfloat16 [8192, 2048], P(('rep', 'shard')), may hold values from -6 to 6
- model_gains: float32 [6, 2048], replicated, may hold values from 0.1 to 1.9
- head_gains: float32 [2, 256], replicated, may hold values from 0.1 to 1.9
- qkv_weight: bfloat16 [2048, 3072], P('shard'), may hold values from -0.125 to 0.125
- out_weight: bfloat16 [2048, 2048], P('shard'), may hold values from -0.125 to 0.125
- laurel_down: bfloat16 [2048, 64], P('shard'), may hold values from -0.125 to 0.125
- laurel_up: bfloat16 [2048, 64], P('shard'), may hold values from -0.75 to 0.75
- gate_up_weight: bfloat16 [2048, 16384], P('shard'), may hold values from -0.125 to 0.125
- down_weight: bfloat16 [2048, 8192], P('shard'), may hold values from -0.0625 to 0.0625
- layer_gate: bfloat16 [2048, 256], P('shard'), may hold values from -0.125 to 0.125
- layer_project: bfloat16 [2048, 256], P('shard'), may hold values from -0.375 to 0.375
Outputs:
- layer_out: bfloat16 [8192, 2048], P(('rep', 'shard'))
- grad_hidden: float32 [8192, 2048], P(('rep', 'shard'))
- grad_vectors: float32 [8192, 256], P(('rep', 'shard'))
- grad_model_gains: float32 [6, 2048], replicated
- grad_head_gains: float32 [2, 256], replicated
- grad_qkv: float32 [2048, 3072], P('shard')
- grad_out: float32 [2048, 2048], P('shard')
- grad_laurel_down: float32 [2048, 64], P('shard')
- grad_laurel_up: float32 [2048, 64], P('shard')
- grad_gate_up: float32 [2048, 16384], P('shard')
- grad_down: float32 [2048, 8192], P('shard')
- grad_layer_gate: float32 [2048, 256], P('shard')
- grad_layer_project: float32 [2048, 256], P('shard')
Inputs may be any that keep to these rules, and one draw needn't show every extreme that they name: positions count the tokens before each token in its own document: 0 at a document's first token, one more at each following one; every sequence of 2048 tokens begins with a document, and one sequence is a single document of 2048 tokens.
All inputs are finite; a program needn't handle non-finite values.
Results may differ from a plain program's by a relative error of at most 0.024.
Values may be sent and summed in bfloat16 or wider, within the bound.
No kernel may reach another device: no remote copies, remote signals or barrier semaphores. Data moves between devices by JAX's collectives and lax.ppermute only.
A program may use at most 768 MiB of HBM per device.

v0:
```python
import math

import jax
import jax.numpy as jnp
from jax import lax
from jax.sharding import PartitionSpec as P

WINDOW = 512


EPSILON = 1e-06
SQRT_HALF = 0.7071067811865476


def from_behind(value, axis, steps):
    count = lax.axis_size(axis)
    initial, last = (max(0, -steps), min(count, count - steps))
    return lax.ppermute(value, axis, [(source, source + steps) for source in range(initial, last)])


def scaled_norm(values, gain_row):
    return (
        values * lax.rsqrt(jnp.mean(values * values, axis=-1, keepdims=True) + EPSILON) * gain_row
    )


def rotate(values, cosine, sine_part):
    half_dim = values.shape[-1] // 2
    first_half = values[..., :half_dim]
    second_half = values[..., half_dim:]
    return jnp.concatenate(
        [
            first_half * cosine - second_half * sine_part,
            second_half * cosine + first_half * sine_part,
        ],
        axis=-1,
    )


def rope_tables(positions, head_dim):
    half_dim = head_dim // 2
    frequency = jnp.exp(
        jnp.arange(half_dim, dtype=jnp.float32) * (-2.0 * math.log(10000.0) / head_dim)
    )
    phase_angle = positions.astype(jnp.float32)[:, None] * frequency[None, :]
    return (jnp.cos(phase_angle)[:, None, :], jnp.sin(phase_angle)[:, None, :])


def dot_plain(left_side, right_side):
    return jnp.dot(left_side, right_side, preferred_element_type=jnp.float32)


def dot_right_t(left_side, right_side):
    return lax.dot_general(
        left_side, right_side, (((1,), (1,)), ((), ())), preferred_element_type=jnp.float32
    )


def dot_left_t(left_side, right_side):
    return lax.dot_general(
        left_side, right_side, (((0,), (0,)), ((), ())), preferred_element_type=jnp.float32
    )


def gelu_tanh(values):
    return jax.nn.gelu(values, approximate=True)


def make_terms(lefts, rights):
    return jnp.concatenate(
        [dot_left_t(left_side, right_side) for left_side, right_side in zip(lefts, rights)], axis=1
    )


def body(
    hidden_in,
    layer_vectors,
    positions,
    cotangent,
    model_gains,
    head_gains,
    qkv_weight,
    out_weight,
    laurel_down,
    laurel_up,
    gate_up_weight,
    down_weight,
    layer_gate,
    layer_project,
):
    token_rows = hidden_in.shape[0]
    head_dim = head_gains.shape[1]
    query_heads = out_weight.shape[1] // head_dim
    kv_heads = (qkv_weight.shape[1] // head_dim - query_heads) // 2
    group_size = query_heads // kv_heads
    ffn_units = down_weight.shape[1]
    score_scale = 1.0 / math.sqrt(head_dim)
    reach_blocks = (WINDOW - 1) // token_rows + 1
    key_rows = (reach_blocks + 1) * token_rows
    kv_width = kv_heads * head_dim
    query_width = query_heads * head_dim
    hidden_f = hidden_in.astype(jnp.float32)
    qkv_full, out_full, down_low_full, up_low_full = (
        lax.all_gather(qkv_weight, "shard", axis=0, tiled=True),
        lax.all_gather(out_weight, "shard", axis=0, tiled=True),
        lax.all_gather(laurel_down, "shard", axis=0, tiled=True),
        lax.all_gather(laurel_up, "shard", axis=0, tiled=True),
    )
    normed_one, norm_one_pull = jax.vjp(scaled_norm, hidden_f, model_gains[0])
    first_norm = normed_one.astype(jnp.bfloat16)
    proj_qkv = dot_plain(first_norm, qkv_full)
    query_pre = proj_qkv[:, :query_width].reshape(token_rows, query_heads, head_dim)
    key_pre = proj_qkv[:, query_width : query_width + kv_width].reshape(
        token_rows, kv_heads, head_dim
    )
    value_pre = proj_qkv[:, query_width + kv_width :]
    cosine, sine_part = rope_tables(positions, head_dim)

    def prepare(query_in, key_in, query_gain, key_gain):
        return (
            rotate(scaled_norm(query_in, query_gain), cosine, sine_part),
            rotate(scaled_norm(key_in, key_gain), cosine, sine_part),
        )

    (query_rot, key_rot), prepare_pull = jax.vjp(
        prepare, query_pre, key_pre, head_gains[0], head_gains[1]
    )
    query_grp = query_rot.astype(jnp.bfloat16).reshape(token_rows, kv_heads, group_size, head_dim)
    own_keys = jnp.concatenate(
        [
            key_rot.astype(jnp.bfloat16).reshape(token_rows, kv_width),
            value_pre.astype(jnp.bfloat16),
        ],
        axis=1,
    )
    earlier = [
        from_behind(own_keys, "shard", step_back) for step_back in range(reach_blocks, 0, -1)
    ]
    all_keys = jnp.concatenate(earlier + [own_keys], axis=0)
    key_all = all_keys[:, :kv_width].reshape(key_rows, kv_heads, head_dim)
    value_all = all_keys[:, kv_width:].reshape(key_rows, kv_heads, head_dim)
    offsets = (
        jnp.arange(token_rows, dtype=jnp.int32)[:, None]
        + reach_blocks * token_rows
        - jnp.arange(key_rows, dtype=jnp.int32)[None, :]
    )
    valid_keys = (offsets >= 0) & (offsets < WINDOW) & (offsets <= positions[:, None])

    def masked_scores():
        raw_scores = (
            jnp.einsum("qcgd,kcd->cgqk", query_grp, key_all, preferred_element_type=jnp.float32)
            * score_scale
        )
        return jnp.where(valid_keys, raw_scores, -1e30)

    scores = masked_scores()
    row_max = jnp.max(scores, axis=-1, keepdims=True)
    exponents = jnp.exp(scores - row_max)
    row_total = jnp.sum(exponents, axis=-1, keepdims=True)
    log_total = row_max + jnp.log(row_total)
    probs_low = (exponents / row_total).astype(jnp.bfloat16)
    mixed = jnp.einsum("cgqk,kcd->qcgd", probs_low, value_all, preferred_element_type=jnp.float32)
    mixed_low = mixed.reshape(token_rows, query_width).astype(jnp.bfloat16)
    attn_pre = dot_right_t(mixed_low, out_full)
    attn_out, attn_pull = jax.vjp(scaled_norm, attn_pre, model_gains[1])
    middle = dot_plain(first_norm, down_low_full).astype(jnp.bfloat16)
    side_pre = dot_right_t(middle, up_low_full)
    side_out, side_pull = jax.vjp(scaled_norm, side_pre, model_gains[2])
    first_sum = (hidden_f + attn_out + first_norm.astype(jnp.float32) + side_out) * SQRT_HALF
    ffn_full = (
        lax.all_gather(gate_up_weight, "shard", axis=0, tiled=True),
        lax.all_gather(down_weight, "shard", axis=0, tiled=True),
        lax.all_gather(layer_gate, "shard", axis=0, tiled=True),
        lax.all_gather(layer_project, "shard", axis=0, tiled=True),
    )
    gate_up_full, down_full, gate_layer_full, project_full = ffn_full
    normed_two, norm_two_pull = jax.vjp(scaled_norm, first_sum, model_gains[3])
    second_norm = normed_two.astype(jnp.bfloat16)
    gate_up = dot_plain(second_norm, gate_up_full)

    def gated_units(gate_and_up):
        return gelu_tanh(gate_and_up[:, :ffn_units]) * gate_and_up[:, ffn_units:]

    hidden_val, hidden_pull = jax.vjp(gated_units, gate_up)
    hidden_low = hidden_val.astype(jnp.bfloat16)
    ffn_pre = dot_right_t(hidden_low, down_full)
    ffn_out, ffn_pull = jax.vjp(scaled_norm, ffn_pre, model_gains[4])
    second_sum = first_sum + ffn_out
    second_low = second_sum.astype(jnp.bfloat16)
    ple_pre = dot_plain(second_low, gate_layer_full)

    def gate_vectors(pre_values, vector_values):
        return gelu_tanh(pre_values) * vector_values

    gated_val, gated_pull = jax.vjp(gate_vectors, ple_pre, layer_vectors.astype(jnp.float32))
    gated_low = gated_val.astype(jnp.bfloat16)
    last_pre = dot_right_t(gated_low, project_full)
    last_out, last_pull = jax.vjp(scaled_norm, last_pre, model_gains[5])
    layer_out = (second_sum + last_out).astype(jnp.bfloat16)
    gate_up_back, down_back, gate_layer_back, project_back = (
        lax.all_gather(gate_up_weight, "shard", axis=0, tiled=True),
        lax.all_gather(down_weight, "shard", axis=0, tiled=True),
        lax.all_gather(layer_gate, "shard", axis=0, tiled=True),
        lax.all_gather(layer_project, "shard", axis=0, tiled=True),
    )
    upstream = cotangent.astype(jnp.float32)
    d_last, grad_gain_five = last_pull(upstream)
    d_last_low = d_last.astype(jnp.bfloat16)
    d_gated = dot_plain(d_last_low, project_back)
    d_ple_pre, grad_vectors = gated_pull(d_gated)
    d_ple_low = d_ple_pre.astype(jnp.bfloat16)
    d_second = upstream + dot_right_t(d_ple_low, gate_layer_back)
    d_ffn, grad_gain_four = ffn_pull(d_second)
    d_ffn_low = d_ffn.astype(jnp.bfloat16)
    d_hidden = dot_plain(d_ffn_low, down_back)
    (d_gate_up,) = hidden_pull(d_hidden)
    d_gate_low = d_gate_up.astype(jnp.bfloat16)
    d_first_part, grad_gain_three = norm_two_pull(dot_right_t(d_gate_low, gate_up_back))
    d_branch = (d_second + d_first_part) * SQRT_HALF
    qkv_back, out_back, down_low_back, up_low_back = (
        lax.all_gather(qkv_weight, "shard", axis=0, tiled=True),
        lax.all_gather(out_weight, "shard", axis=0, tiled=True),
        lax.all_gather(laurel_down, "shard", axis=0, tiled=True),
        lax.all_gather(laurel_up, "shard", axis=0, tiled=True),
    )
    d_side, grad_gain_two = side_pull(d_branch)
    d_side_low = d_side.astype(jnp.bfloat16)
    d_middle_low = dot_plain(d_side_low, up_low_back).astype(jnp.bfloat16)
    d_attn, grad_gain_one = attn_pull(d_branch)
    d_attn_low = d_attn.astype(jnp.bfloat16)
    d_mixed_low = (
        dot_plain(d_attn_low, out_back)
        .astype(jnp.bfloat16)
        .reshape(token_rows, kv_heads, group_size, head_dim)
    )
    probabilities = jnp.exp(masked_scores() - log_total)
    d_probs = jnp.einsum(
        "qcgd,kcd->cgqk", d_mixed_low, value_all, preferred_element_type=jnp.float32
    )
    d_values = jnp.einsum(
        "cgqk,qcgd->kcd", probs_low, d_mixed_low, preferred_element_type=jnp.float32
    )
    row_dot = jnp.sum(probabilities * d_probs, axis=-1, keepdims=True)
    d_scores = (probabilities * (d_probs - row_dot)).astype(jnp.bfloat16)
    d_queries = (
        jnp.einsum("cgqk,kcd->qcgd", d_scores, key_all, preferred_element_type=jnp.float32)
        * score_scale
    )
    d_keys = (
        jnp.einsum("cgqk,qcgd->kcd", d_scores, query_grp, preferred_element_type=jnp.float32)
        * score_scale
    )
    key_grads = jnp.concatenate(
        [d_keys.reshape(key_rows, kv_width), d_values.reshape(key_rows, kv_width)], axis=1
    )
    pieces = [
        key_grads[block_index * token_rows : (block_index + 1) * token_rows]
        for block_index in range(reach_blocks + 1)
    ]
    returned = [
        from_behind(
            pieces[reach_blocks - step_back].astype(jnp.bfloat16), "shard", -step_back
        ).astype(jnp.float32)
        for step_back in range(1, reach_blocks + 1)
    ]
    own_grads = pieces[reach_blocks]
    for returned_piece in returned:
        own_grads = own_grads + returned_piece
    d_query_pre, d_key_pre, grad_query_gain, grad_key_gain = prepare_pull(
        (
            d_queries.reshape(token_rows, query_heads, head_dim),
            own_grads[:, :kv_width].reshape(token_rows, kv_heads, head_dim),
        )
    )
    d_proj = jnp.concatenate(
        [
            d_query_pre.reshape(token_rows, query_width),
            d_key_pre.reshape(token_rows, kv_width),
            own_grads[:, kv_width:],
        ],
        axis=1,
    ).astype(jnp.bfloat16)
    d_first_norm = (
        dot_right_t(d_proj, qkv_back) + dot_right_t(d_middle_low, down_low_back) + d_branch
    )
    d_input_part, grad_gain_zero = norm_one_pull(d_first_norm)
    grad_hidden = d_branch + d_input_part
    rights = [d_proj, mixed_low, d_middle_low, middle, d_gate_low, hidden_low, d_ple_low, gated_low]
    lefts = [
        first_norm,
        d_attn_low,
        first_norm,
        d_side_low,
        second_norm,
        d_ffn_low,
        second_low,
        d_last_low,
    ]
    shard_part = lax.psum_scatter(
        make_terms(lefts, rights).astype(jnp.bfloat16), "shard", scatter_dimension=0, tiled=True
    )
    summed = lax.psum(shard_part, "rep").astype(jnp.float32)
    model_part = jnp.stack(
        [
            grad_gain_zero,
            grad_gain_one,
            grad_gain_two,
            grad_gain_three,
            grad_gain_four,
            grad_gain_five,
        ]
    )
    head_part = jnp.stack([grad_query_gain, grad_key_gain])
    grad_model_gains, grad_head_gains = lax.psum((model_part, head_part), ("rep", "shard"))
    widths = [
        qkv_weight.shape[1],
        out_weight.shape[1],
        laurel_down.shape[1],
        laurel_up.shape[1],
        gate_up_weight.shape[1],
        down_weight.shape[1],
        layer_gate.shape[1],
        layer_project.shape[1],
    ]
    splits = []
    column_start = 0
    for column_width in widths:
        splits.append(summed[:, column_start : column_start + column_width])
        column_start = column_start + column_width
    return (
        layer_out,
        grad_hidden,
        grad_vectors,
        grad_model_gains,
        grad_head_gains,
        splits[0],
        splits[1],
        splits[2],
        splits[3],
        splits[4],
        splits[5],
        splits[6],
        splits[7],
    )


def solution(mesh):
    return jax.shard_map(
        body,
        mesh=mesh,
        in_specs=(
            P(("rep", "shard"), None),
            P(("rep", "shard"), None),
            P(("rep", "shard")),
            P(("rep", "shard"), None),
            P(),
            P(),
            P("shard", None),
            P("shard", None),
            P("shard", None),
            P("shard", None),
            P("shard", None),
            P("shard", None),
            P("shard", None),
            P("shard", None),
        ),
        out_specs=(
            P(("rep", "shard"), None),
            P(("rep", "shard"), None),
            P(("rep", "shard"), None),
            P(),
            P(),
            P("shard", None),
            P("shard", None),
            P("shard", None),
            P("shard", None),
            P("shard", None),
            P("shard", None),
            P("shard", None),
            P("shard", None),
        ),
        check_vma=False,
    )
```

profile of v0, /device:TPU:0, one launch (start us, length us, event | category | flops | bytes accessed | tf_op | source)
XLA Modules:
  0.0 3037.7 jit_solution(16085401255709531326)
XLA Ops:
  13.2 16.5 all_gather.34
  29.7 20.0 all_gather.35
  52.7 79.1 %all-gather.7.cloned.1.call-done = bf16[2048,3072]{1,0:T(8,128)(2,1)} async-done(((bf16[256,3072]{1,0:T(8,128)(2,1)}), bf16[2048,3072]{1,0:T(8,128)(2,1)}) %all-gather.7.cloned.1.call-update) | async-done | bytes 12582928 | tf_op jit(solution)/shard_map/all_gather | solution.py:104
  154.5 16.3 collective-permute-done
  187.5 38.2 %all-gather.9.cloned.1.call-done = bf16[2048,2048]{1,0:T(8,128)(2,1)} async-done(((bf16[256,2048]{1,0:T(8,128)(2,1)}), bf16[2048,2048]{1,0:T(8,128)(2,1)}) %all-gather.9.cloned.1.call-update) | async-done | bytes 8388624 | tf_op jit(solution)/shard_map/all_gather | solution.py:105
  233.0 561.6 %all-gather.11.cloned.1.call-done = bf16[2048,16384]{1,0:T(8,128)(2,1)} async-done(((bf16[256,16384]{1,0:T(8,128)(2,1)}), bf16[2048,16384]{1,0:T(8,128)(2,1)}) %all-gather.11.cloned.1.call-update) | async-done | bytes 67108880 | tf_op jit(solution)/shard_map/all_gather | solution.py:171
  794.7 37.0 %fusion.77 = f32[256,16384]{1,0:T(8,128)} fusion(bf16[2048,16384]{1,0:T(8,128)(2,1)} %all-gather.11.cloned.1.call-done, f32[256,2048]{1,0:T(8,128)S(1)} %get-tuple-element.74, f32[2048]{0:T(1024)S(1)} %bitcast.146, f32[256]{0:T(256)S(1)} %get-tuple-element.114), kind=kOutput, calls=%fused_computation.192 | convolution fusion | flops 17181442048 | bytes 85992448 | tf_op jit(solution)/shard_map/dot_general | solution.py:50
  831.7 9.1 multiply_convert_fusion
  840.8 242.2 %all-gather.13.cloned.1.call-done = bf16[2048,8192]{1,0:T(8,128)(2,1)} async-done(((bf16[256,8192]{1,0:T(8,128)(2,1)}), bf16[2048,8192]{1,0:T(8,128)(2,1)}) %all-gather.13.cloned.1.call-update) | async-done | bytes 33554448 | tf_op jit(solution)/shard_map/all_gather | solution.py:172
  1083.0 17.5 multiply_reduce_fusion.11
  1106.4 21.5 all-gather.17.cloned.1.call-done
  1139.0 32.0 %fusion.12 = (f32[256,8192]{1,0:T(8,128)}, f32[256,8192]{1,0:T(8,128)}) fusion(f32[256,16384]{1,0:T(8,128)} %fusion.77, bf16[256,2048]{1,0:T(8,128)(2,1)S(1)} %fusion.23, bf16[2048,8192]{1,0:T(8,128)(2,1)} %all-gather.13.cloned.1.call-done), kind=kOutput, calls=%fused_computation.45 | convolution fusion | flops 8636071936 | bytes 68157440 | tf_op jit(solution)/shard_map/dot_general | solution.py:50
  1171.0 32.0 %multiply_reduce_fusion.2 = (f32[2048]{0:T(1024)}, f32[256]{0:T(256)S(1)}, f32[256,2048]{1,0:T(8,128)}) fusion(f32[256,2048]{1,0:T(8,128)S(1)} %copy-done.8, f32[256]{0:T(256)S(1)} %get-tuple-element.114, f32[2048]{0:T(1024)S(1)} %bitcast.147, bf16[2048,16384]{1,0:T(8,128)(2,1)} %all-gather.11.cloned.1.call-done, f32[256,8192]{1,0:T(8,128)} %get-tuple-element.76, ...), kind=kOutput, calls=%fused_computation.74 | convolution fusion | flops 17191925760 | bytes 88098816 | tf_op jit(solution)/shard_map/dot_general | solution.py:54
  1210.8 6.7 convolution_convert_fusion.6
  1244.0 15.9 convolution_convert_fusion.1
  1260.0 34.6 %convolution_convert_fusion = bf16[2048,16384]{1,0:T(8,128)(2,1)} fusion(f32[256,8192]{1,0:T(8,128)} %get-tuple-element.76, f32[256,8192]{1,0:T(8,128)} %get-tuple-element.75, f32[256,2048]{1,0:T(8,128)S(1)} %copy-done.8, f32[2048]{0:T(1024)S(1)} %bitcast.149, f32[256]{0:T(256)S(1)} %get-tuple-element.114), kind=kOutput, calls=%fused_computation | convolution fusion | flops 17223385088 | bytes 85992448 | tf_op jit(solution)/shard_map/dot_general | solution.py:60
  1318.2 12.5 copy.106
  1349.9 6.8 convolution_convert_fusion.2
  1356.7 175.6 %concatenate.38 = bf16[2048,30336]{1,0:T(8,128)(2,1)} concatenate(bf16[2048,3072]{1,0:T(8,128)(2,1)} %convolution_convert_fusion.2, bf16[2048,2048]{1,0:T(8,128)(2,1)} %copy.106, bf16[2048,64]{1,0:T(8,128)(2,1)} %copy.107, bf16[2048,64]{1,0:T(8,128)(2,1)} %copy.108, bf16[2048,16384]{1,0:T(8,128)(2,1)} %convolution_convert_fusion, bf16[2048,8192]{1,0:T(8,128)(2,1)} %convolution_convert_fusion.1, ...), dimensions={1} | concatenate | bytes 248512512 | tf_op jit(solution)/shard_map/concatenate | solution.py:70
  1532.4 1177.8 %reduce-scatter.2.cloned.1.call-done = bf16[256,30336]{1,0:T(8,128)(2,1)} async-done(((bf16[2048,30336]{1,0:T(8,128)(2,1)}), bf16[256,30336]{1,0:T(8,128)(2,1)}) %reduce-scatter.2.cloned.1.call-update) | async-done | bytes 15532048 | tf_op jit(solution)/shard_map/reduce_scatter | solution.py:299
  2710.2 7.0 fusion.46
  2719.8 39.7 %all-reduce.6 = (f32[6,2048]{1,0:T(8,128)}, f32[2,256]{1,0:T(2,128)}) all-reduce(f32[6,2048]{1,0:T(8,128)S(1)} %stack.8, f32[2,256]{1,0:T(2,128)S(1)} %pad_maximum_fusion.9), channel_id=1, replica_groups=mesh['rep'=4,'shard'=8] {'rep','shard'}, use_global_device_ids=true, to_apply=%region_25.26 | all-reduce | flops 12800 | bytes 102400 | tf_op jit(solution)/shard_map/psum | solution.py:314
  2763.3 238.5 %all-reduce.9.cloned.1.call-done = bf16[256,30336]{1,0:T(8,128)(2,1)} async-done(((bf16[256,30336]{1,0:T(8,128)(2,1)}), bf16[256,30336]{1,0:T(8,128)(2,1)}) %all-reduce.9.cloned.1.call-update) | async-done | bytes 15532048 | tf_op jit(solution)/shard_map/psum | solution.py:302
  3018.8 11.5 slice.153
  (362 shorter events, 171.8 us)
Async XLA Ops:
  7.2 124.6 %all-gather.7.cloned.1.call-start = ((), (), s32[]{:S(2)}) async-start(), calls=%async_computation.1 | async-start | bytes 14155776 | tf_op jit(solution)/shard_map/all_gather | solution.py:104
  7.9 217.7 %all-gather.9.cloned.1.call-start = ((), (), s32[]{:S(2)}) async-start(), calls=%async_computation.2 | async-start | bytes 9437184 | tf_op jit(solution)/shard_map/all_gather | solution.py:105
  8.7 786.0 %all-gather.11.cloned.1.call-start = ((), (), s32[]{:S(2)}) async-start(), calls=%async_computation.3 | async-start | bytes 75497472 | tf_op jit(solution)/shard_map/all_gather | solution.py:171
  9.5 1073.5 %all-gather.13.cloned.1.call-start = ((), (), s32[]{:S(2)}) async-start(), calls=%async_computation.4 | async-start | bytes 37748736 | tf_op jit(solution)/shard_map/all_gather | solution.py:172
  10.0 1094.7 %all-gather.15.cloned.1.call-start = ((), (), s32[]{:S(2)}) async-start(), calls=%async_computation.5 | async-start | bytes 1179648 | tf_op jit(solution)/shard_map/all_gather | solution.py:173
  10.6 1117.3 %all-gather.17.cloned.1.call-start = ((), (), s32[]{:S(2)}) async-start(), calls=%async_computation.6 | async-start | bytes 1179648 | tf_op jit(solution)/shard_map/all_gather | solution.py:174
  11.2 2699.0 %reduce-scatter.2.cloned.1.call-start = ((), (), s32[]{:S(2)}) async-start(), calls=%async_computation.7 | async-start | bytes 139788288 | tf_op jit(solution)/shard_map/reduce_scatter | solution.py:299
  11.6 220.1 %copy-start.84 = (f32[256]{0:T(256)}, f32[256]{0:T(256)S(1)}, u32[]{:S(2)}) copy-start(f32[256]{0:T(256)S(1)} %fusion.62) | copy-start | bytes 3076
  11.7 129.3 %copy-start.97 = (f32[1,256]{1,0:T(1,128)}, f32[1,256]{1,0:T(1,128)S(1)}, u32[]{:S(2)}) copy-start(f32[1,256]{1,0:T(1,128)S(1)} %get-tuple-element.110) | copy-start | bytes 3076
  11.7 140.2 %copy-start.95 = (f32[1,256]{1,0:T(1,128)}, f32[1,256]{1,0:T(1,128)S(1)}, u32[]{:S(2)}) copy-start(f32[1,256]{1,0:T(1,128)S(1)} %get-tuple-element.109) | copy-start | bytes 3076
  11.7 220.0 %copy-start.71 = (f32[1,2048]{1,0:T(1,128)}, f32[1,2048]{1,0:T(1,128)S(1)}, u32[]{:S(2)}) copy-start(f32[1,2048]{1,0:T(1,128)S(1)} %get-tuple-element.107) | copy-start | bytes 24580
  13.2 168.8 %copy-start.29 = (pred[256,768]{0,1:T(8,128)(4,1)}, pred[256,768]{0,1:T(8,128)(4,1)S(1)}, u32[]{:S(2)}) copy-start(pred[256,768]{0,1:T(8,128)(4,1)S(1)} %fusion.41) | copy-start | bytes 589828
  52.1 86.2 %copy-start.100 = (f32[256]{0:T(256)}, f32[256]{0:T(256)S(1)}, u32[]{:S(2)}) copy-start(f32[256]{0:T(256)S(1)} %get-tuple-element.115) | copy-start | bytes 3076
  52.6 88.7 %copy-start.45 = (f32[256,128]{1,0:T(8,128)}, f32[256,128]{1,0:T(8,128)S(1)}, u32[]{:S(2)}) copy-start(f32[256,128]{1,0:T(8,128)S(1)} %get-tuple-element.112) | copy-start | bytes 393220
  52.6 100.5 %copy-start.43 = (f32[256,128]{1,0:T(8,128)}, f32[256,128]{1,0:T(8,128)S(1)}, u32[]{:S(2)}) copy-start(f32[256,128]{1,0:T(8,128)S(1)} %get-tuple-element.111) | copy-start | bytes 393220
  142.8 11.7 collective-permute-start.1
  145.7 25.1 collective-permute-start
  187.4 44.2 %copy-start.33 = (bf16[2,256,4,256]{3,1,2,0:T(8,128)(2,1)}, bf16[2,256,4,256]{3,1,2,0:T(8,128)(2,1)S(1)}, u32[]{:S(2)}) copy-start(bf16[2,256,4,256]{3,1,2,0:T(8,128)(2,1)S(1)} %convolution_convert_fusion.9) | copy-start | bytes 3145732
  233.0 598.7 %copy-start.7 = (f32[256,2048]{1,0:T(8,128)}, f32[256,2048]{1,0:T(8,128)S(1)}, u32[]{:S(2)}) copy-start(f32[256,2048]{1,0:T(8,128)S(1)} %get-tuple-element.74) | copy-start | bytes 6291460
  1210.3 85.3 %copy-start.75 = (bf16[256,64]{0,1:T(8,128)(2,1)}, bf16[256,64]{0,1:T(8,128)(2,1)S(1)}, u32[]{:S(2)}) copy-start(bf16[256,64]{0,1:T(8,128)(2,1)S(1)} %convolution_convert_fusion.10) | copy-start | bytes 98308
  1315.5 19.6 collective-permute-start.2
  1316.8 21.1 collective-permute-start.3
  1532.3 1469.5 %all-reduce.9.cloned.1.call-start = ((), (), s32[]{:S(2)}) async-start(), calls=%async_computation.8 | async-start | bytes 31064064 | tf_op jit(solution)/shard_map/psum | solution.py:302
  2717.3 42.2 %copy-start.99 = (f32[256]{0:T(256)S(1)}, f32[256]{0:T(256)}, u32[]{:S(2)}) copy-start(f32[256]{0:T(256)} %copy-done.98) | copy-start | bytes 3076
  (97 other events, 756.4 us)
Sparse Core Ops, SparseCore 0:
  9.7 122.0 all-gather.6
  133.4 92.2 all-gather.8
  227.3 567.3 all-gather.10
  796.1 286.8 all-gather.12
  1084.4 20.2 all-gather.14
  1106.2 21.7 all-gather.16
  1532.5 1177.6 reduce-scatter.1
  2714.2 287.5 all-reduce.8
where the time goes:
time: 3050 us; the launch traced here: 3040 us
  waiting for transfers between devices  2380 us (78%)
  local copies, waits for them, and re-layouts  255 us (8%)
  matrix products  244 us (8%)
  blocking collectives  76.3 us (3%)
  other arithmetic  55.2 us (2%)
    reduce_scatter x1, waiting for transfers between devices, body(): lax.psum_scatter(make_terms(lefts, rights).astype(jnp.bfloat16), 'shard',...  1180 us
    all_gather x1, waiting for transfers between devices, body(): lax.all_gather(gate_up_weight, 'shard', axis=0, tiled=True)  562 us
    all_gather x1, waiting for transfers between devices, body(): lax.all_gather(down_weight, 'shard', axis=0, tiled=True)  242 us
    psum x1, waiting for transfers between devices, body(): summed = lax.psum(shard_part, 'rep').astype(jnp.float32)  238 us
    concatenate x1, local copies, waits for them, and re-layouts, make_terms(): jnp.concatenate([dot_left_t(left_side, right_side) for left_side, right_s...  176 us
    dot_general x8, matrix products, dot_plain(): return jnp.dot(left_side, right_side, preferred_element_type=jnp.float32)  86.1 us
    all_gather x1, waiting for transfers between devices, body(): lax.all_gather(qkv_weight, 'shard', axis=0, tiled=True)  79.1 us
    dot_general x8, matrix products, dot_right_t(): lax.dot_general(left_side, right_side, (((1,), (1,)), ((), ())), preferre...  70 us
  transfers between devices with their start and end apart: 12, of which 10 were waited for; matrix products, arithmetic and copies ran while one was open for 5% of the time, Pallas kernels for 0%

commit v1 on v0

v1 whole, which is shorter than its diff:
```python
import math

import jax
import jax.numpy as jnp
import numpy as np
from jax import lax
from jax.sharding import Mesh
from jax.sharding import PartitionSpec as P

WINDOW = 512
EPSILON = 1e-06
SQRT_HALF = 0.7071067811865476
BF = jnp.bfloat16
F32 = jnp.float32
REP = ("ra", "rb")


def scaled_norm(values, gain_row):
    return (
        values * lax.rsqrt(jnp.mean(values * values, axis=-1, keepdims=True) + EPSILON) * gain_row
    )


def rotate(values, cosine, sine_part):
    half_dim = values.shape[-1] // 2
    first_half = values[..., :half_dim]
    second_half = values[..., half_dim:]
    return jnp.concatenate(
        [
            first_half * cosine - second_half * sine_part,
            second_half * cosine + first_half * sine_part,
        ],
        axis=-1,
    )


def rope_tables(positions, head_dim):
    half_dim = head_dim // 2
    frequency = jnp.exp(
        jnp.arange(half_dim, dtype=jnp.float32) * (-2.0 * math.log(10000.0) / head_dim)
    )
    phase_angle = positions.astype(jnp.float32)[:, None] * frequency[None, :]
    return (jnp.cos(phase_angle)[:, None, :], jnp.sin(phase_angle)[:, None, :])


def dot_plain(left_side, right_side):
    return jnp.dot(left_side, right_side, preferred_element_type=jnp.float32)


def dot_right_t(left_side, right_side):
    return lax.dot_general(
        left_side, right_side, (((1,), (1,)), ((), ())), preferred_element_type=jnp.float32
    )


def dot_left_t(left_side, right_side):
    return lax.dot_general(
        left_side, right_side, (((0,), (0,)), ((), ())), preferred_element_type=jnp.float32
    )


def gelu_tanh(values):
    return jax.nn.gelu(values, approximate=True)


def after(value, *others):
    return lax.optimization_barrier((value,) + others)[0]


def swap(value, axis):
    return lax.ppermute(value, axis, [(0, 1), (1, 0)])


def square():
    return lax.axis_size("ra") == 2 and lax.axis_size("rb") == 2


def rep_count():
    return lax.axis_size("ra") * lax.axis_size("rb")


def rep_id():
    return lax.axis_index("ra") * lax.axis_size("rb") + lax.axis_index("rb")


def rep_of(k):
    return rep_id() ^ k if square() else k


def rep_gather(value):
    if not square():
        whole = lax.all_gather(value, REP, axis=0)
        return [whole[k] for k in range(rep_count())]
    half = value.shape[0] // 2
    from_b = swap(value, "rb")
    from_a = swap(value, "ra")
    far_one = swap(from_a[:half], "rb")
    far_two = swap(from_b[half:], "ra")
    return [value, from_b, from_a, jnp.concatenate([far_one, far_two], axis=0)]


def rep_scatter(parts):
    if not square():
        return lax.psum_scatter(jnp.stack(parts), REP, scatter_dimension=0).astype(F32)
    half = parts[3].shape[0] // 2
    far_one = swap(parts[3][:half], "rb")
    far_two = swap(parts[3][half:], "ra")
    to_b = jnp.concatenate(
        [parts[1][:half].astype(F32), parts[1][half:].astype(F32) + far_two.astype(F32)], axis=0
    ).astype(BF)
    to_a = jnp.concatenate(
        [parts[2][:half].astype(F32) + far_one.astype(F32), parts[2][half:].astype(F32)], axis=0
    ).astype(BF)
    from_b = swap(to_b, "rb")
    from_a = swap(to_a, "ra")
    return parts[0].astype(F32) + from_b.astype(F32) + from_a.astype(F32)


def shift(value, steps):
    count = lax.axis_size("line")
    return lax.ppermute(value, "line", [(i, (i + steps) % count) for i in range(count)])


def line_slots(value):
    count = lax.axis_size("line")
    place = lax.axis_index("line")
    ups, downs = [value], [value]
    for s in range(1, count):
        ups.append(lax.ppermute(ups[-1], "line", [(i, i + 1) for i in range(s - 1, count - 1)]))
        downs.append(lax.ppermute(downs[-1], "line", [(i + 1, i) for i in range(0, count - s)]))
    first = (ups[1], downs[1])
    return [value] + [
        jnp.where(place >= s, ups[s], downs[count - s]) for s in range(1, count)
    ], first


def place_slots(slots):
    count = lax.axis_size("line")
    place = lax.axis_index("line")
    whole = jnp.zeros((count,) + slots[0].shape, slots[0].dtype)
    for s in range(count):
        whole = lax.dynamic_update_index_in_dim(whole, slots[s], (place - s) % count, 0)
    return whole.reshape((count * slots[0].shape[0],) + slots[0].shape[1:])


def line_scatter(blocks):
    count = lax.axis_size("line")
    place = lax.axis_index("line")

    def block(j):
        return lax.dynamic_index_in_dim(blocks, jnp.clip(j, 0, count - 1), 0, keepdims=False)

    going_up = going_down = None
    for t in range(1, count):
        up = block(place + count - t)
        down = block(place - count + t)
        if going_up is not None:
            up = (up.astype(F32) + going_up.astype(F32)).astype(BF)
            down = (down.astype(F32) + going_down.astype(F32)).astype(BF)
        going_up = lax.ppermute(up, "line", [(i, i + 1) for i in range(t)])
        going_down = lax.ppermute(down, "line", [(count - 1 - i, count - 2 - i) for i in range(t)])
    own = block(place).astype(F32)
    return (own + going_up.astype(F32) + going_down.astype(F32)).astype(BF)


def sum_everywhere(value):
    sizes = [lax.axis_size(a) for a in ("core", "rb", "ra", "line")]
    if any(n & (n - 1) for n in sizes):
        return lax.psum(value, ("ra", "rb", "line", "core"))
    for axis, n in zip(("core", "rb", "ra", "line"), sizes):
        step = 1
        while step < n:
            value = value + lax.ppermute(value, axis, [(i, i ^ step) for i in range(n)])
            step *= 2
    return value


def by_core(mine, other, axis):
    first = lax.axis_index("core") == 0
    return jnp.concatenate(
        [jnp.where(first, mine, other), jnp.where(first, other, mine)], axis=axis
    )


def pick(pair, which):
    return jnp.where(which == 0, pair[0], pair[1])


def body(
    hidden_in,
    layer_vectors,
    positions,
    cotangent,
    model_gains,
    head_gains,
    qkv_weight,
    out_weight,
    laurel_down,
    laurel_up,
    gate_up_weight,
    down_weight,
    layer_gate,
    layer_project,
):
    tokens, width = hidden_in.shape
    head_dim = head_gains.shape[1]
    query_heads = out_weight.shape[1] // head_dim
    kv_heads = (qkv_weight.shape[1] // head_dim - query_heads) // 2
    group = query_heads // kv_heads
    ffn_units = down_weight.shape[1]
    rank = laurel_down.shape[1]
    ple = layer_gate.shape[1]
    score_scale = 1.0 / math.sqrt(head_dim)
    reps = rep_count()
    line = lax.axis_size("line")
    cores = 2
    core = lax.axis_index("core")
    rep = rep_id()
    place = lax.axis_index("line")
    weight_rows = qkv_weight.shape[0]
    sub = weight_rows // reps
    group_width = group * head_dim
    part_width = group_width + 2 * head_dim
    small_width = rank + ple
    units = ffn_units // (reps * cores)
    pair = 2 * tokens
    assert kv_heads == cores and pair >= WINDOW

    qkv_rows = lax.dynamic_slice_in_dim(qkv_weight, rep * sub, sub, 0)
    out_rows = lax.dynamic_slice_in_dim(out_weight, rep * sub, sub, 0)

    def qkv_columns(rows, c):
        return jnp.concatenate(
            [
                lax.dynamic_slice_in_dim(rows, c * group_width, group_width, 1),
                lax.dynamic_slice_in_dim(
                    rows, query_heads * head_dim + c * head_dim, head_dim, 1
                ),
                lax.dynamic_slice_in_dim(
                    rows, (query_heads + kv_heads) * head_dim + c * head_dim, head_dim, 1
                ),
            ],
            axis=1,
        )

    down_small = jnp.concatenate([laurel_down, layer_gate], axis=1)
    up_small = jnp.concatenate([laurel_up, layer_project], axis=1)
    small_pair = (
        lax.dynamic_slice_in_dim(down_small, rep * sub, sub, 0),
        lax.dynamic_slice_in_dim(up_small, rep * sub, sub, 0),
    )

    def out_columns(rows, c):
        return jnp.concatenate(
            [
                lax.dynamic_slice_in_dim(rows, c * group_width, group_width, 1),
                pick(small_pair, c),
            ],
            axis=1,
        )

    def both_cores_rows(columns, rows):
        mine = columns(rows, core)
        other = swap(columns(rows, 1 - core), "core")
        first = core == 0
        return jnp.stack([jnp.where(first, mine, other), jnp.where(first, other, mine)])

    def spread(block, line_after=None, rep_after=None):
        if line_after is not None:
            block = after(block, *line_after)
        slots = [block] + [shift(block, s) for s in range(1, line)]
        on_line = slots[1:]
        whole = jnp.zeros((line, cores, reps, sub, block.shape[-1]), BF)
        last = None
        for s in range(line):
            slot = slots[s] if rep_after is None else after(slots[s], *rep_after)
            pieces = rep_gather(slot)
            last = pieces[1:]
            for k in range(reps):
                whole = lax.dynamic_update_slice(
                    whole,
                    pieces[k][None, :, None],
                    ((place - s) % line, 0, rep_of(k), 0, 0),
                )
        return whole.reshape(line * cores * reps * sub, block.shape[-1]), on_line, last

    qkv_block = both_cores_rows(qkv_columns, qkv_rows)
    out_block = both_cores_rows(out_columns, out_rows)
    qkv_part, qkv_line, qkv_last = spread(qkv_block)
    out_small, out_line, out_last = spread(out_block, qkv_line, qkv_last)
    out_part = out_small[:, :group_width]
    small_mine = out_small[:, group_width:]
    small_other = swap(small_mine, "core")
    first_core = core == 0
    down_small_full = jnp.where(first_core, small_mine, small_other)
    up_small_full = jnp.where(first_core, small_other, small_mine)
    down_low_full, gate_layer_full = down_small_full[:, :rank], down_small_full[:, rank:]
    up_low_full, project_full = up_small_full[:, :rank], up_small_full[:, rank:]

    def ffn_columns(c):
        start = (rep * cores + c) * units
        return [
            lax.dynamic_slice_in_dim(gate_up_weight, start, units, 1),
            lax.dynamic_slice_in_dim(gate_up_weight, ffn_units + start, units, 1),
            lax.dynamic_slice_in_dim(down_weight, start, units, 1),
        ]

    ffn_mine = ffn_columns(core)
    ffn_sent = ffn_columns(1 - core)
    ffn_whole = []
    previous = out_line
    for mine, sent in zip(ffn_mine, ffn_sent):
        block = by_core(mine, swap(sent, "core"), 0)
        slots, previous = line_slots(after(block, *previous))
        ffn_whole.append(place_slots(slots))
    gate_weight, up_weight, down_cols = ffn_whole
    gate_up_cols = jnp.concatenate([gate_weight, up_weight], axis=1)

    hidden_pair = jnp.concatenate([hidden_in, swap(hidden_in, "core")], axis=0)
    pos_pair = jnp.concatenate([positions, swap(positions, "core")], axis=0)
    steps = jnp.arange(tokens, dtype=jnp.int32)
    index = jnp.concatenate([core * tokens + steps, (1 - core) * tokens + steps])
    hidden_f = hidden_in.astype(F32)
    first_pair = scaled_norm(hidden_pair.astype(F32), model_gains[0]).astype(BF)
    normed_one, norm_one_pull = jax.vjp(scaled_norm, hidden_f, model_gains[0])
    first_norm = normed_one.astype(BF)
    proj = dot_plain(first_pair, qkv_part)
    query_pre = proj[:, :group_width].reshape(pair, group, head_dim)
    key_pre = proj[:, group_width : group_width + head_dim].reshape(pair, 1, head_dim)
    value_own = proj[:, group_width + head_dim :].astype(BF)
    cosine, sine_part = rope_tables(pos_pair, head_dim)

    def prepare(query_in, key_in, query_gain, key_gain):
        return (
            rotate(scaled_norm(query_in, query_gain), cosine, sine_part),
            rotate(scaled_norm(key_in, key_gain), cosine, sine_part),
        )

    (query_rot, key_rot), prepare_pull = jax.vjp(
        prepare, query_pre, key_pre, head_gains[0], head_gains[1]
    )
    query_low = query_rot.astype(BF)
    own_keys = jnp.concatenate([key_rot.astype(BF).reshape(pair, head_dim), value_own], axis=1)
    up_line = [(i, i + 1) for i in range(line - 1)]
    earlier = lax.ppermute(own_keys, "line", up_line)
    all_keys = jnp.concatenate([earlier, own_keys], axis=0)
    key_all = all_keys[:, :head_dim]
    value_all = all_keys[:, head_dim:]
    key_index = jnp.concatenate([index - pair, index])
    offsets = index[:, None] - key_index[None, :]
    valid_keys = (offsets >= 0) & (offsets < WINDOW) & (offsets <= pos_pair[:, None])

    def masked_scores():
        raw = jnp.einsum("qgd,kd->gqk", query_low, key_all, preferred_element_type=F32)
        return jnp.where(valid_keys, raw * score_scale, -1e30)

    scores = masked_scores()
    row_max = jnp.max(scores, axis=-1, keepdims=True)
    exponents = jnp.exp(scores - row_max)
    row_total = jnp.sum(exponents, axis=-1, keepdims=True)
    log_total = row_max + jnp.log(row_total)
    probs_low = (exponents / row_total).astype(BF)
    mixed = jnp.einsum("gqk,kd->qgd", probs_low, value_all, preferred_element_type=F32)
    mixed_low = mixed.reshape(pair, group_width).astype(BF)
    attn_sum = dot_right_t(mixed_low, out_part)
    attn_pre = attn_sum[:tokens] + swap(attn_sum[tokens:], "core")
    attn_out, attn_pull = jax.vjp(scaled_norm, attn_pre, model_gains[1])
    middle = dot_plain(first_norm, down_low_full).astype(BF)
    side_pre = dot_right_t(middle, up_low_full)
    side_out, side_pull = jax.vjp(scaled_norm, side_pre, model_gains[2])
    first_sum = (hidden_f + attn_out + first_norm.astype(F32) + side_out) * SQRT_HALF
    normed_two, norm_two_pull = jax.vjp(scaled_norm, first_sum, model_gains[3])

    def plane_gather(value):
        chunks = []
        for block in rep_gather(value):
            chunks += [block, swap(block, "core")]
        return jnp.concatenate(chunks, axis=0)

    def plane_scatter(whole):
        parts = []
        for k in range(reps):
            mine = whole[k * pair : k * pair + tokens]
            theirs = swap(whole[k * pair + tokens : (k + 1) * pair], "core")
            parts.append((mine.astype(F32) + theirs.astype(F32)).astype(BF))
        return rep_scatter(parts)

    second_all = plane_gather(normed_two.astype(BF))
    gate_up = dot_plain(second_all, gate_up_cols)

    def gated_units(gate_and_up):
        return gelu_tanh(gate_and_up[:, :units]) * gate_and_up[:, units:]

    hidden_val, hidden_pull = jax.vjp(gated_units, gate_up)
    hidden_low = hidden_val.astype(BF)
    ffn_pre = plane_scatter(dot_right_t(hidden_low, down_cols).astype(BF))
    ffn_out, ffn_pull = jax.vjp(scaled_norm, ffn_pre, model_gains[4])
    second_sum = first_sum + ffn_out
    second_low = second_sum.astype(BF)
    ple_pre = dot_plain(second_low, gate_layer_full)

    def gate_vectors(pre_values, vector_values):
        return gelu_tanh(pre_values) * vector_values

    gated_val, gated_pull = jax.vjp(gate_vectors, ple_pre, layer_vectors.astype(F32))
    gated_low = gated_val.astype(BF)
    last_pre = dot_right_t(gated_low, project_full)
    last_out, last_pull = jax.vjp(scaled_norm, last_pre, model_gains[5])
    layer_out = (second_sum + last_out).astype(BF)

    upstream = cotangent.astype(F32)
    d_last, grad_gain_five = last_pull(upstream)
    d_last_low = d_last.astype(BF)
    d_gated = dot_plain(d_last_low, project_full)
    d_ple_pre, grad_vectors = gated_pull(d_gated)
    d_ple_low = d_ple_pre.astype(BF)
    d_second = upstream + dot_right_t(d_ple_low, gate_layer_full)
    d_ffn, grad_gain_four = ffn_pull(d_second)
    d_ffn_all = plane_gather(d_ffn.astype(BF))
    d_hidden = dot_plain(d_ffn_all, down_cols)
    (d_gate_up,) = hidden_pull(d_hidden)
    d_gate_low = d_gate_up.astype(BF)

    def ffn_gradient(term):
        mine = line_scatter(term.reshape(line, cores * weight_rows, units))
        halves = mine.reshape(cores, weight_rows, units)
        keep = pick(halves, core)
        other = swap(pick(halves, 1 - core), "core")
        return by_core(keep, other, 1)

    def lay_out(blocks, total):
        out = jnp.zeros((weight_rows, total), F32)
        for block, start in blocks:
            out = lax.dynamic_update_slice(out, block.astype(F32), (0, start))
        return out

    def spread_columns(mine, offset):
        return [
            (block, offset + rep_of(k) * cores * units)
            for k, block in enumerate(rep_gather(mine))
        ]

    down_own = ffn_gradient(dot_left_t(d_ffn_all, hidden_low).astype(BF))
    d_second_norm = plane_scatter(dot_right_t(d_gate_low, gate_up_cols).astype(BF))
    gate_up_terms = dot_left_t(second_all, d_gate_low).astype(BF)
    gate_own = ffn_gradient(gate_up_terms[:, :units])
    up_own = ffn_gradient(gate_up_terms[:, units:])
    grad_down = lay_out(spread_columns(down_own, 0), ffn_units)
    grad_gate_up = lay_out(
        spread_columns(gate_own, 0) + spread_columns(up_own, ffn_units), 2 * ffn_units
    )

    d_first_part, grad_gain_three = norm_two_pull(d_second_norm)
    d_branch = (d_second + d_first_part) * SQRT_HALF
    d_side, grad_gain_two = side_pull(d_branch)
    d_side_low = d_side.astype(BF)
    d_middle_low = dot_plain(d_side_low, up_low_full).astype(BF)
    d_attn, grad_gain_one = attn_pull(d_branch)
    d_attn_low = d_attn.astype(BF)
    d_attn_pair = jnp.concatenate([d_attn_low, swap(d_attn_low, "core")], axis=0)
    d_mixed_low = dot_plain(d_attn_pair, out_part).astype(BF).reshape(pair, group, head_dim)
    probabilities = jnp.exp(masked_scores() - log_total)
    d_probs = jnp.einsum("qgd,kd->gqk", d_mixed_low, value_all, preferred_element_type=F32)
    d_values = jnp.einsum("gqk,qgd->kd", probs_low, d_mixed_low, preferred_element_type=F32)
    row_dot = jnp.sum(probabilities * d_probs, axis=-1, keepdims=True)
    d_scores = (probabilities * (d_probs - row_dot)).astype(BF)
    d_queries = (
        jnp.einsum("gqk,kd->qgd", d_scores, key_all, preferred_element_type=F32) * score_scale
    )
    d_keys = (
        jnp.einsum("gqk,qgd->kd", d_scores, query_low, preferred_element_type=F32) * score_scale
    )
    key_grads = jnp.concatenate([d_keys, d_values], axis=1)
    down_line = [(i + 1, i) for i in range(line - 1)]
    returned = lax.ppermute(key_grads[:pair].astype(BF), "line", down_line)
    own_grads = key_grads[pair:] + returned.astype(F32)
    d_query_pre, d_key_pre, grad_query_gain, grad_key_gain = prepare_pull(
        (d_queries, own_grads[:, :head_dim].reshape(pair, 1, head_dim))
    )
    d_proj = jnp.concatenate(
        [
            d_query_pre.reshape(pair, group_width),
            d_key_pre.reshape(pair, head_dim),
            own_grads[:, head_dim:],
        ],
        axis=1,
    ).astype(BF)
    norm_sum = dot_right_t(d_proj, qkv_part)
    d_first_norm = (
        norm_sum[:tokens]
        + swap(norm_sum[tokens:], "core")
        + dot_right_t(d_middle_low, down_low_full)
        + d_branch
    )
    d_input_part, grad_gain_zero = norm_one_pull(d_first_norm)
    grad_hidden = d_branch + d_input_part

    def reduce_rows(term):
        blocks = term.reshape(line, cores, reps, sub, term.shape[-1])
        parts = [
            lax.dynamic_index_in_dim(blocks, rep_of(k), 2, keepdims=False) for k in range(reps)
        ]
        mine = line_scatter(rep_scatter(parts).astype(BF))
        keep = pick(mine, core)
        other = swap(pick(mine, 1 - core), "core")
        first = core == 0
        both = jnp.stack([jnp.where(first, keep, other), jnp.where(first, other, keep)])
        whole = jnp.zeros((cores, reps, sub, term.shape[-1]), F32)
        for k, block in enumerate(rep_gather(jnp.swapaxes(both, 0, 1))):
            whole = lax.dynamic_update_slice(
                whole,
                jnp.swapaxes(block, 0, 1)[:, None].astype(F32),
                (0, rep_of(k), 0, 0),
            )
        return whole.reshape(cores, weight_rows, term.shape[-1])

    small_terms = (
        jnp.concatenate(
            [dot_left_t(first_norm, d_middle_low), dot_left_t(second_low, d_ple_low)], axis=1
        ).astype(BF),
        jnp.concatenate(
            [dot_left_t(d_side_low, middle), dot_left_t(d_last_low, gated_low)], axis=1
        ).astype(BF),
    )
    small_term = (
        pick(small_terms, core).astype(F32)
        + swap(pick(small_terms, 1 - core), "core").astype(F32)
    ).astype(BF)
    out_term = dot_left_t(d_attn_pair, mixed_low).astype(BF)
    out_red = reduce_rows(jnp.concatenate([out_term, small_term], axis=1))
    qkv_red = reduce_rows(dot_left_t(first_pair, d_proj).astype(BF))
    grad_qkv = jnp.concatenate(
        [qkv_red[c, :, :group_width] for c in range(cores)]
        + [qkv_red[c, :, group_width : group_width + head_dim] for c in range(cores)]
        + [qkv_red[c, :, group_width + head_dim :] for c in range(cores)],
        axis=1,
    )
    grad_out = jnp.concatenate([out_red[c, :, :group_width] for c in range(cores)], axis=1)
    grad_laurel_down = out_red[0, :, group_width : group_width + rank]
    grad_layer_gate = out_red[0, :, group_width + rank :]
    grad_laurel_up = out_red[1, :, group_width : group_width + rank]
    grad_layer_project = out_red[1, :, group_width + rank :]

    model_part = jnp.stack(
        [
            grad_gain_zero,
            grad_gain_one,
            grad_gain_two,
            grad_gain_three,
            grad_gain_four,
            grad_gain_five,
        ]
    )
    head_part = jnp.stack([grad_query_gain, grad_key_gain])
    gains = sum_everywhere(
        jnp.concatenate([model_part.reshape(-1, head_dim), head_part], axis=0)
    )
    grad_model_gains = gains[: -head_part.shape[0]].reshape(model_part.shape)
    grad_head_gains = gains[-head_part.shape[0] :]
    return (
        layer_out,
        grad_hidden,
        grad_vectors,
        grad_model_gains,
        grad_head_gains,
        grad_qkv,
        grad_out,
        grad_laurel_down,
        grad_laurel_up,
        grad_gate_up,
        grad_down,
        grad_layer_gate,
        grad_layer_project,
    )


def solution(mesh):
    reps, shards = mesh.shape["rep"], mesh.shape["shard"]
    fine = Mesh(
        np.asarray(mesh.devices).reshape(reps // 2, 2, shards // 2, 2), ("ra", "rb", "line", "core")
    )
    rows = P(("ra", "rb", "line", "core"), None)
    owned = P(("line", "core"), None)
    return jax.shard_map(
        body,
        mesh=fine,
        in_specs=(rows, rows, P(("ra", "rb", "line", "core")), rows, P(), P()) + (owned,) * 8,
        out_specs=(rows, rows, rows, P(), P()) + (owned,) * 8,
        check_vma=False,
    )
```

time: 3050 us -> 1290 us (0.42)
  waiting for transfers between devices: 2380 us -> 525 us
  starting transfers between devices: 8.06 us -> 266 us
  local copies, waits for them, and re-layouts: 255 us -> 151 us
  other arithmetic: 55.2 us -> 158 us
  blocking collectives: 76.3 us -> 0 us
  matrix products: 244 us -> 179 us
    reduce_scatter x1 -> x0, waiting for transfers between devices: 1180 us -> none  [body(): lax.psum_scatter(make_terms(lefts, rights).astype(jnp.bfloat16), 'shard',...]
    all_gather x6 -> x0, waiting for transfers between devices: 944 us -> none  [the longest x1 562 us: body(): lax.all_gather(gate_up_weight, 'shard', axis=0, tiled=True)]
    ppermute x4 -> x170, waiting for transfers between devices: 19.1 us -> 525 us  [the longest x109 203 us: swap(): return lax.ppermute(value, axis, [(0, 1), (1, 0)])]
    ppermute x4 -> x170, starting transfers between devices: 7.75 us -> 266 us  [the longest x109 103 us: swap(): return lax.ppermute(value, axis, [(0, 1), (1, 0)])]
    psum x1 -> x0, waiting for transfers between devices: 238 us -> none  [body(): summed = lax.psum(shard_part, 'rep').astype(jnp.float32)]
    concatenate x1 -> x6, local copies, waits for them, and re-layouts: 176 us -> 10.7 us  [the longest x1 8.32 us: body(): out_red = reduce_rows(jnp.concatenate([out_term, small_term], axis=1))]
    psum x1 -> x0, blocking collectives: 39.7 us -> none  [body(): lax.psum((model_part, head_part), ('rep', 'shard'))]
    all_gather x2 -> x0, blocking collectives: 36.5 us -> none  [the longest x1 20 us: body(): lax.all_gather(laurel_up, 'shard', axis=0, tiled=True)]
  transfers between devices with their start and end apart: 12 -> 170, of which waited for: 10 -> 59; matrix products, arithmetic and copies ran while one was open for 5% -> 25% of each run, Pallas kernels for 0% -> 0%
where the time goes in v1:
time: 1290 us; the launch traced here: 1280 us
  waiting for transfers between devices  525 us (41%)
  starting transfers between devices  266 us (21%)
  matrix products  179 us (14%)
  other arithmetic  158 us (12%)
  local copies, waits for them, and re-layouts  151 us (12%)
    ppermute x109, waiting for transfers between devices, swap(): return lax.ppermute(value, axis, [(0, 1), (1, 0)])  203 us
    ppermute x9, waiting for transfers between devices, line_slots(): lax.ppermute(downs[-1], 'line', [(i + 1, i) for i in range(0, count - s)])  130 us
    ppermute x15, waiting for transfers between devices, line_scatter(): going_up = lax.ppermute(up, 'line', [(i, i + 1) for i in range(t)])  112 us
    ppermute x109, starting transfers between devices, swap(): return lax.ppermute(value, axis, [(0, 1), (1, 0)])  103 us
    ppermute x15, starting transfers between devices, line_scatter(): going_up = lax.ppermute(up, 'line', [(i, i + 1) for i in range(t)])  68.2 us
    dot_general x8, matrix products, dot_plain(): return jnp.dot(left_side, right_side, preferred_element_type=jnp.float32)  59.8 us
    dot_general x8, matrix products, dot_right_t(): lax.dot_general(left_side, right_side, (((1,), (1,)), ((), ())), preferre...  54.1 us
    dot_general x8, matrix products, dot_left_t(): lax.dot_general(left_side, right_side, (((0,), (0,)), ((), ())), preferre...  47.5 us
  transfers between devices with their start and end apart: 170, of which 59 were waited for; matrix products, arithmetic and copies ran while one was open for 25% of the time, Pallas kernels for 0%

profile of v1, /device:TPU:0, one launch (start us, length us, event | category | flops | bytes accessed | tf_op | source)
XLA Modules:
  0.0 1283.1 jit_solution(5013336668547017768)
XLA Ops:
  47.5 14.9 %collective-permute-done.11 = bf16[2,64,1536]{2,1,0:T(8,128)(2,1)S(1)} collective-permute-done((bf16[2,64,1536]{2,1,0:T(8,128)(2,1)S(1)}, bf16[2,64,1536]{2,1,0:T(8,128)(2,1)S(1)}, u32[]{:S(2)}, u32[]{:S(2)}) %collective-permute-start.11) | collective-permute-done | bytes 393248 | tf_op jit(solution)/shard_map/ppermute | solution.py:121
  244.6 17.5 %collective-permute-done.61 = bf16[512,1024]{1,0:T(8,128)(2,1)S(1)} collective-permute-done((bf16[512,1024]{1,0:T(8,128)(2,1)S(1)}, bf16[512,1024]{1,0:T(8,128)(2,1)S(1)}, u32[]{:S(2)}, u32[]{:S(2)}) %collective-permute-start.61) | collective-permute-done | bytes 1048608 | tf_op jit(solution)/shard_map/ppermute | solution.py:129
  272.3 18.1 %collective-permute-done.56 = bf16[512,1024]{1,0:T(8,128)(2,1)S(1)} collective-permute-done((bf16[512,1024]{1,0:T(8,128)(2,1)}, bf16[512,1024]{1,0:T(8,128)(2,1)S(1)}, u32[]{:S(2)}, u32[]{:S(2)}) %collective-permute-start.56) | collective-permute-done | bytes 1048608 | tf_op jit(solution)/shard_map/ppermute | solution.py:130
  297.1 15.8 %collective-permute-done.63 = bf16[512,1024]{1,0:T(8,128)(2,1)S(1)} collective-permute-done((bf16[512,1024]{1,0:T(8,128)(2,1)S(1)}, bf16[512,1024]{1,0:T(8,128)(2,1)S(1)}, u32[]{:S(2)}, u32[]{:S(2)}) %collective-permute-start.63) | collective-permute-done | bytes 1048608 | tf_op jit(solution)/shard_map/ppermute | solution.py:130
  316.3 19.0 %collective-permute-done.57 = bf16[512,1024]{1,0:T(8,128)(2,1)S(1)} collective-permute-done((bf16[512,1024]{1,0:T(8,128)(2,1)S(1)}, bf16[512,1024]{1,0:T(8,128)(2,1)S(1)}, u32[]{:S(2)}, u32[]{:S(2)}) %collective-permute-start.57) | collective-permute-done | bytes 1048608 | tf_op jit(solution)/shard_map/ppermute | solution.py:130
  340.9 16.9 %collective-permute-done.69 = bf16[512,1024]{1,0:T(8,128)(2,1)S(1)} collective-permute-done((bf16[512,1024]{1,0:T(8,128)(2,1)S(1)}, bf16[512,1024]{1,0:T(8,128)(2,1)S(1)}, u32[]{:S(2)}, u32[]{:S(2)}) %collective-permute-start.69) | collective-permute-done | bytes 1048608 | tf_op jit(solution)/shard_map/ppermute | solution.py:130
  364.2 16.1 %collective-permute-done.64 = bf16[512,1024]{1,0:T(8,128)(2,1)S(1)} collective-permute-done((bf16[512,1024]{1,0:T(8,128)(2,1)S(1)}, bf16[512,1024]{1,0:T(8,128)(2,1)S(1)}, u32[]{:S(2)}, u32[]{:S(2)}) %collective-permute-start.64) | collective-permute-done | bytes 1048608 | tf_op jit(solution)/shard_map/ppermute | solution.py:130
  382.7 18.4 %collective-permute-done.70 = bf16[512,1024]{1,0:T(8,128)(2,1)S(1)} collective-permute-done((bf16[512,1024]{1,0:T(8,128)(2,1)S(1)}, bf16[512,1024]{1,0:T(8,128)(2,1)S(1)}, u32[]{:S(2)}, u32[]{:S(2)}) %collective-permute-start.70) | collective-permute-done | bytes 1048608 | tf_op jit(solution)/shard_map/ppermute | solution.py:130
  409.2 19.8 %collective-permute-done.71 = bf16[512,1024]{1,0:T(8,128)(2,1)S(1)} collective-permute-done((bf16[512,1024]{1,0:T(8,128)(2,1)S(1)}, bf16[512,1024]{1,0:T(8,128)(2,1)S(1)}, u32[]{:S(2)}, u32[]{:S(2)}) %collective-permute-start.71) | collective-permute-done | bytes 1048608 | tf_op jit(solution)/shard_map/ppermute | solution.py:130
  432.7 22.7 %fusion.10 = f32[2048,2048]{1,0:T(8,128)S(1)} fusion(bf16[2048,2048]{1,0:T(8,128)(2,1)} %constant_dynamic-update-slice_fusion.3, bf16[2048,1024]{1,0:T(8,128)(2,1)} %bitcast.636, bf16[2048,1024]{1,0:T(8,128)(2,1)} %bitcast.638), kind=kOutput, calls=%fused_computation.27 | convolution fusion | flops 17196646400 | bytes 33554432 | tf_op jit(solution)/shard_map/dot_general | solution.py:47
  498.7 21.8 %collective-permute-done.81 = bf16[256,2048]{1,0:T(8,128)(2,1)S(1)} collective-permute-done((bf16[256,2048]{1,0:T(8,128)(2,1)S(1)}, bf16[256,2048]{1,0:T(8,128)(2,1)S(1)}, u32[]{:S(2)}, u32[]{:S(2)}) %collective-permute-start.81) | collective-permute-done | bytes 1048608 | tf_op jit(solution)/shard_map/ppermute | solution.py:71
  538.4 19.1 %collective-permute-done.85 = bf16[256,2048]{1,0:T(8,128)(2,1)} collective-permute-done((bf16[256,2048]{1,0:T(8,128)(2,1)}, bf16[256,2048]{1,0:T(8,128)(2,1)}, u32[]{:S(2)}, u32[]{:S(2)}) %collective-permute-start.85) | collective-permute-done | bytes 1048608 | tf_op jit(solution)/shard_map/ppermute | solution.py:71
  580.0 24.2 %fusion.21 = (f32[2048,1024]{1,0:T(8,128)}, f32[2048,1024]{1,0:T(8,128)}) fusion(f32[2048,2048]{1,0:T(8,128)} %copy-done.17, bf16[2048,2048]{1,0:T(8,128)(2,1)} %constant_dynamic-update-slice_fusion.12, bf16[2048,1024]{1,0:T(8,128)(2,1)S(1)} %bitcast.635), kind=kOutput, calls=%fused_computation.61 | convolution fusion | flops 8636071936 | bytes 46137344 | tf_op jit(solution)/shard_map/dot_general | solution.py:47
  604.2 24.7 %convolution_convert_fusion.2 = bf16[2048,2048]{1,0:T(8,128)(2,1)} fusion(bf16[2048,1024]{1,0:T(8,128)(2,1)} %bitcast.637, bf16[2048,1024]{1,0:T(8,128)(2,1)} %bitcast.639, f32[2048,1024]{1,0:T(8,128)} %get-tuple-element.76, f32[2048,1024]{1,0:T(8,128)} %get-tuple-element.75), kind=kOutput, calls=%fused_computation.23 | convolution fusion | flops 17209229312 | bytes 33554432 | tf_op jit(solution)/shard_map/dot_general | solution.py:51
  628.9 26.5 %convolution_convert_fusion = bf16[2048,2048]{1,0:T(8,128)(2,1)} fusion(bf16[2048,2048]{1,0:T(8,128)(2,1)} %constant_dynamic-update-slice_fusion.3, f32[2048,1024]{1,0:T(8,128)} %get-tuple-element.76, f32[2048,1024]{1,0:T(8,128)} %get-tuple-element.75), kind=kOutput, calls=%fused_computation.21 | convolution fusion | flops 17192452096 | bytes 33554432 | tf_op jit(solution)/shard_map/dot_general | solution.py:57
  701.9 20.2 %collective-permute-done.148 = bf16[512,1024]{1,0:T(8,128)(2,1)} collective-permute-done((bf16[512,1024]{1,0:T(8,128)(2,1)}, bf16[512,1024]{1,0:T(8,128)(2,1)}, u32[]{:S(2)}, u32[]{:S(2)}) %collective-permute-start.148) | collective-permute-done | bytes 1048608 | tf_op jit(solution)/shard_map/ppermute | solution.py:160
  725.4 18.2 %collective-permute-done.159 = bf16[512,1024]{1,0:T(8,128)(2,1)} collective-permute-done((bf16[512,1024]{1,0:T(8,128)(2,1)S(1)}, bf16[512,1024]{1,0:T(8,128)(2,1)}, u32[]{:S(2)}, u32[]{:S(2)}) %collective-permute-start.159) | collective-permute-done | bytes 1048608 | tf_op jit(solution)/shard_map/ppermute | solution.py:160
  755.0 16.7 %collective-permute-done.138 = bf16[512,1024]{1,0:T(8,128)(2,1)} collective-permute-done((bf16[512,1024]{1,0:T(8,128)(2,1)S(1)}, bf16[512,1024]{1,0:T(8,128)(2,1)}, u32[]{:S(2)}, u32[]{:S(2)}) %collective-permute-start.138) | collective-permute-done | bytes 1048608 | tf_op jit(solution)/shard_map/ppermute | solution.py:160
  773.4 20.8 %collective-permute-done.149 = bf16[512,1024]{1,0:T(8,128)(2,1)S(1)} collective-permute-done((bf16[512,1024]{1,0:T(8,128)(2,1)S(1)}, bf16[512,1024]{1,0:T(8,128)(2,1)S(1)}, u32[]{:S(2)}, u32[]{:S(2)}) %collective-permute-start.149) | collective-permute-done | bytes 1048608 | tf_op jit(solution)/shard_map/ppermute | solution.py:160
  840.6 19.8 %collective-permute-start.161 = (bf16[512,1024]{1,0:T(8,128)(2,1)}, bf16[512,1024]{1,0:T(8,128)(2,1)}, u32[]{:S(2)}, u32[]{:S(2)}) collective-permute-start(bf16[512,1024]{1,0:T(8,128)(2,1)} %get-tuple-element.110), channel_id=1, source_target_pairs={{0,2},{2,4},{4,6},{1,3},{3,5},{5,7},{8,10},{10,12},{12,14},{9,11},... | collective-permute-start | bytes 3145736 | tf_op jit(solution)/shard_map/ppermute | solution.py:160
  947.3 13.3 %collective-permute-start.164 = (bf16[512,1024]{1,0:T(8,128)(2,1)S(1)}, bf16[512,1024]{1,0:T(8,128)(2,1)S(1)}, u32[]{:S(2)}, u32[]{:S(2)}) collective-permute-start(bf16[512,1024]{1,0:T(8,128)(2,1)S(1)} %copy-done.78), channel_id=1, source_target_pairs={{6,4},{4,2},{2,0},{7,5},{5,3},{3,1},{14,12},{12,10},{10,8},{15,13}... | collective-permute-start | bytes 3145736 | tf_op jit(solution)/shard_map/ppermute | solution.py:161
  1031.1 15.2 %collective-permute-done.155 = bf16[256,2048]{1,0:T(8,128)(2,1)} collective-permute-done((bf16[256,2048]{1,0:T(8,128)(2,1)}, bf16[256,2048]{1,0:T(8,128)(2,1)}, u32[]{:S(2)}, u32[]{:S(2)}) %collective-permute-start.155) | collective-permute-done | bytes 1048608 | tf_op jit(solution)/shard_map/ppermute | solution.py:71
  1080.1 26.8 %collective-permute-done.125 = bf16[4,2,64,1344]{3,2,1,0:T(8,128)(2,1)S(1)} collective-permute-done((bf16[4,2,64,1344]{3,2,1,0:T(8,128)(2,1)S(1)}, bf16[4,2,64,1344]{3,2,1,0:T(8,128)(2,1)S(1)}, u32[]{:S(2)}, u32[]{:S(2)}) %collective-permute-start.125) | collective-permute-done | bytes 1376288 | tf_op jit(solution)/shard_map/ppermute | solution.py:71
  1123.1 28.8 %collective-permute-done.147 = bf16[128,2048]{1,0:T(8,128)(2,1)} collective-permute-done((bf16[128,2048]{1,0:T(8,128)(2,1)}, bf16[128,2048]{1,0:T(8,128)(2,1)}, u32[]{:S(2)}, u32[]{:S(2)}) %collective-permute-start.147) | collective-permute-done | bytes 524320 | tf_op jit(solution)/shard_map/ppermute | solution.py:71
  (997 shorter events, 803.0 us)
Async XLA Ops:
  169.1 64.8 %collective-permute-start.60 = (bf16[256,1024]{1,0:T(8,128)(2,1)}, bf16[256,1024]{1,0:T(8,128)(2,1)}, u32[]{:S(2)}, u32[]{:S(2)}) collective-permute-start(bf16[256,1024]{1,0:T(8,128)(2,1)} %get-tuple-element.97), channel_id=1, source_target_pairs={{0,1},{1,0},{2,3},{3,2},{4,5},{5,4},{6,7},{7,6},{8,9},{9,8},{10,11... | collective-permute-start | bytes 1572872 | tf_op jit(solution)/shard_map/ppermute | solution.py:71
  169.2 66.2 %collective-permute-start.54 = (bf16[512,1024]{1,0:T(8,128)(2,1)}, bf16[512,1024]{1,0:T(8,128)(2,1)}, u32[]{:S(2)}, u32[]{:S(2)}) collective-permute-start(bf16[512,1024]{1,0:T(8,128)(2,1)} %pad_maximum_fusion.19), channel_id=1, source_target_pairs={{0,2},{2,4},{4,6},{1,3},{3,5},{5,7},{8,10},{10,12},{12,14},{9,11},... | collective-permute-start | bytes 3145736 | tf_op jit(solution)/shard_map/ppermute | solution.py:129
  230.9 61.6 %collective-permute-start.43 = (f32[256,2048]{1,0:T(8,128)S(1)}, f32[256,2048]{1,0:T(8,128)S(1)}, u32[]{:S(2)}, u32[]{:S(2)}) collective-permute-start(f32[256,2048]{1,0:T(8,128)S(1)} %slice.587), channel_id=1, source_target_pairs={{0,1},{1,0},{2,3},{3,2},{4,5},{5,4},{6,7},{7,6},{8,9},{9,8},{10,11... | collective-permute-start | bytes 6291464 | tf_op jit(solution)/shard_map/ppermute | solution.py:71
  267.9 68.7 %collective-permute-start.68 = (bf16[512,1024]{1,0:T(8,128)(2,1)S(1)}, bf16[512,1024]{1,0:T(8,128)(2,1)S(1)}, u32[]{:S(2)}, u32[]{:S(2)}) collective-permute-start(bf16[512,1024]{1,0:T(8,128)(2,1)S(1)} %pad_maximum_fusion.21), channel_id=1, source_target_pairs={{0,2},{2,4},{4,6},{1,3},{3,5},{5,7},{8,10},{10,12},{12,14},{9,11},... | collective-permute-start | bytes 3145736 | tf_op jit(solution)/shard_map/ppermute | solution.py:129
  677.5 75.7 %collective-permute-start.140 = (bf16[512,1024]{1,0:T(8,128)(2,1)S(1)}, bf16[512,1024]{1,0:T(8,128)(2,1)}, u32[]{:S(2)}, u32[]{:S(2)}) collective-permute-start(bf16[512,1024]{1,0:T(8,128)(2,1)S(1)} %get-tuple-element.121), channel_id=1, source_target_pairs={{6,4},{7,5},{14,12},{15,13},{22,20},{23,21},{30,28},{31,29}} | collective-permute-start | bytes 3145736 | tf_op jit(solution)/shard_map/ppermute | solution.py:161
  682.8 72.1 %collective-permute-start.151 = (bf16[512,1024]{1,0:T(8,128)(2,1)S(1)}, bf16[512,1024]{1,0:T(8,128)(2,1)}, u32[]{:S(2)}, u32[]{:S(2)}) collective-permute-start(bf16[512,1024]{1,0:T(8,128)(2,1)S(1)} %get-tuple-element.117), channel_id=1, source_target_pairs={{6,4},{7,5},{14,12},{15,13},{22,20},{23,21},{30,28},{31,29}} | collective-permute-start | bytes 3145736 | tf_op jit(solution)/shard_map/ppermute | solution.py:161
  685.4 58.2 %collective-permute-start.159 = (bf16[512,1024]{1,0:T(8,128)(2,1)S(1)}, bf16[512,1024]{1,0:T(8,128)(2,1)}, u32[]{:S(2)}, u32[]{:S(2)}) collective-permute-start(bf16[512,1024]{1,0:T(8,128)(2,1)S(1)} %get-tuple-element.112), channel_id=1, source_target_pairs={{0,2},{1,3},{8,10},{9,11},{16,18},{17,19},{24,26},{25,27}} | collective-permute-start | bytes 3145736 | tf_op jit(solution)/shard_map/ppermute | solution.py:160
  699.5 51.3 %collective-permute-start.96 = (bf16[128,2048]{1,0:T(8,128)(2,1)S(1)}, bf16[128,2048]{1,0:T(8,128)(2,1)S(1)}, u32[]{:S(2)}, u32[]{:S(2)}) collective-permute-start(bf16[128,2048]{1,0:T(8,128)(2,1)S(1)} %get-tuple-element.159), channel_id=1, source_target_pairs={{0,8},{8,0},{1,9},{9,1},{2,10},{10,2},{3,11},{11,3},{4,12},{12,4},... | collective-permute-start | bytes 1572872 | tf_op jit(solution)/shard_map/ppermute | solution.py:71
  752.4 52.0 %collective-permute-start.162 = (bf16[512,1024]{1,0:T(8,128)(2,1)S(1)}, bf16[512,1024]{1,0:T(8,128)(2,1)S(1)}, u32[]{:S(2)}, u32[]{:S(2)}) collective-permute-start(bf16[512,1024]{1,0:T(8,128)(2,1)S(1)} %get-tuple-element.113), channel_id=1, source_target_pairs={{6,4},{7,5},{14,12},{15,13},{22,20},{23,21},{30,28},{31,29}} | collective-permute-start | bytes 3145736 | tf_op jit(solution)/shard_map/ppermute | solution.py:161
  753.3 61.7 %collective-permute-start.160 = (bf16[512,1024]{1,0:T(8,128)(2,1)S(1)}, bf16[512,1024]{1,0:T(8,128)(2,1)S(1)}, u32[]{:S(2)}, u32[]{:S(2)}) collective-permute-start(bf16[512,1024]{1,0:T(8,128)(2,1)S(1)} %fusion.48), channel_id=1, source_target_pairs={{0,2},{2,4},{1,3},{3,5},{8,10},{10,12},{9,11},{11,13},{16,18},{18,... | collective-permute-start | bytes 3145736 | tf_op jit(solution)/shard_map/ppermute | solution.py:160
  754.9 67.9 %collective-permute-start.90 = (bf16[256,2048]{1,0:T(8,128)(2,1)}, bf16[256,2048]{1,0:T(8,128)(2,1)S(1)}, u32[]{:S(2)}, u32[]{:S(2)}) collective-permute-start(bf16[256,2048]{1,0:T(8,128)(2,1)} %get-tuple-element.83), channel_id=1, source_target_pairs={{0,1},{1,0},{2,3},{3,2},{4,5},{5,4},{6,7},{7,6},{8,9},{9,8},{10,11... | collective-permute-start | bytes 3145736 | tf_op jit(solution)/shard_map/ppermute | solution.py:71
  771.7 51.9 %collective-permute-start.97 = (bf16[256,2048]{1,0:T(8,128)(2,1)S(1)}, bf16[256,2048]{1,0:T(8,128)(2,1)S(1)}, u32[]{:S(2)}, u32[]{:S(2)}) collective-permute-start(bf16[256,2048]{1,0:T(8,128)(2,1)S(1)} %pad_maximum_fusion.26), channel_id=1, source_target_pairs={{0,16},{16,0},{1,17},{17,1},{2,18},{18,2},{3,19},{19,3},{4,20},{20... | collective-permute-start | bytes 3145736 | tf_op jit(solution)/shard_map/ppermute | solution.py:71
  815.0 132.0 %collective-permute-start.139 = (bf16[512,1024]{1,0:T(8,128)(2,1)}, bf16[512,1024]{1,0:T(8,128)(2,1)}, u32[]{:S(2)}, u32[]{:S(2)}) collective-permute-start(bf16[512,1024]{1,0:T(8,128)(2,1)} %get-tuple-element.118), channel_id=1, source_target_pairs={{0,2},{2,4},{4,6},{1,3},{3,5},{5,7},{8,10},{10,12},{12,14},{9,11},... | collective-permute-start | bytes 3145736 | tf_op jit(solution)/shard_map/ppermute | solution.py:160
  835.7 137.0 %collective-permute-start.150 = (bf16[512,1024]{1,0:T(8,128)(2,1)}, bf16[512,1024]{1,0:T(8,128)(2,1)}, u32[]{:S(2)}, u32[]{:S(2)}) collective-permute-start(bf16[512,1024]{1,0:T(8,128)(2,1)} %get-tuple-element.114), channel_id=1, source_target_pairs={{0,2},{2,4},{4,6},{1,3},{3,5},{5,7},{8,10},{10,12},{12,14},{9,11},... | collective-permute-start | bytes 3145736 | tf_op jit(solution)/shard_map/ppermute | solution.py:160
  840.6 136.6 %collective-permute-start.161 = (bf16[512,1024]{1,0:T(8,128)(2,1)}, bf16[512,1024]{1,0:T(8,128)(2,1)}, u32[]{:S(2)}, u32[]{:S(2)}) collective-permute-start(bf16[512,1024]{1,0:T(8,128)(2,1)} %get-tuple-element.110), channel_id=1, source_target_pairs={{0,2},{2,4},{4,6},{1,3},{3,5},{5,7},{8,10},{10,12},{12,14},{9,11},... | collective-permute-start | bytes 3145736 | tf_op jit(solution)/shard_map/ppermute | solution.py:160
  863.2 97.4 %collective-permute-start.142 = (bf16[512,1024]{1,0:T(8,128)(2,1)}, bf16[512,1024]{1,0:T(8,128)(2,1)}, u32[]{:S(2)}, u32[]{:S(2)}) collective-permute-start(bf16[512,1024]{1,0:T(8,128)(2,1)} %fusion.59), channel_id=1, source_target_pairs={{6,4},{4,2},{2,0},{7,5},{5,3},{3,1},{14,12},{12,10},{10,8},{15,13}... | collective-permute-start | bytes 3145736 | tf_op jit(solution)/shard_map/ppermute | solution.py:161
  1012.2 56.5 %collective-permute-start.166 = (bf16[256,2048]{1,0:T(8,128)(2,1)S(1)}, bf16[256,2048]{1,0:T(8,128)(2,1)S(1)}, u32[]{:S(2)}, u32[]{:S(2)}) collective-permute-start(bf16[256,2048]{1,0:T(8,128)(2,1)S(1)} %copy-done.80), channel_id=1, source_target_pairs={{0,8},{8,0},{1,9},{9,1},{2,10},{10,2},{3,11},{11,3},{4,12},{12,4},... | collective-permute-start | bytes 3145736 | tf_op jit(solution)/shard_map/ppermute | solution.py:71
  1023.8 52.1 %collective-permute-start.167 = (bf16[256,2048]{1,0:T(8,128)(2,1)S(1)}, bf16[256,2048]{1,0:T(8,128)(2,1)S(1)}, u32[]{:S(2)}, u32[]{:S(2)}) collective-permute-start(bf16[256,2048]{1,0:T(8,128)(2,1)S(1)} %copy-done.80), channel_id=1, source_target_pairs={{0,16},{16,0},{1,17},{17,1},{2,18},{18,2},{3,19},{19,3},{4,20},{20... | collective-permute-start | bytes 3145736 | tf_op jit(solution)/shard_map/ppermute | solution.py:71
  1031.1 80.6 %collective-permute-start.100 = (f32[256,2048]{1,0:T(8,128)S(1)}, f32[256,2048]{1,0:T(8,128)S(1)}, u32[]{:S(2)}, u32[]{:S(2)}) collective-permute-start(f32[256,2048]{1,0:T(8,128)S(1)} %copy-done.69), channel_id=1, source_target_pairs={{0,1},{1,0},{2,3},{3,2},{4,5},{5,4},{6,7},{7,6},{8,9},{9,8},{10,11... | collective-permute-start | bytes 6291464 | tf_op jit(solution)/shard_map/ppermute | solution.py:71
  1046.3 60.5 %collective-permute-start.125 = (bf16[4,2,64,1344]{3,2,1,0:T(8,128)(2,1)S(1)}, bf16[4,2,64,1344]{3,2,1,0:T(8,128)(2,1)S(1)}, u32[]{:S(2)}, u32[]{:S(2)}) collective-permute-start(bf16[4,2,64,1344]{3,2,1,0:T(8,128)(2,1)S(1)} %copy-done.73), channel_id=1, source_target_pairs={{0,16},{16,0},{1,17},{17,1},{2,18},{18,2},{3,19},{19,3},{4,20},{20... | collective-permute-start | bytes 4128776 | tf_op jit(solution)/shard_map/ppermute | solution.py:71
  1053.5 54.8 %collective-permute-start.123 = (bf16[4,2,64,1344]{3,2,1,0:T(8,128)(2,1)S(1)}, bf16[4,2,64,1344]{3,2,1,0:T(8,128)(2,1)S(1)}, u32[]{:S(2)}, u32[]{:S(2)}) collective-permute-start(bf16[4,2,64,1344]{3,2,1,0:T(8,128)(2,1)S(1)} %copy-done.72), channel_id=1, source_target_pairs={{0,8},{8,0},{1,9},{9,1},{2,10},{10,2},{3,11},{11,3},{4,12},{12,4},... | collective-permute-start | bytes 4128776 | tf_op jit(solution)/shard_map/ppermute | solution.py:71
  1068.6 130.9 %collective-permute-start.109 = (bf16[4,2,64,1536]{3,2,1,0:T(8,128)(2,1)}, bf16[4,2,64,1536]{3,2,1,0:T(8,128)(2,1)}, u32[]{:S(2)}, u32[]{:S(2)}) collective-permute-start(bf16[4,2,64,1536]{3,2,1,0:T(8,128)(2,1)} %pad_maximum_fusion.9), channel_id=1, source_target_pairs={{0,16},{16,0},{1,17},{17,1},{2,18},{18,2},{3,19},{19,3},{4,20},{20... | collective-permute-start | bytes 4718600 | tf_op jit(solution)/shard_map/ppermute | solution.py:71
  1075.9 123.6 %collective-permute-start.107 = (bf16[4,2,64,1536]{3,2,1,0:T(8,128)(2,1)}, bf16[4,2,64,1536]{3,2,1,0:T(8,128)(2,1)}, u32[]{:S(2)}, u32[]{:S(2)}) collective-permute-start(bf16[4,2,64,1536]{3,2,1,0:T(8,128)(2,1)} %pad_maximum_fusion.8), channel_id=1, source_target_pairs={{0,8},{8,0},{1,9},{9,1},{2,10},{10,2},{3,11},{11,3},{4,12},{12,4},... | collective-permute-start | bytes 4718600 | tf_op jit(solution)/shard_map/ppermute | solution.py:71
  1111.7 57.5 %collective-permute-start.158 = (bf16[128,2048]{1,0:T(8,128)(2,1)}, bf16[128,2048]{1,0:T(8,128)(2,1)}, u32[]{:S(2)}, u32[]{:S(2)}) collective-permute-start(bf16[128,2048]{1,0:T(8,128)(2,1)} %slice.663), channel_id=1, source_target_pairs={{0,16},{16,0},{1,17},{17,1},{2,18},{18,2},{3,19},{19,3},{4,20},{20... | collective-permute-start | bytes 1572872 | tf_op jit(solution)/shard_map/ppermute | solution.py:71
  (309 other events, 6826.9 us)

commit v2 on v1

v2 whole, which is shorter than its diff:
```python
import functools
import math

import jax
import jax.numpy as jnp
import numpy as np
from jax import lax
from jax.sharding import Mesh
from jax.sharding import PartitionSpec as P

WINDOW = 512
EPSILON = 1e-06
SQRT_HALF = 0.7071067811865476
BF = jnp.bfloat16
F32 = jnp.float32


def scaled_norm(values, gain_row):
    return (
        values * lax.rsqrt(jnp.mean(values * values, axis=-1, keepdims=True) + EPSILON) * gain_row
    )


def rotate(values, cosine, sine_part):
    half_dim = values.shape[-1] // 2
    first_half = values[..., :half_dim]
    second_half = values[..., half_dim:]
    return jnp.concatenate(
        [
            first_half * cosine - second_half * sine_part,
            second_half * cosine + first_half * sine_part,
        ],
        axis=-1,
    )


def rope_tables(positions, head_dim):
    half_dim = head_dim // 2
    frequency = jnp.exp(
        jnp.arange(half_dim, dtype=jnp.float32) * (-2.0 * math.log(10000.0) / head_dim)
    )
    phase_angle = positions.astype(jnp.float32)[:, None] * frequency[None, :]
    return (jnp.cos(phase_angle)[:, None, :], jnp.sin(phase_angle)[:, None, :])


def dot_plain(left_side, right_side):
    return jnp.dot(left_side, right_side, preferred_element_type=jnp.float32)


def dot_right_t(left_side, right_side):
    return lax.dot_general(
        left_side, right_side, (((1,), (1,)), ((), ())), preferred_element_type=jnp.float32
    )


def dot_left_t(left_side, right_side):
    return lax.dot_general(
        left_side, right_side, (((0,), (0,)), ((), ())), preferred_element_type=jnp.float32
    )


def gelu_tanh(values):
    return jax.nn.gelu(values, approximate=True)


def after(value, *others):
    return lax.optimization_barrier((value,) + others)[0]


def gelu_terms(gate, up):
    root = 0.7978845608
    square = gate * gate
    bend = jnp.tanh(root * (gate + 0.044715 * gate * square))
    half = 0.5 * (1.0 + bend)
    value = gate * half
    slope = half + 0.5 * gate * (1.0 - bend * bend) * root * (1.0 + 3.0 * 0.044715 * square)
    return value.astype(BF), (slope * up).astype(BF)


def swap(value, axis):
    return lax.ppermute(value, axis, [(0, 1), (1, 0)])


def place_on(axes):
    place = jnp.int32(0)
    for axis in axes:
        place = place * 2 + lax.axis_index(axis)
    return place


def combine(*values):
    total = values[0].astype(F32)
    for value in values[1:]:
        total = total + value.astype(F32)
    return total.astype(BF)


class Order:
    def __init__(self):
        self.last = ()

    def go(self, *values):
        return list(lax.optimization_barrier(values + self.last)[: len(values)])

    def mark(self, *values):
        self.last = tuple(values)
        return list(values)

    def put(self, value, axis):
        return Transfer(swap(value, axis))

    def wait(self, *transfers):
        for transfer, value in zip(
            transfers, self.mark(*self.go(*[transfer.value for transfer in transfers]))
        ):
            transfer.value = value


class Transfer:
    def __init__(self, value):
        self.value = value


class Gather:
    def __init__(self, value, axes, order):
        self.axes, self.order, self.value = axes, order, value
        self.sent = [order.put(value, axis) for axis in axes] if len(axes) == 2 else []
        self.first = self.sent

    def next(self):
        if len(self.axes) == 2:
            half = self.value.shape[0] // 2
            from_one, from_two = [transfer.value for transfer in self.sent]
            self.sent = [
                self.order.put(from_two[half:], self.axes[0]),
                self.order.put(from_one[:half], self.axes[1]),
            ]

    def near_blocks(self):
        return [self.value, self.first[1].value, self.first[0].value]

    def far_block(self):
        return jnp.concatenate([self.sent[1].value, self.sent[0].value], axis=0)

    def blocks(self):
        if len(self.axes) == 2:
            return self.near_blocks() + [self.far_block()]
        blocks = [self.value]
        for axis in reversed(self.axes):
            blocks = blocks + [swap(block, axis) for block in blocks]
        return blocks


class Scatter:
    def __init__(self, parts, axes, order):
        self.parts, self.axes, self.order = parts, axes, order
        self.half = parts[0].shape[0] // 2
        self.sent = []
        if len(axes) == 2:
            self.sent = [
                order.put(parts[3][self.half :], axes[0]),
                order.put(parts[3][: self.half], axes[1]),
            ]

    def next(self):
        if len(self.axes) == 2:
            half, (own, one, two, far) = self.half, self.parts
            via_two, via_one = [transfer.value for transfer in self.sent]
            two = jnp.concatenate([combine(two[:half], via_one), two[half:]], axis=0)
            one = jnp.concatenate([one[:half], combine(one[half:], via_two)], axis=0)
            self.sent = [self.order.put(two, self.axes[0]), self.order.put(one, self.axes[1])]

    def total(self):
        parts = self.parts
        if len(self.axes) != 2:
            for axis in self.axes:
                half = len(parts) // 2
                parts = [
                    combine(mine, swap(theirs, axis))
                    for mine, theirs in zip(parts[:half], parts[half:])
                ]
            return parts[0].astype(F32)
        total = parts[0].astype(F32)
        for transfer in self.sent:
            total = total + transfer.value.astype(F32)
        return total


def reorder(blocks, axes):
    count = len(axes)
    for bit, axis in enumerate(reversed(axes)):
        flip = lax.axis_index(axis) == 1
        blocks = [jnp.where(flip, blocks[k ^ (1 << bit)], blocks[k]) for k in range(1 << count)]
    return blocks


def stack_pair(mine, other, axis, dim):
    first = lax.axis_index(axis) == 0
    return jnp.stack([jnp.where(first, mine, other), jnp.where(first, other, mine)], axis=dim)


def pick(value, which, dim=0):
    return lax.dynamic_index_in_dim(value, which, dim, keepdims=False)


def body(
    rep_axes,
    line_axes,
    hidden_in,
    layer_vectors,
    positions,
    cotangent,
    model_gains,
    head_gains,
    qkv_weight,
    out_weight,
    laurel_down,
    laurel_up,
    gate_up_weight,
    down_weight,
    layer_gate,
    layer_project,
):
    far_axes, near_axis = line_axes[:-1], line_axes[-1]
    team_axes = rep_axes
    shard_axes = line_axes + ("core",)
    tokens, width = hidden_in.shape
    head_dim = head_gains.shape[1]
    query_heads = out_weight.shape[1] // head_dim
    kv_heads = (qkv_weight.shape[1] // head_dim - query_heads) // 2
    group = query_heads // kv_heads
    ffn_units = down_weight.shape[1]
    rank = laurel_down.shape[1]
    score_scale = 1.0 / math.sqrt(head_dim)
    reps = 1 << len(rep_axes)
    line = 1 << len(line_axes)
    teams = 1 << len(far_axes)
    cores = 2
    core = lax.axis_index("core")
    rep = place_on(rep_axes)
    near = lax.axis_index(near_axis)
    weight_rows = qkv_weight.shape[0]
    group_width = group * head_dim
    kv_width = 2 * head_dim
    query_part = group_width // reps
    kv_part = kv_width // reps
    units = ffn_units // reps
    pair = 2 * tokens
    assert kv_heads == cores and pair >= WINDOW

    order = Order()
    go, mark, put, wait = order.go, order.mark, order.put, order.wait

    def waits(*transfers):
        wait(*[transfer for transfer in transfers if transfer is not None])

    def qkv_columns(c):
        key_start = query_heads * head_dim + c * head_dim
        value_start = (query_heads + kv_heads) * head_dim + c * head_dim
        offset = rep * kv_part
        kv_start = jnp.where(offset < head_dim, key_start + offset, value_start + offset - head_dim)
        return jnp.concatenate(
            [
                lax.dynamic_slice_in_dim(
                    qkv_weight, c * group_width + rep * query_part, query_part, 1
                ),
                lax.dynamic_slice_in_dim(qkv_weight, kv_start, kv_part, 1),
            ],
            axis=1,
        )

    def out_columns(c):
        return lax.dynamic_slice_in_dim(
            out_weight, c * group_width + rep * query_part, query_part, 1
        )

    attention_rows = jnp.concatenate(
        [qkv_columns(c) for c in range(cores)]
        + [out_columns(c) for c in range(cores)]
        + [laurel_down, laurel_up, layer_gate, layer_project],
        axis=1,
    )
    attention_whole = lax.all_gather(attention_rows, shard_axes, axis=0, tiled=True)
    part = query_part + kv_part
    qkv_own = lax.dynamic_slice_in_dim(attention_whole, core * part, part, 1)
    out_own = lax.dynamic_slice_in_dim(
        attention_whole, cores * part + core * query_part, query_part, 1
    )

    def ffn_rows(source, start):
        return lax.dynamic_slice_in_dim(source, start + rep * units, units, 1)

    ffn_mine = jnp.concatenate(
        [
            ffn_rows(gate_up_weight, 0),
            ffn_rows(gate_up_weight, ffn_units),
            ffn_rows(down_weight, 0),
        ],
        axis=1,
    )
    hidden_sent = put(hidden_in, "core")
    pos_sent = put(positions, "core")
    wait(hidden_sent, pos_sent)

    hidden_pair = jnp.concatenate([hidden_in, hidden_sent.value], axis=0)
    pos_pair = jnp.concatenate([positions, pos_sent.value], axis=0)
    steps = jnp.arange(tokens, dtype=jnp.int32)
    index = jnp.concatenate([core * tokens + steps, (1 - core) * tokens + steps])
    hidden_f = hidden_in.astype(F32)
    first_pair = scaled_norm(hidden_pair.astype(F32), model_gains[0]).astype(BF)
    normed_one, norm_one_pull = jax.vjp(scaled_norm, hidden_f, model_gains[0])
    cosine, sine_part = rope_tables(pos_pair, head_dim)
    first_pair, cosine, sine_part = mark(first_pair, cosine, sine_part)
    first_norm = first_pair[:tokens]
    ffn_mine, qkv_own, out_own = mark(*go(ffn_mine, qkv_own, out_own))
    ffn_whole = lax.all_gather(ffn_mine, shard_axes, axis=0, tiled=True)
    gate_up_cols = ffn_whole[:, : 2 * units]
    down_cols = ffn_whole[:, 2 * units :]
    qkv_gather = Gather(qkv_own, rep_axes, order)
    ple = layer_gate.shape[1]
    small_full = go(attention_whole)[0][:, cores * (part + query_part) :]
    down_low_full = small_full[:, :rank]
    up_low_full = small_full[:, rank : 2 * rank]
    gate_layer_full = small_full[:, 2 * rank : 2 * rank + ple]
    project_full = small_full[:, 2 * rank + ple :]
    middle = dot_plain(first_norm, down_low_full).astype(BF)
    side_pre, middle = mark(dot_right_t(middle, up_low_full), middle)
    waits(*qkv_gather.sent)
    qkv_gather.next()
    waits(*qkv_gather.sent)
    ordered_heads = query_part != head_dim

    def head_order(blocks):
        return reorder(blocks, rep_axes) if ordered_heads else blocks

    out_gather = Gather(go(out_own)[0], rep_axes, order)
    qkv_blocks = qkv_gather.blocks()
    (qkv_part,) = mark(
        jnp.concatenate(
            head_order([block[:, :query_part] for block in qkv_blocks])
            + reorder([block[:, query_part:] for block in qkv_blocks], rep_axes),
            axis=1,
        )
    )
    proj = dot_plain(first_pair, qkv_part)
    query_pre = proj[:, :group_width].reshape(pair, group, head_dim)
    key_pre = proj[:, group_width : group_width + head_dim].reshape(pair, 1, head_dim)
    value_own = proj[:, group_width + head_dim :].astype(BF)

    def prepare(query_in, key_in, query_gain, key_gain):
        return (
            rotate(scaled_norm(query_in, query_gain), cosine, sine_part),
            rotate(scaled_norm(key_in, key_gain), cosine, sine_part),
        )

    (query_rot, key_rot), prepare_pull = jax.vjp(
        prepare, query_pre, key_pre, head_gains[0], head_gains[1]
    )
    query_low = query_rot.astype(BF)
    own_keys = jnp.concatenate([key_rot.astype(BF).reshape(pair, head_dim), value_own], axis=1)
    own_keys, query_low = mark(own_keys, query_low)
    keys_sent = Transfer(
        lax.ppermute(own_keys, line_axes, [(i, i + 1) for i in range(line - 1)])
    )
    waits(keys_sent, *out_gather.sent)
    out_gather.next()
    earlier = keys_sent.value
    all_keys = jnp.concatenate([earlier, own_keys], axis=0)
    key_all = all_keys[:, :head_dim]
    value_all = all_keys[:, head_dim:]
    key_index = jnp.concatenate([index - pair, index])
    offsets = index[:, None] - key_index[None, :]
    valid_keys = (offsets >= 0) & (offsets < WINDOW) & (offsets <= pos_pair[:, None])

    def masked_scores():
        raw = jnp.einsum("qgd,kd->gqk", query_low, key_all, preferred_element_type=F32)
        return jnp.where(valid_keys, raw * score_scale, -1e30)

    scores = masked_scores()
    row_max = jnp.max(scores, axis=-1, keepdims=True)
    exponents = jnp.exp(scores - row_max)
    row_total = jnp.sum(exponents, axis=-1, keepdims=True)
    log_total = row_max + jnp.log(row_total)
    probs_low = (exponents / row_total).astype(BF)
    mixed = jnp.einsum("gqk,kd->qgd", probs_low, value_all, preferred_element_type=F32)
    (mixed_low,) = mark(mixed.reshape(pair, group_width).astype(BF))
    waits(*out_gather.sent)
    (out_part,) = mark(jnp.concatenate(head_order(out_gather.blocks()), axis=1))
    (attn_sum,) = mark(dot_right_t(mixed_low, out_part))
    attn_sent = put(attn_sum[tokens:], "core")
    wait(attn_sent)
    attn_pre = attn_sum[:tokens] + attn_sent.value
    attn_out, attn_pull = jax.vjp(scaled_norm, attn_pre, model_gains[1])
    side_out, side_pull = jax.vjp(scaled_norm, side_pre, model_gains[2])
    first_sum = (hidden_f + attn_out + first_norm.astype(F32) + side_out) * SQRT_HALF
    normed_two, norm_two_pull = jax.vjp(scaled_norm, first_sum, model_gains[3])
    second_norm, first_sum = mark(normed_two.astype(BF), first_sum)

    team = reps
    staged = team == 4
    groups = [[0], [1, 2], [3]] if staged else [list(range(team))]

    def group_of(blocks, g):
        return jnp.concatenate([blocks[k] for k in groups[g]], axis=0)

    def by_block(results):
        parts = [None] * team
        for group, result in zip(groups, results):
            for i, k in enumerate(group):
                parts[k] = result[i * tokens : (i + 1) * tokens]
        return parts

    def step_blocks(gather, g):
        if not staged:
            return group_of(gather.blocks(), 0)
        if g == 0:
            return gather.value
        if g == 1:
            return jnp.concatenate(gather.near_blocks()[1:], axis=0)
        return gather.far_block()

    second_gather = Gather(second_norm, team_axes, order)
    second_groups, gate_ups, hidden_groups, norm_groups = [], [], [], []

    def gate_step(g):
        second_groups.append(step_blocks(second_gather, g))
        (block,) = go(second_groups[-1])
        gate_up = dot_plain(block, gate_up_cols)
        hidden = (gelu_tanh(gate_up[:, :units]) * gate_up[:, units:]).astype(BF)
        gate_up, hidden = mark(gate_up, hidden)
        gate_ups.append(gate_up)
        hidden_groups.append(hidden)

    def down_step(g):
        (block,) = go(hidden_groups[g])
        norm_groups.extend(mark(dot_right_t(block, down_cols).astype(BF)))

    waits(*second_gather.sent)
    second_gather.next()
    waits(*second_gather.sent)
    first_gather = Gather(go(first_norm)[0], rep_axes, order)
    waits(*first_gather.sent)
    first_gather.next()
    waits(*first_gather.sent)
    first_others = jnp.stack(first_gather.blocks()[1:])
    first_sent = put(first_others, "core")
    wait(first_sent)
    (first_all,) = mark(
        jnp.concatenate(
            [first_pair]
            + [block for pair_blocks in zip(first_others, first_sent.value) for block in pair_blocks],
            axis=0,
        )
    )
    for g in range(len(groups)):
        gate_step(g)
    for g in range(len(groups)):
        down_step(g)
    ffn_scatter = Scatter(by_block(norm_groups), team_axes, order)
    second_all = jnp.concatenate(second_groups, axis=0)
    hidden_all = jnp.concatenate(hidden_groups, axis=0)
    second_all, hidden_all = mark(*go(second_all, hidden_all))
    waits(*ffn_scatter.sent)
    ffn_scatter.next()
    ffn_terms = []
    for gate_up in go(*gate_ups):
        ffn_terms.append(gelu_terms(gate_up[:, :units], gate_up[:, units:]))
    mark(*[term for terms in ffn_terms for term in terms])
    waits(*ffn_scatter.sent)
    (ffn_pre,) = mark(ffn_scatter.total())
    ffn_out, ffn_pull = jax.vjp(scaled_norm, ffn_pre, model_gains[4])
    second_sum = first_sum + ffn_out
    second_low = second_sum.astype(BF)
    ple_pre = dot_plain(second_low, gate_layer_full)

    def gate_vectors(pre_values, vector_values):
        return gelu_tanh(pre_values) * vector_values

    gated_val, gated_pull = jax.vjp(gate_vectors, ple_pre, layer_vectors.astype(F32))
    gated_low = gated_val.astype(BF)
    last_pre = dot_right_t(gated_low, project_full)
    last_out, last_pull = jax.vjp(scaled_norm, last_pre, model_gains[5])
    layer_out = (second_sum + last_out).astype(BF)

    upstream = cotangent.astype(F32)
    d_last, grad_gain_five = last_pull(upstream)
    d_last_low = d_last.astype(BF)
    d_gated = dot_plain(d_last_low, project_full)
    d_ple_pre, grad_vectors = gated_pull(d_gated)
    d_ple_low = d_ple_pre.astype(BF)
    d_second = upstream + dot_right_t(d_ple_low, gate_layer_full)
    d_ffn, grad_gain_four = ffn_pull(d_second)
    (d_ffn_low,) = mark(d_ffn.astype(BF))
    ple_terms = jnp.concatenate(
        [dot_left_t(second_low, d_ple_low), dot_left_t(d_last_low, gated_low)], axis=1
    ).astype(BF)
    ple_rows = lax.psum_scatter(ple_terms, shard_axes, scatter_dimension=0, tiled=True)
    d_ffn_gather = Gather(d_ffn_low, team_axes, order)
    d_ffn_groups, d_gate_groups, d_norm_groups = [], [], []

    def back_step(g):
        d_ffn_groups.append(step_blocks(d_ffn_gather, g))
        (block,) = go(d_ffn_groups[-1])
        value, slope = ffn_terms[g]
        d_hidden = dot_plain(block, down_cols)
        d_gate = (d_hidden * slope.astype(F32)).astype(BF)
        d_up = (d_hidden * value.astype(F32)).astype(BF)
        d_gate_groups.append(jnp.concatenate([d_gate, d_up], axis=1))
        d_norm = dot_right_t(d_gate_groups[-1], gate_up_cols).astype(BF)
        d_norm_groups.extend(mark(d_norm))

    if staged:
        back_step(0)
        waits(*d_ffn_gather.sent)
        d_ffn_gather.next()
        back_step(1)
        waits(*d_ffn_gather.sent)
        back_step(2)
    else:
        back_step(0)
    norm_scatter = Scatter(by_block(d_norm_groups), team_axes, order)

    def keep(value, axis, dim):
        return pick(value, lax.axis_index(axis), dim)

    def send(value, axis, dim):
        return put(pick(value, 1 - lax.axis_index(axis), dim), axis)

    def far_send(value):
        return send(value, far_axes[0], 0) if len(far_axes) == 1 else None

    def far_halve(value, transfer):
        if len(far_axes) == 1:
            return combine(keep(value, far_axes[0], 0), transfer.value)
        for axis in far_axes:
            value = value.reshape((2, value.shape[0] // 2) + value.shape[1:])
            value = combine(
                keep(value, axis, 0), swap(pick(value, 1 - lax.axis_index(axis), 0), axis)
            )
        return value

    class FfnGradient:
        def __init__(self, term):
            self.mine = lax.psum_scatter(term, shard_axes, scatter_dimension=0, tiled=True)

        def spread(self):
            self.gather = Gather(go(self.mine[:, :units])[0], rep_axes, order)

        def columns(self):
            blocks = reorder(go(*self.gather.blocks()), rep_axes)
            (whole,) = mark(jnp.concatenate([block.astype(F32) for block in blocks], axis=1))
            return whole

    (d_ffn_all,) = mark(jnp.concatenate(go(*d_ffn_groups), axis=0))
    (down_terms,) = mark(dot_left_t(d_ffn_all, hidden_all).astype(BF))
    down_terms, ple_rows = lax.optimization_barrier((down_terms, ple_rows))
    down_grad = FfnGradient(down_terms)
    waits(*norm_scatter.sent)
    norm_scatter.next()
    (d_gate_all,) = mark(jnp.concatenate(go(*d_gate_groups), axis=0))
    (gate_terms,) = mark(dot_left_t(second_all, d_gate_all[:, :units]).astype(BF))
    gate_grad = FfnGradient(gate_terms)
    waits(*norm_scatter.sent)
    d_second_norm = norm_scatter.total()
    d_first_part, grad_gain_three = norm_two_pull(d_second_norm)
    d_branch = (d_second + d_first_part) * SQRT_HALF
    d_attn, grad_gain_one = attn_pull(d_branch)
    d_attn_low, d_branch = mark(d_attn.astype(BF), d_branch)
    d_attn_sent = put(d_attn_low, "core")
    d_side, grad_gain_two = side_pull(go(d_branch)[0])
    d_side_low = d_side.astype(BF)
    d_middle_low = dot_plain(d_side_low, up_low_full).astype(BF)
    laurel_terms = jnp.concatenate(
        [dot_left_t(first_norm, d_middle_low), dot_left_t(d_side_low, middle)], axis=1
    ).astype(BF)
    d_middle_low, laurel_terms = mark(d_middle_low, laurel_terms)
    wait(d_attn_sent)
    d_attn_pair = jnp.concatenate([d_attn_low, d_attn_sent.value], axis=0)
    (d_mixed_low,) = mark(dot_plain(d_attn_pair, out_part).astype(BF))
    d_mixed_low = d_mixed_low.reshape(pair, group, head_dim)
    (out_term,) = mark(dot_left_t(go(d_attn_pair)[0], mixed_low).astype(BF))

    def columns(value):
        return jnp.split(value, reps, axis=1)

    out_scatter = Scatter(head_order(columns(go(out_term)[0])), rep_axes, order)
    probabilities = jnp.exp(masked_scores() - log_total)
    (d_mixed_low,) = go(d_mixed_low)
    d_probs = jnp.einsum("qgd,kd->gqk", d_mixed_low, value_all, preferred_element_type=F32)
    row_dot = jnp.sum(probabilities * d_probs, axis=-1, keepdims=True)
    (d_scores,) = mark((probabilities * (d_probs - row_dot)).astype(BF))
    waits(*out_scatter.sent)
    out_scatter.next()
    (d_scores,) = go(d_scores)
    d_values = jnp.einsum("gqk,qgd->kd", probs_low, d_mixed_low, preferred_element_type=F32)
    d_keys = (
        jnp.einsum("gqk,qgd->kd", d_scores, query_low, preferred_element_type=F32) * score_scale
    )
    (key_grads,) = mark(jnp.concatenate([d_keys, d_values], axis=1))
    returned = Transfer(
        lax.ppermute(
            key_grads[:pair].astype(BF), line_axes, [(i + 1, i) for i in range(line - 1)]
        )
    )
    d_queries = (
        jnp.einsum("gqk,kd->qgd", go(d_scores)[0], key_all, preferred_element_type=F32)
        * score_scale
    )
    (d_queries,) = mark(d_queries)
    down_grad.spread()
    (up_terms,) = mark(dot_left_t(go(second_all)[0], d_gate_all[:, units:]).astype(BF))
    up_grad = FfnGradient(up_terms)
    waits(returned, *out_scatter.sent)
    own_grads = key_grads[pair:] + returned.value.astype(F32)
    d_query_pre, d_key_pre, grad_query_gain, grad_key_gain = prepare_pull(
        (d_queries, own_grads[:, :head_dim].reshape(pair, 1, head_dim))
    )
    d_proj = jnp.concatenate(
        [
            d_query_pre.reshape(pair, group_width),
            d_key_pre.reshape(pair, head_dim),
            own_grads[:, head_dim:],
        ],
        axis=1,
    ).astype(BF)
    (d_proj,) = mark(d_proj)

    def rep_put(value, k):
        return Transfer(lax.ppermute(value, rep_axes, [(i, i ^ k) for i in range(reps)]))

    proj_parts = [
        jnp.concatenate([one, two], axis=1)
        for one, two in zip(
            head_order(columns(d_proj[:, :group_width])),
            reorder(columns(d_proj[:, group_width:]), rep_axes),
        )
    ]
    proj_sent = [rep_put(proj_parts[k], k) for k in range(1, reps)]
    (out_total,) = mark(out_scatter.total().astype(BF))
    (norm_sum,) = mark(dot_right_t(go(d_proj)[0], qkv_part))
    norm_sent = put(norm_sum[tokens:], "core")
    waits(*proj_sent, *down_grad.gather.sent)
    proj_all = jnp.concatenate([proj_parts[0]] + [part.value for part in proj_sent], axis=0)
    (qkv_total,) = mark(dot_left_t(first_all, go(proj_all)[0]).astype(BF))

    def core_columns(value):
        return [jnp.where(core == c, value, jnp.zeros_like(value)) for c in range(cores)]

    (attention_terms,) = mark(
        jnp.concatenate(
            core_columns(qkv_total) + core_columns(out_total) + [laurel_terms], axis=1
        )
    )
    attention_sum = lax.psum_scatter(
        attention_terms, shard_axes, scatter_dimension=0, tiled=True
    )
    down_grad.gather.next()
    wait(norm_sent)
    d_first_norm = (
        norm_sum[:tokens]
        + norm_sent.value
        + dot_right_t(d_middle_low, down_low_full)
        + d_branch
    )
    d_input_part, grad_gain_zero = norm_one_pull(d_first_norm)
    grad_hidden, grad_gain_zero = mark(d_branch + d_input_part, grad_gain_zero)
    model_part = jnp.stack(
        [
            grad_gain_zero,
            grad_gain_one,
            grad_gain_two,
            grad_gain_three,
            grad_gain_four,
            grad_gain_five,
        ]
    )
    head_part = jnp.stack([grad_query_gain, grad_key_gain])
    gains = jnp.concatenate([model_part.reshape(-1, head_dim), head_part], axis=0)
    gain_axes = rep_axes + line_axes + ("core",)

    def gain_put(pair_axes):
        if len(pair_axes) == 1:
            return [put(gains, pair_axes[0])]
        across = lax.ppermute(gains, pair_axes, [(i, 3 - i) for i in range(4)])
        return [put(gains, pair_axes[0]), put(gains, pair_axes[1]), Transfer(across)]

    def gain_sum(transfers):
        values = [transfer.value for transfer in transfers]
        if len(values) == 1:
            return gains + values[0]
        return (gains + values[0]) + (values[1] + values[2])

    gain_steps = [gain_axes[i : i + 2] for i in range(0, len(gain_axes), 2)]
    gain_sent = gain_put(gain_steps[0])
    small_sum = go(ple_rows)[0]
    small_sent = put(small_sum, rep_axes[0])
    waits(small_sent, *down_grad.gather.sent, *gain_sent)
    gate_grad.spread()
    gains = gain_sum(gain_sent)
    gain_sent = gain_put(gain_steps[1])
    for axis in rep_axes[1:]:
        small_sum = combine(small_sum, small_sent.value)
        small_sent = put(small_sum, axis)
    grad_down = down_grad.columns()
    waits(small_sent, *gate_grad.gather.sent, *gain_sent)
    gate_grad.gather.next()
    ple_sum = small_sum.astype(F32) + small_sent.value.astype(F32)
    gains = gain_sum(gain_sent)
    for step in gain_steps[2:-1]:
        gain_sent = gain_put(step)
        waits(*gain_sent)
        gains = gain_sum(gain_sent)
    gain_sent = gain_put(gain_steps[-1])
    waits(*gain_sent, *gate_grad.gather.sent)
    gains = gain_sum(gain_sent)
    gate_columns = gate_grad.columns()
    up_grad.spread()
    waits(*up_grad.gather.sent)
    up_grad.gather.next()
    (attention_sum,) = go(attention_sum)
    waits(*up_grad.gather.sent)
    attention_width = cores * (part + query_part)
    (attention_sum,) = go(attention_sum)
    attention_gather = Gather(attention_sum[:, :attention_width], rep_axes, order)
    laurel_sum = attention_sum[:, attention_width:]
    laurel_sent = put(laurel_sum, rep_axes[0])
    up_columns = up_grad.columns()
    waits(laurel_sent, *attention_gather.sent)
    attention_gather.next()
    for axis in rep_axes[1:]:
        laurel_sum = combine(laurel_sum, laurel_sent.value)
        laurel_sent = put(laurel_sum, axis)
    grad_gate_up = jnp.concatenate([gate_columns, up_columns], axis=1)
    (grad_gate_up,) = mark(*go(grad_gate_up))
    waits(laurel_sent, *attention_gather.sent)
    attention_blocks = reorder(attention_gather.blocks(), rep_axes)
    grad_qkv = jnp.concatenate(
        [
            block[:, c * part : c * part + query_part].astype(F32)
            for c in range(cores)
            for block in attention_blocks
        ]
        + [
            block[:, c * part + query_part : (c + 1) * part].astype(F32)
            for half in (attention_blocks[: reps // 2], attention_blocks[reps // 2 :])
            for c in range(cores)
            for block in half
        ],
        axis=1,
    )
    grad_out = jnp.concatenate(
        [
            block[:, cores * part + c * query_part : cores * part + (c + 1) * query_part].astype(
                F32
            )
            for c in range(cores)
            for block in attention_blocks
        ],
        axis=1,
    )
    laurel_sum = laurel_sum.astype(F32) + laurel_sent.value.astype(F32)
    grad_laurel_down, grad_laurel_up = laurel_sum[:, :rank], laurel_sum[:, rank:]
    grad_layer_gate, grad_layer_project = ple_sum[:, :ple], ple_sum[:, ple:]
    grad_model_gains = gains[: -head_part.shape[0]].reshape(model_part.shape)
    grad_head_gains = gains[-head_part.shape[0] :]
    return (
        layer_out,
        grad_hidden,
        grad_vectors,
        grad_model_gains,
        grad_head_gains,
        grad_qkv,
        grad_out,
        grad_laurel_down,
        grad_laurel_up,
        grad_gate_up,
        grad_down,
        grad_layer_gate,
        grad_layer_project,
    )


def solution(mesh):
    reps, shards = mesh.shape["rep"], mesh.shape["shard"]
    rep_axes = tuple(f"rep{i}" for i in range(reps.bit_length() - 1))
    line_axes = tuple(f"line{i}" for i in range(shards.bit_length() - 2))
    axes = rep_axes + line_axes + ("core",)
    assert 1 << len(axes) == reps * shards
    fine = Mesh(np.asarray(mesh.devices).reshape((2,) * len(axes)), axes)
    rows, owned = P(axes, None), P(line_axes + ("core",), None)
    return jax.shard_map(
        functools.partial(body, rep_axes, line_axes),
        mesh=fine,
        in_specs=(rows, rows, P(axes), rows, P(), P()) + (owned,) * 8,
        out_specs=(rows, rows, rows, P(), P()) + (owned,) * 8,
        check_vma=False,
    )
```

time: 1290 us -> 953 us (0.74)
  starting transfers between devices: 266 us -> 79.6 us
  waiting for transfers between devices: 525 us -> 375 us
  matrix products: 179 us -> 236 us
  local copies, waits for them, and re-layouts: 151 us -> 112 us
  other arithmetic: 158 us -> 123 us
    ppermute x61 -> x7, waiting for transfers between devices: 321 us -> 41.8 us  [the longest x1 24.7 us: body(): lax.ppermute(key_grads[:pair].astype(BF), line_axes, [(i + 1, i) for i in...]
    ppermute x61 -> x7, starting transfers between devices: 163 us -> 21.5 us  [the longest x2 14.4 us: gain_put(): across = lax.ppermute(gains, pair_axes, [(i, 3 - i) for i in range(4)])]
    all_gather x0 -> x2, waiting for transfers between devices: none -> 75.8 us  [the longest x1 71.4 us: body(): lax.all_gather(attention_rows, shard_axes, axis=0, tiled=True)]
    ppermute x109 -> x63, waiting for transfers between devices: 203 us -> 257 us  [swap(): return lax.ppermute(value, axis, [(0, 1), (1, 0)])]
    ppermute x109 -> x63, starting transfers between devices: 103 us -> 57.1 us  [swap(): return lax.ppermute(value, axis, [(0, 1), (1, 0)])]
    dot_general x8 -> x12, matrix products: 54.1 us -> 90.5 us  [dot_right_t(): lax.dot_general(left_side, right_side, (((1,), (1,)), ((), ())), preferre...]
    dynamic_update_slice x37 -> x0, other arithmetic: 29.8 us -> none  [the longest x12 20.9 us: lay_out(): out = lax.dynamic_update_slice(out, block.astype(F32), (0, start))]
    convert_element_type x27 -> x13, other arithmetic: 44 us -> 20.2 us  [the longest x3 9.35 us: gelu_terms(): return (value.astype(BF), (slope * up).astype(BF))]
  transfers between devices with their start and end apart: 170 -> 77, of which waited for: 59 -> 44; matrix products, arithmetic and copies ran while one was open for 25% -> 37% of each run, Pallas kernels for 0% -> 0%
where the time goes in v2:
time: 953 us; the launch traced here: 943 us
  waiting for transfers between devices  375 us (39%)
  matrix products  236 us (25%)
  other arithmetic  123 us (13%)
  local copies, waits for them, and re-layouts  112 us (12%)
  starting transfers between devices  79.6 us (8%)
  between operations  16.9 us (2%)
    ppermute x63, waiting for transfers between devices, swap(): return lax.ppermute(value, axis, [(0, 1), (1, 0)])  257 us
    dot_general x12, matrix products, dot_right_t(): lax.dot_general(left_side, right_side, (((1,), (1,)), ((), ())), preferre...  90.5 us
    all_gather x1, waiting for transfers between devices, body(): lax.all_gather(attention_rows, shard_axes, axis=0, tiled=True)  71.4 us
    dot_general x12, matrix products, dot_plain(): return jnp.dot(left_side, right_side, preferred_element_type=jnp.float32)  68 us
    ppermute x63, starting transfers between devices, swap(): return lax.ppermute(value, axis, [(0, 1), (1, 0)])  57.1 us
    dot_general x9, matrix products, dot_left_t(): lax.dot_general(left_side, right_side, (((0,), (0,)), ((), ())), preferre...  54.7 us
    unnamed x326, local copies, waits for them, and re-layouts  52.8 us
    ppermute x1, waiting for transfers between devices, body(): lax.ppermute(key_grads[:pair].astype(BF), line_axes, [(i + 1, i) for i in...  24.7 us
  transfers between devices with their start and end apart: 77, of which 44 were waited for; matrix products, arithmetic and copies ran while one was open for 37% of the time, Pallas kernels for 0%

profile of v2, /device:TPU:0, one launch (start us, length us, event | category | flops | bytes accessed | tf_op | source)
XLA Modules:
  0.0 943.0 jit_solution(7752862374563156551)
XLA Ops:
  22.3 71.4 %all-gather.3.cloned.1.call-done = bf16[2048,1920]{1,0:T(8,128)(2,1)} async-done(((bf16[256,1920]{1,0:T(8,128)(2,1)}), bf16[2048,1920]{1,0:T(8,128)(2,1)}) %all-gather.3.cloned.1.call-update) | async-done | bytes 7864336 | tf_op jit(solution)/shard_map/all_gather | solution.py:283
  111.1 24.3 %collective-permute-done.3 = bf16[2048,384]{1,0:T(8,128)(2,1)S(1)} collective-permute-done((bf16[2048,384]{1,0:T(8,128)(2,1)S(1)}, bf16[2048,384]{1,0:T(8,128)(2,1)S(1)}, u32[]{:S(2)}, u32[]{:S(2)}) %collective-permute-start.3) | collective-permute-done | bytes 1572896 | tf_op jit(solution)/shard_map/ppermute | solution.py:81
  139.1 16.5 %collective-permute-done.5 = bf16[1024,384]{1,0:T(8,128)(2,1)S(1)} collective-permute-done((bf16[1024,384]{1,0:T(8,128)(2,1)S(1)}, bf16[1024,384]{1,0:T(8,128)(2,1)S(1)}, u32[]{:S(2)}, u32[]{:S(2)}) %collective-permute-start.5) | collective-permute-done | bytes 786464 | tf_op jit(solution)/shard_map/ppermute | solution.py:81
  180.4 13.1 %collective-permute-done.6 = bf16[512,512]{1,0:T(8,128)(2,1)} collective-permute-done((bf16[512,512]{1,0:T(8,128)(2,1)}, bf16[512,512]{1,0:T(8,128)(2,1)}, u32[]{:S(2)}, u32[]{:S(2)}) %collective-permute-start.6) | collective-permute-done | bytes 524320 | tf_op jit(solution)/shard_map/ppermute | solution.py:363
  207.2 14.9 %fusion.176 = f32[512,2048]{1,0:T(8,128)S(1)} fusion(bf16[512,1024]{0,1:T(8,128)(2,1)S(1)} %bitcast.194, bf16[1024,256]{1,0:T(8,128)(2,1)S(1)} %collective-permute-done.9, bf16[1024,256]{1,0:T(8,128)(2,1)S(1)} %collective-permute-done.10, bf16[2048,256]{1,0:T(8,128)(2,1)} %collective-permute-done.7, bf16[2048,256]{1,0:T(8,128)(2,1)} %collective-permute-done.8, ...), kind=kOutput, calls=%fused_computation.478 | convolution fusion | flops 2168455168 | bytes 9437184 | tf_op jit(solution)/shard_map/dot_general | solution.py:51
  232.7 22.3 %collective-permute-done.13 = bf16[256,2048]{1,0:T(8,128)(2,1)S(1)} collective-permute-done((bf16[256,2048]{1,0:T(8,128)(2,1)S(1)}, bf16[256,2048]{1,0:T(8,128)(2,1)S(1)}, u32[]{:S(2)}, u32[]{:S(2)}) %collective-permute-start.13) | collective-permute-done | bytes 1048608 | tf_op jit(solution)/shard_map/ppermute | solution.py:81
  258.5 10.7 %collective-permute-done.15 = bf16[128,2048]{1,0:T(8,128)(2,1)S(1)} collective-permute-done((bf16[128,2048]{1,0:T(8,128)(2,1)S(1)}, bf16[128,2048]{1,0:T(8,128)(2,1)S(1)}, u32[]{:S(2)}, u32[]{:S(2)}) %collective-permute-start.15) | collective-permute-done | bytes 524320 | tf_op jit(solution)/shard_map/ppermute | solution.py:81
  272.4 20.2 %collective-permute-done.17 = bf16[256,2048]{1,0:T(8,128)(2,1)S(1)} collective-permute-done((bf16[256,2048]{1,0:T(8,128)(2,1)S(1)}, bf16[256,2048]{1,0:T(8,128)(2,1)S(1)}, u32[]{:S(2)}, u32[]{:S(2)}) %collective-permute-start.17) | collective-permute-done | bytes 1048608 | tf_op jit(solution)/shard_map/ppermute | solution.py:81
  333.8 11.7 %fusion.12 = f32[512,4096]{1,0:T(8,128)S(1)} fusion(bf16[512,2048]{1,0:T(8,128)(2,1)S(1)} %copy-done.38, bf16[2048,6144]{1,0:T(8,128)(2,1)} %all-gather.5.cloned.1.call-done), kind=kOutput, calls=%fused_computation.22 | convolution fusion | flops 8589934592 | bytes 27262976 | tf_op jit(solution)/shard_map/dot_general | solution.py:47
  405.2 14.6 %collective-permute-done.23 = bf16[256,2048]{1,0:T(8,128)(2,1)S(1)} collective-permute-done((bf16[256,2048]{1,0:T(8,128)(2,1)S(1)}, bf16[256,2048]{1,0:T(8,128)(2,1)S(1)}, u32[]{:S(2)}, u32[]{:S(2)}) %collective-permute-start.23) | collective-permute-done | bytes 1048608 | tf_op jit(solution)/shard_map/ppermute | solution.py:81
  444.6 11.0 %fusion.54 = bf16[256,2048]{1,0:T(8,128)(2,1)S(1)} fusion(bf16[2048,6144]{1,0:T(8,128)(2,1)} %all-gather.5.cloned.1.call-done, bf16[256,2048]{1,0:T(8,128)(2,1)} %get-tuple-element.407, bf16[256,2048]{1,0:T(8,128)(2,1)} %get-tuple-element.406), kind=kOutput, calls=%fused_computation.103 | convolution fusion | flops 4299685888 | bytes 19922944 | tf_op jit(solution)/shard_map/dot_general | solution.py:51
  474.4 15.2 %fusion.48 = bf16[512,2048]{1,0:T(8,128)(2,1)} fusion(bf16[2048,6144]{1,0:T(8,128)(2,1)} %all-gather.5.cloned.1.call-done, bf16[512,2048]{1,0:T(8,128)(2,1)S(1)} %get-tuple-element.383, bf16[512,2048]{1,0:T(8,128)(2,1)S(1)} %get-tuple-element.382), kind=kOutput, calls=%fused_computation.95 | convolution fusion | flops 8599371776 | bytes 23068672 | tf_op jit(solution)/shard_map/dot_general | solution.py:51
  499.6 12.0 %fusion.57 = bf16[256,2048]{1,0:T(8,128)(2,1)} fusion(bf16[2048,6144]{1,0:T(8,128)(2,1)} %all-gather.5.cloned.1.call-done, bf16[256,2048]{1,0:T(8,128)(2,1)} %get-tuple-element.405, bf16[256,2048]{1,0:T(8,128)(2,1)} %get-tuple-element.404), kind=kOutput, calls=%fused_computation.104 | convolution fusion | flops 4299685888 | bytes 19922944 | tf_op jit(solution)/shard_map/dot_general | solution.py:51
  511.6 14.0 %convolution_convert_fusion.2 = bf16[2048,2048]{1,0:T(8,128)(2,1)} fusion(bf16[1024,2048]{1,0:T(8,128)(2,1)} %pad_maximum_fusion.1, bf16[256,2048]{1,0:T(8,128)(2,1)} %copy-done.81, bf16[512,2048]{1,0:T(8,128)(2,1)} %copy-done.68, bf16[256,2048]{1,0:T(8,128)(2,1)} %fusion.91), kind=kOutput, calls=%fused_computation.12 | convolution fusion | flops 8606711808 | bytes 16777216 | tf_op jit(solution)/shard_map/dot_general | solution.py:57
  544.0 11.4 %convolution_convert_fusion.1 = bf16[2048,2048]{1,0:T(8,128)(2,1)} fusion(bf16[1024,2048]{1,0:T(8,128)(2,1)S(1)} %copy-done.78, bf16[1024,4096]{1,0:T(8,128)(2,1)S(1)} %constant_dynamic-update-slice_fusion.17), kind=kOutput, calls=%fused_computation.11 | convolution fusion | flops 8594128896 | bytes 16777216 | tf_op jit(solution)/shard_map/dot_general | solution.py:57
  562.1 17.2 %collective-permute-done.31 = bf16[256,2048]{1,0:T(8,128)(2,1)S(1)} collective-permute-done((bf16[256,2048]{1,0:T(8,128)(2,1)S(1)}, bf16[256,2048]{1,0:T(8,128)(2,1)S(1)}, u32[]{:S(2)}, u32[]{:S(2)}) %collective-permute-start.31) | collective-permute-done | bytes 1048608 | tf_op jit(solution)/shard_map/ppermute | solution.py:81
  610.8 10.3 %fusion.2 = bf16[4,512,1024]{1,2,0:T(8,128)(2,1)} fusion(f32[1024,512,4]{1,0,2:T(8,128)} %copy-done.4, f32[4,512]{1,0:T(4,128)S(1)} %log_add_fusion, pred[512,1024]{0,1:T(8,128)(4,1)S(1)} %copy-done.23, bf16[512,4,256]{0,2,1:T(8,128)(2,1)} %copy.157, bf16[1024,512]{1,0:T(8,128)(2,1)S(1)} %copy-done.51), kind=kOutput, calls=%fused_computation.5 | convolution fusion | flops 2168458240 | bytes 25182208 | tf_op jit(solution)/shard_map/sub | solution.py:591
  627.5 13.7 %convolution_convert_fusion = bf16[2048,2048]{1,0:T(8,128)(2,1)} fusion(bf16[1024,2048]{1,0:T(8,128)(2,1)S(1)} %copy-done.79, bf16[1024,4096]{1,0:T(8,128)(2,1)} %copy-done.67), kind=kOutput, calls=%fused_computation.10 | convolution fusion | flops 8594128896 | bytes 16777216 | tf_op jit(solution)/shard_map/dot_general | solution.py:57
  659.0 24.7 %collective-permute-done.36 = bf16[512,512]{1,0:T(8,128)(2,1)} collective-permute-done((bf16[512,512]{1,0:T(8,128)(2,1)}, bf16[512,512]{1,0:T(8,128)(2,1)}, u32[]{:S(2)}, u32[]{:S(2)}) %collective-permute-start.36) | collective-permute-done | bytes 524320 | tf_op jit(solution)/shard_map/ppermute | solution.py:601
  732.7 18.5 %collective-permute-done.44 = bf16[256,2048]{1,0:T(8,128)(2,1)} collective-permute-done((bf16[256,2048]{1,0:T(8,128)(2,1)}, bf16[256,2048]{1,0:T(8,128)(2,1)}, u32[]{:S(2)}, u32[]{:S(2)}) %collective-permute-start.44) | collective-permute-done | bytes 1048608 | tf_op jit(solution)/shard_map/ppermute | solution.py:81
  792.4 13.1 %collective-permute-start.56 = (f32[50,256]{1,0:T(8,128)S(1)}, f32[50,256]{1,0:T(8,128)S(1)}, u32[]{:S(2)}, u32[]{:S(2)}) collective-permute-start(f32[50,256]{1,0:T(8,128)S(1)} %add_add_fusion.9), channel_id=1, source_target_pairs={{0,6},{2,4},{4,2},{6,0},{1,7},{3,5},{5,3},{7,1},{8,14},{10,12},{12... | collective-permute-start | bytes 153608 | tf_op jit(solution)/shard_map/ppermute | solution.py:684
  815.5 19.6 %collective-permute-done.51 = bf16[256,512]{0,1:T(8,128)(2,1)S(1)} collective-permute-done((bf16[256,512]{0,1:T(8,128)(2,1)S(1)}, bf16[256,512]{0,1:T(8,128)(2,1)S(1)}, u32[]{:S(2)}, u32[]{:S(2)}) %collective-permute-start.51) | collective-permute-done | bytes 262176 | tf_op jit(solution)/shard_map/ppermute | solution.py:81
  854.8 18.7 %collective-permute-done.61 = bf16[256,2048]{1,0:T(8,128)(2,1)S(1)} collective-permute-done((bf16[256,2048]{1,0:T(8,128)(2,1)}, bf16[256,2048]{1,0:T(8,128)(2,1)S(1)}, u32[]{:S(2)}, u32[]{:S(2)}) %collective-permute-start.61) | collective-permute-done | bytes 1048608 | tf_op jit(solution)/shard_map/ppermute | solution.py:81
  899.5 9.4 collective-permute-done.64
  (698 shorter events, 497.6 us)
Async XLA Ops:
  7.2 86.5 %all-gather.3.cloned.1.call-start = ((), (), s32[]{:S(2)}) async-start(), calls=%async_computation.5 | async-start | bytes 8847360 | tf_op jit(solution)/shard_map/all_gather | solution.py:283
  13.1 308.5 %all-gather.5.cloned.1.call-start = ((), (), s32[]{:S(2)}) async-start(), calls=%async_computation.6 | async-start | bytes 28311552 | tf_op jit(solution)/shard_map/all_gather | solution.py:316
  97.6 428.0 %reduce-scatter.6.cloned.1.call-start = ((), (), s32[]{:S(2)}) async-start(), calls=%async_computation.7 | async-start | bytes 2359296 | tf_op jit(solution)/shard_map/reduce_scatter | solution.py:497
  98.8 36.5 %collective-permute-start.3 = (bf16[2048,384]{1,0:T(8,128)(2,1)S(1)}, bf16[2048,384]{1,0:T(8,128)(2,1)S(1)}, u32[]{:S(2)}, u32[]{:S(2)}) collective-permute-start(bf16[2048,384]{1,0:T(8,128)(2,1)S(1)} %constant_dynamic-slice_fusion.1), channel_id=1, source_target_pairs={{0,8},{8,0},{1,9},{9,1},{2,10},{10,2},{3,11},{11,3},{4,12},{12,4},... | collective-permute-start | bytes 4718600 | tf_op jit(solution)/shard_map/ppermute | solution.py:81
  100.4 36.3 %collective-permute-start.2 = (bf16[2048,384]{1,0:T(8,128)(2,1)S(1)}, bf16[2048,384]{1,0:T(8,128)(2,1)S(1)}, u32[]{:S(2)}, u32[]{:S(2)}) collective-permute-start(bf16[2048,384]{1,0:T(8,128)(2,1)S(1)} %constant_dynamic-slice_fusion.1), channel_id=1, source_target_pairs={{0,16},{16,0},{1,17},{17,1},{2,18},{18,2},{3,19},{19,3},{4,20},{20... | collective-permute-start | bytes 4718600 | tf_op jit(solution)/shard_map/ppermute | solution.py:81
  155.8 37.6 %collective-permute-start.8 = (bf16[2048,256]{1,0:T(8,128)(2,1)}, bf16[2048,256]{1,0:T(8,128)(2,1)}, u32[]{:S(2)}, u32[]{:S(2)}) collective-permute-start(bf16[2048,256]{1,0:T(8,128)(2,1)} %constant_dynamic-slice_fusion), channel_id=1, source_target_pairs={{0,8},{8,0},{1,9},{9,1},{2,10},{10,2},{3,11},{11,3},{4,12},{12,4},... | collective-permute-start | bytes 3145736 | tf_op jit(solution)/shard_map/ppermute | solution.py:81
  157.3 36.2 %collective-permute-start.7 = (bf16[2048,256]{1,0:T(8,128)(2,1)}, bf16[2048,256]{1,0:T(8,128)(2,1)}, u32[]{:S(2)}, u32[]{:S(2)}) collective-permute-start(bf16[2048,256]{1,0:T(8,128)(2,1)} %constant_dynamic-slice_fusion), channel_id=1, source_target_pairs={{0,16},{16,0},{1,17},{17,1},{2,18},{18,2},{3,19},{19,3},{4,20},{20... | collective-permute-start | bytes 3145736 | tf_op jit(solution)/shard_map/ppermute | solution.py:81
  229.8 25.2 %collective-permute-start.13 = (bf16[256,2048]{1,0:T(8,128)(2,1)S(1)}, bf16[256,2048]{1,0:T(8,128)(2,1)S(1)}, u32[]{:S(2)}, u32[]{:S(2)}) collective-permute-start(bf16[256,2048]{1,0:T(8,128)(2,1)S(1)} %get-tuple-element.166), channel_id=1, source_target_pairs={{0,8},{8,0},{1,9},{9,1},{2,10},{10,2},{3,11},{11,3},{4,12},{12,4},... | collective-permute-start | bytes 3145736 | tf_op jit(solution)/shard_map/ppermute | solution.py:81
  231.2 24.9 %collective-permute-start.12 = (bf16[256,2048]{1,0:T(8,128)(2,1)S(1)}, bf16[256,2048]{1,0:T(8,128)(2,1)S(1)}, u32[]{:S(2)}, u32[]{:S(2)}) collective-permute-start(bf16[256,2048]{1,0:T(8,128)(2,1)S(1)} %get-tuple-element.166), channel_id=1, source_target_pairs={{0,16},{16,0},{1,17},{17,1},{2,18},{18,2},{3,19},{19,3},{4,20},{20... | collective-permute-start | bytes 3145736 | tf_op jit(solution)/shard_map/ppermute | solution.py:81
  436.5 278.7 %reduce-scatter.8.cloned.1.call-start = ((), (), s32[]{:S(2)}) async-start(), calls=%async_computation.8 | async-start | bytes 9437184 | tf_op jit(solution)/shard_map/reduce_scatter | solution.py:544
  461.6 28.0 %collective-permute-start.28 = (bf16[128,2048]{1,0:T(8,128)(2,1)}, bf16[128,2048]{1,0:T(8,128)(2,1)}, u32[]{:S(2)}, u32[]{:S(2)}) collective-permute-start(bf16[128,2048]{1,0:T(8,128)(2,1)} %slice.475), channel_id=1, source_target_pairs={{0,8},{8,0},{1,9},{9,1},{2,10},{10,2},{3,11},{11,3},{4,12},{12,4},... | collective-permute-start | bytes 1572872 | tf_op jit(solution)/shard_map/ppermute | solution.py:81
  463.0 26.7 %collective-permute-start.27 = (bf16[128,2048]{1,0:T(8,128)(2,1)S(1)}, bf16[128,2048]{1,0:T(8,128)(2,1)}, u32[]{:S(2)}, u32[]{:S(2)}) collective-permute-start(bf16[128,2048]{1,0:T(8,128)(2,1)S(1)} %slice.474), channel_id=1, source_target_pairs={{0,16},{16,0},{1,17},{17,1},{2,18},{18,2},{3,19},{19,3},{4,20},{20... | collective-permute-start | bytes 1572872 | tf_op jit(solution)/shard_map/ppermute | solution.py:81
  525.6 280.5 %reduce-scatter.10.cloned.1.call-start = ((), (), s32[]{:S(2)}) async-start(), calls=%async_computation.9 | async-start | bytes 9437184 | tf_op jit(solution)/shard_map/reduce_scatter | solution.py:544
  555.4 298.1 %reduce-scatter.14.cloned.1.call-start = ((), (), s32[]{:S(2)}) async-start(), calls=%async_computation.11 | async-start | bytes 9437184 | tf_op jit(solution)/shard_map/reduce_scatter | solution.py:544
  641.2 250.6 %reduce-scatter.12.cloned.1.call-start = ((), (), s32[]{:S(2)}) async-start(), calls=%async_computation.10 | async-start | bytes 6488064 | tf_op jit(solution)/shard_map/reduce_scatter | solution.py:654
  647.7 36.1 %collective-permute-start.36 = (bf16[512,512]{1,0:T(8,128)(2,1)}, bf16[512,512]{1,0:T(8,128)(2,1)}, u32[]{:S(2)}, u32[]{:S(2)}) collective-permute-start(bf16[512,512]{1,0:T(8,128)(2,1)} %fusion.114), channel_id=1, source_target_pairs={{2,0},{4,2},{6,4},{3,1},{5,3},{7,5},{10,8},{12,10},{14,12},{11,9},... | collective-permute-start | bytes 1572872 | tf_op jit(solution)/shard_map/ppermute | solution.py:601
  651.9 31.8 %collective-permute-start.37 = (bf16[2048,256]{1,0:T(8,128)(2,1)}, bf16[2048,256]{1,0:T(8,128)(2,1)}, u32[]{:S(2)}, u32[]{:S(2)}) collective-permute-start(bf16[2048,256]{1,0:T(8,128)(2,1)} %pad_maximum_fusion.20), channel_id=1, source_target_pairs={{0,16},{16,0},{1,17},{17,1},{2,18},{18,2},{3,19},{19,3},{4,20},{20... | collective-permute-start | bytes 3145736 | tf_op jit(solution)/shard_map/ppermute | solution.py:81
  653.7 30.0 %collective-permute-start.38 = (bf16[2048,256]{1,0:T(8,128)(2,1)}, bf16[2048,256]{1,0:T(8,128)(2,1)}, u32[]{:S(2)}, u32[]{:S(2)}) collective-permute-start(bf16[2048,256]{1,0:T(8,128)(2,1)} %pad_maximum_fusion.21), channel_id=1, source_target_pairs={{0,8},{8,0},{1,9},{9,1},{2,10},{10,2},{3,11},{11,3},{4,12},{12,4},... | collective-permute-start | bytes 3145736 | tf_op jit(solution)/shard_map/ppermute | solution.py:81
  715.2 36.0 %collective-permute-start.44 = (bf16[256,2048]{1,0:T(8,128)(2,1)}, bf16[256,2048]{1,0:T(8,128)(2,1)}, u32[]{:S(2)}, u32[]{:S(2)}) collective-permute-start(bf16[256,2048]{1,0:T(8,128)(2,1)} %reduce-scatter.8.cloned.1.call-done), channel_id=1, source_target_pairs={{0,8},{8,0},{1,9},{9,1},{2,10},{10,2},{3,11},{11,3},{4,12},{12,4},... | collective-permute-start | bytes 3145736 | tf_op jit(solution)/shard_map/ppermute | solution.py:81
  716.2 36.2 %collective-permute-start.43 = (bf16[256,2048]{1,0:T(8,128)(2,1)}, bf16[256,2048]{1,0:T(8,128)(2,1)}, u32[]{:S(2)}, u32[]{:S(2)}) collective-permute-start(bf16[256,2048]{1,0:T(8,128)(2,1)} %reduce-scatter.8.cloned.1.call-done), channel_id=1, source_target_pairs={{0,16},{16,0},{1,17},{17,1},{2,18},{18,2},{3,19},{19,3},{4,20},{20... | collective-permute-start | bytes 3145736 | tf_op jit(solution)/shard_map/ppermute | solution.py:81
  731.7 42.6 %collective-permute-start.39 = (f32[256,2048]{1,0:T(8,128)}, f32[256,2048]{1,0:T(8,128)}, u32[]{:S(2)}, u32[]{:S(2)}) collective-permute-start(f32[256,2048]{1,0:T(8,128)} %slice.578), channel_id=1, source_target_pairs={{0,1},{1,0},{2,3},{3,2},{4,5},{5,4},{6,7},{7,6},{8,9},{9,8},{10,11... | collective-permute-start | bytes 6291464 | tf_op jit(solution)/shard_map/ppermute | solution.py:81
  806.1 29.0 %collective-permute-start.53 = (bf16[256,2048]{1,0:T(8,128)(2,1)}, bf16[256,2048]{1,0:T(8,128)(2,1)S(1)}, u32[]{:S(2)}, u32[]{:S(2)}) collective-permute-start(bf16[256,2048]{1,0:T(8,128)(2,1)} %reduce-scatter.10.cloned.1.call-done), channel_id=1, source_target_pairs={{0,8},{8,0},{1,9},{9,1},{2,10},{10,2},{3,11},{11,3},{4,12},{12,4},... | collective-permute-start | bytes 3145736 | tf_op jit(solution)/shard_map/ppermute | solution.py:81
  807.2 27.9 %collective-permute-start.52 = (bf16[256,2048]{1,0:T(8,128)(2,1)}, bf16[256,2048]{1,0:T(8,128)(2,1)S(1)}, u32[]{:S(2)}, u32[]{:S(2)}) collective-permute-start(bf16[256,2048]{1,0:T(8,128)(2,1)} %reduce-scatter.10.cloned.1.call-done), channel_id=1, source_target_pairs={{0,16},{16,0},{1,17},{17,1},{2,18},{18,2},{3,19},{19,3},{4,20},{20... | collective-permute-start | bytes 3145736 | tf_op jit(solution)/shard_map/ppermute | solution.py:81
  810.5 24.6 %collective-permute-start.51 = (bf16[256,512]{0,1:T(8,128)(2,1)S(1)}, bf16[256,512]{0,1:T(8,128)(2,1)S(1)}, u32[]{:S(2)}, u32[]{:S(2)}) collective-permute-start(bf16[256,512]{0,1:T(8,128)(2,1)S(1)} %add_convert_fusion.9), channel_id=1, source_target_pairs={{0,8},{8,0},{1,9},{9,1},{2,10},{10,2},{3,11},{11,3},{4,12},{12,4},... | collective-permute-start | bytes 786440 | tf_op jit(solution)/shard_map/ppermute | solution.py:81
  (195 other events, 2208.5 us)
Sparse Core Ops, SparseCore 0:
  13.2 80.4 all-gather.2
  97.7 223.7 all-gather.4
  436.6 49.6 reduce-scatter.5
  525.7 104.0 reduce-scatter.7
  632.0 99.1 reduce-scatter.9
  733.4 91.4 reduce-scatter.13
  827.2 63.5 reduce-scatter.11

commit v3 on v2

--- a/solution.py
+++ b/solution.py
@@ -5,6 +5,8 @@
 import jax.numpy as jnp
 import numpy as np
 from jax import lax
+from jax.experimental import pallas as pl
+from jax.experimental.pallas import tpu as pltpu
 from jax.sharding import Mesh
 from jax.sharding import PartitionSpec as P
 
@@ -57,6 +59,27 @@
     return lax.dot_general(
         left_side, right_side, (((0,), (0,)), ((), ())), preferred_element_type=jnp.float32
     )
+
+
+def terms_kernel(left_ref, right_ref, out_ref):
+    out_ref[...] = dot_left_t(left_ref[...], right_ref[...]).astype(out_ref.dtype)
+
+
+def gradient_terms(left_side, right_side, size, block):
+    rows, columns = left_side.shape
+    step = math.gcd(columns, 512)
+    return pl.pallas_call(
+        terms_kernel,
+        grid=(columns // step,),
+        in_specs=[
+            pl.BlockSpec((rows, step), lambda i: (0, i)),
+            pl.BlockSpec((rows, size), lambda i: (0, block)),
+        ],
+        out_specs=pl.BlockSpec((step, size), lambda i: (i, 0)),
+        out_shape=jax.ShapeDtypeStruct((columns, size), BF),
+        cost_estimate=pl.CostEstimate(flops=1, bytes_accessed=1, transcendentals=0),
+        compiler_params=pltpu.CompilerParams(vmem_limit_bytes=40 * 1024 * 1024),
+    )(left_side, right_side)
 
 
 def gelu_tanh(values):
@@ -274,10 +297,17 @@
             out_weight, c * group_width + rep * query_part, query_part, 1
         )
 
+    ple = layer_gate.shape[1]
+    ple_part = ple // reps
     attention_rows = jnp.concatenate(
         [qkv_columns(c) for c in range(cores)]
         + [out_columns(c) for c in range(cores)]
-        + [laurel_down, laurel_up, layer_gate, layer_project],
+        + [
+            laurel_down,
+            laurel_up,
+            lax.dynamic_slice_in_dim(layer_gate, rep * ple_part, ple_part, 1),
+            lax.dynamic_slice_in_dim(layer_project, rep * ple_part, ple_part, 1),
+        ],
         axis=1,
     )
     attention_whole = lax.all_gather(attention_rows, shard_axes, axis=0, tiled=True)
@@ -317,12 +347,10 @@
     gate_up_cols = ffn_whole[:, : 2 * units]
     down_cols = ffn_whole[:, 2 * units :]
     qkv_gather = Gather(qkv_own, rep_axes, order)
-    ple = layer_gate.shape[1]
     small_full = go(attention_whole)[0][:, cores * (part + query_part) :]
     down_low_full = small_full[:, :rank]
     up_low_full = small_full[:, rank : 2 * rank]
-    gate_layer_full = small_full[:, 2 * rank : 2 * rank + ple]
-    project_full = small_full[:, 2 * rank + ple :]
+    ple_own = small_full[:, 2 * rank :]
     middle = dot_plain(first_norm, down_low_full).astype(BF)
     side_pre, middle = mark(dot_right_t(middle, up_low_full), middle)
     waits(*qkv_gather.sent)
@@ -420,28 +448,20 @@
         return gather.far_block()
 
     second_gather = Gather(second_norm, team_axes, order)
-    second_groups, gate_ups, hidden_groups, norm_groups = [], [], [], []
-
-    def gate_step(g):
-        second_groups.append(step_blocks(second_gather, g))
-        (block,) = go(second_groups[-1])
-        gate_up = dot_plain(block, gate_up_cols)
-        hidden = (gelu_tanh(gate_up[:, :units]) * gate_up[:, units:]).astype(BF)
-        gate_up, hidden = mark(gate_up, hidden)
-        gate_ups.append(gate_up)
-        hidden_groups.append(hidden)
-
-    def down_step(g):
-        (block,) = go(hidden_groups[g])
-        norm_groups.extend(mark(dot_right_t(block, down_cols).astype(BF)))
-
     waits(*second_gather.sent)
     second_gather.next()
     waits(*second_gather.sent)
     first_gather = Gather(go(first_norm)[0], rep_axes, order)
-    waits(*first_gather.sent)
+    ple_gather = Gather(go(ple_own)[0], rep_axes, order)
+    waits(*first_gather.sent, *ple_gather.sent)
     first_gather.next()
-    waits(*first_gather.sent)
+    ple_gather.next()
+    waits(*first_gather.sent, *ple_gather.sent)
+    ple_blocks = reorder(ple_gather.blocks(), rep_axes)
+    gate_layer_full, project_full = mark(
+        jnp.concatenate([block[:, :ple_part] for block in ple_blocks], axis=1),
+        jnp.concatenate([block[:, ple_part:] for block in ple_blocks], axis=1),
+    )
     first_others = jnp.stack(first_gather.blocks()[1:])
     first_sent = put(first_others, "core")
     wait(first_sent)
@@ -452,20 +472,18 @@
             axis=0,
         )
     )
-    for g in range(len(groups)):
-        gate_step(g)
-    for g in range(len(groups)):
-        down_step(g)
-    ffn_scatter = Scatter(by_block(norm_groups), team_axes, order)
-    second_all = jnp.concatenate(second_groups, axis=0)
-    hidden_all = jnp.concatenate(hidden_groups, axis=0)
-    second_all, hidden_all = mark(*go(second_all, hidden_all))
+    (second_all,) = mark(jnp.concatenate(go(*second_gather.blocks()), axis=0))
+    gate_up = dot_plain(second_all, gate_up_cols)
+    hidden_all = (gelu_tanh(gate_up[:, :units]) * gate_up[:, units:]).astype(BF)
+    gate_up, hidden_all = mark(gate_up, hidden_all)
+    (norm_all,) = mark(dot_right_t(hidden_all, down_cols).astype(BF))
+    ffn_scatter = Scatter(
+        [norm_all[k * tokens : (k + 1) * tokens] for k in range(team)], team_axes, order
+    )
     waits(*ffn_scatter.sent)
     ffn_scatter.next()
-    ffn_terms = []
-    for gate_up in go(*gate_ups):
-        ffn_terms.append(gelu_terms(gate_up[:, :units], gate_up[:, units:]))
-    mark(*[term for terms in ffn_terms for term in terms])
+    (gate_up,) = go(gate_up)
+    ffn_value, ffn_slope = mark(*gelu_terms(gate_up[:, :units], gate_up[:, units:]))
     waits(*ffn_scatter.sent)
     (ffn_pre,) = mark(ffn_scatter.total())
     ffn_out, ffn_pull = jax.vjp(scaled_norm, ffn_pre, model_gains[4])
@@ -501,7 +519,9 @@
     def back_step(g):
         d_ffn_groups.append(step_blocks(d_ffn_gather, g))
         (block,) = go(d_ffn_groups[-1])
-        value, slope = ffn_terms[g]
+        at = sum(len(group) for group in groups[:g]) * tokens
+        rows = slice(at, at + len(groups[g]) * tokens)
+        value, slope = ffn_value[rows], ffn_slope[rows]
         d_hidden = dot_plain(block, down_cols)
         d_gate = (d_hidden * slope.astype(F32)).astype(BF)
         d_up = (d_hidden * value.astype(F32)).astype(BF)
@@ -510,14 +530,14 @@
         d_norm_groups.extend(mark(d_norm))
 
     if staged:
+        waits(*d_ffn_gather.sent)
+        d_ffn_gather.next()
         back_step(0)
         waits(*d_ffn_gather.sent)
-        d_ffn_gather.next()
-        back_step(1)
-        waits(*d_ffn_gather.sent)
-        back_step(2)
-    else:
-        back_step(0)
+    (d_ffn_all,) = mark(jnp.concatenate(go(*d_ffn_gather.blocks()), axis=0))
+    (down_terms,) = mark(gradient_terms(d_ffn_all, hidden_all, units, 0))
+    for g in range(1 if staged else 0, len(groups)):
+        back_step(g)
     norm_scatter = Scatter(by_block(d_norm_groups), team_axes, order)
 
     def keep(value, axis, dim):
@@ -544,22 +564,27 @@
             self.mine = lax.psum_scatter(term, shard_axes, scatter_dimension=0, tiled=True)
 
         def spread(self):
-            self.gather = Gather(go(self.mine[:, :units])[0], rep_axes, order)
-
-        def columns(self):
-            blocks = reorder(go(*self.gather.blocks()), rep_axes)
-            (whole,) = mark(jnp.concatenate([block.astype(F32) for block in blocks], axis=1))
-            return whole
-
-    (d_ffn_all,) = mark(jnp.concatenate(go(*d_ffn_groups), axis=0))
-    (down_terms,) = mark(dot_left_t(d_ffn_all, hidden_all).astype(BF))
+            self.gather = Gather(go(self.mine)[0], rep_axes, order)
+
+        def place(self, whole, blocks, first, start=0):
+            for k, block in enumerate(go(*blocks), first):
+                whole = lax.dynamic_update_slice(
+                    whole, block.astype(F32), (0, start + rep_of(k) * units)
+                )
+            return mark(whole)[0]
+
+    def rep_of(k):
+        return rep ^ k
+
     down_terms, ple_rows = lax.optimization_barrier((down_terms, ple_rows))
     down_grad = FfnGradient(down_terms)
     waits(*norm_scatter.sent)
     norm_scatter.next()
     (d_gate_all,) = mark(jnp.concatenate(go(*d_gate_groups), axis=0))
-    (gate_terms,) = mark(dot_left_t(second_all, d_gate_all[:, :units]).astype(BF))
+    (gate_terms,) = mark(gradient_terms(second_all, d_gate_all, units, 0))
     gate_grad = FfnGradient(gate_terms)
+    (up_terms,) = mark(gradient_terms(go(second_all)[0], d_gate_all, units, 1))
+    up_grad = FfnGradient(up_terms)
     waits(*norm_scatter.sent)
     d_second_norm = norm_scatter.total()
     d_first_part, grad_gain_three = norm_two_pull(d_second_norm)
@@ -589,8 +614,13 @@
     d_probs = jnp.einsum("qgd,kd->gqk", d_mixed_low, value_all, preferred_element_type=F32)
     row_dot = jnp.sum(probabilities * d_probs, axis=-1, keepdims=True)
     (d_scores,) = mark((probabilities * (d_probs - row_dot)).astype(BF))
-    waits(*out_scatter.sent)
+    small_sum = go(ple_rows)[0]
+    small_sent = put(small_sum, rep_axes[0])
+    waits(small_sent, *out_scatter.sent)
     out_scatter.next()
+    for axis in rep_axes[1:]:
+        small_sum = combine(small_sum, small_sent.value)
+        small_sent = put(small_sum, axis)
     (d_scores,) = go(d_scores)
     d_values = jnp.einsum("gqk,qgd->kd", probs_low, d_mixed_low, preferred_element_type=F32)
     d_keys = (
@@ -608,9 +638,8 @@
     )
     (d_queries,) = mark(d_queries)
     down_grad.spread()
-    (up_terms,) = mark(dot_left_t(go(second_all)[0], d_gate_all[:, units:]).astype(BF))
-    up_grad = FfnGradient(up_terms)
-    waits(returned, *out_scatter.sent)
+    waits(returned, small_sent, *out_scatter.sent, *down_grad.gather.sent)
+    ple_sum = small_sum.astype(F32) + small_sent.value.astype(F32)
     own_grads = key_grads[pair:] + returned.value.astype(F32)
     d_query_pre, d_key_pre, grad_query_gain, grad_key_gain = prepare_pull(
         (d_queries, own_grads[:, :head_dim].reshape(pair, 1, head_dim))
@@ -636,9 +665,8 @@
         )
     ]
     proj_sent = [rep_put(proj_parts[k], k) for k in range(1, reps)]
+    down_grad.gather.next()
     (out_total,) = mark(out_scatter.total().astype(BF))
-    (norm_sum,) = mark(dot_right_t(go(d_proj)[0], qkv_part))
-    norm_sent = put(norm_sum[tokens:], "core")
     waits(*proj_sent, *down_grad.gather.sent)
     proj_all = jnp.concatenate([proj_parts[0]] + [part.value for part in proj_sent], axis=0)
     (qkv_total,) = mark(dot_left_t(first_all, go(proj_all)[0]).astype(BF))
@@ -654,7 +682,9 @@
     attention_sum = lax.psum_scatter(
         attention_terms, shard_axes, scatter_dimension=0, tiled=True
     )
-    down_grad.gather.next()
+    gate_grad.spread()
+    (norm_sum,) = mark(dot_right_t(go(d_proj)[0], qkv_part))
+    norm_sent = put(norm_sum[tokens:], "core")
     wait(norm_sent)
     d_first_norm = (
         norm_sum[:tokens]
@@ -692,46 +722,43 @@
 
     gain_steps = [gain_axes[i : i + 2] for i in range(0, len(gain_axes), 2)]
     gain_sent = gain_put(gain_steps[0])
-    small_sum = go(ple_rows)[0]
-    small_sent = put(small_sum, rep_axes[0])
-    waits(small_sent, *down_grad.gather.sent, *gain_sent)
-    gate_grad.spread()
+    grad_down = jnp.zeros((weight_rows, ffn_units), F32)
+    grad_down = down_grad.place(grad_down, down_grad.gather.blocks(), 0)
+    waits(*gain_sent, *gate_grad.gather.sent)
+    gate_grad.gather.next()
     gains = gain_sum(gain_sent)
     gain_sent = gain_put(gain_steps[1])
-    for axis in rep_axes[1:]:
-        small_sum = combine(small_sum, small_sent.value)
-        small_sent = put(small_sum, axis)
-    grad_down = down_grad.columns()
-    waits(small_sent, *gate_grad.gather.sent, *gain_sent)
-    gate_grad.gather.next()
-    ple_sum = small_sum.astype(F32) + small_sent.value.astype(F32)
+    waits(*gain_sent, *gate_grad.gather.sent)
+    up_grad.spread()
     gains = gain_sum(gain_sent)
     for step in gain_steps[2:-1]:
         gain_sent = gain_put(step)
         waits(*gain_sent)
         gains = gain_sum(gain_sent)
     gain_sent = gain_put(gain_steps[-1])
-    waits(*gain_sent, *gate_grad.gather.sent)
+    grad_gate_up = jnp.zeros((weight_rows, 2 * ffn_units), F32)
+    grad_gate_up = gate_grad.place(grad_gate_up, gate_grad.gather.blocks(), 0)
+    waits(*gain_sent, *up_grad.gather.sent)
+    up_grad.gather.next()
     gains = gain_sum(gain_sent)
-    gate_columns = gate_grad.columns()
-    up_grad.spread()
+    if staged:
+        grad_gate_up = up_grad.place(grad_gate_up, up_grad.gather.near_blocks(), 0, ffn_units)
     waits(*up_grad.gather.sent)
-    up_grad.gather.next()
+    if staged:
+        far_block = [up_grad.gather.far_block()]
+        grad_gate_up = up_grad.place(grad_gate_up, far_block, 3, ffn_units)
+    else:
+        grad_gate_up = up_grad.place(grad_gate_up, up_grad.gather.blocks(), 0, ffn_units)
     (attention_sum,) = go(attention_sum)
-    waits(*up_grad.gather.sent)
     attention_width = cores * (part + query_part)
-    (attention_sum,) = go(attention_sum)
     attention_gather = Gather(attention_sum[:, :attention_width], rep_axes, order)
     laurel_sum = attention_sum[:, attention_width:]
     laurel_sent = put(laurel_sum, rep_axes[0])
-    up_columns = up_grad.columns()
     waits(laurel_sent, *attention_gather.sent)
     attention_gather.next()
     for axis in rep_axes[1:]:
         laurel_sum = combine(laurel_sum, laurel_sent.value)
         laurel_sent = put(laurel_sum, axis)
-    grad_gate_up = jnp.concatenate([gate_columns, up_columns], axis=1)
-    (grad_gate_up,) = mark(*go(grad_gate_up))
     waits(laurel_sent, *attention_gather.sent)
     attention_blocks = reorder(attention_gather.blocks(), rep_axes)
     grad_qkv = jnp.concatenate(

time: 953 us -> 913 us (0.958)
  waiting for transfers between devices: 375 us -> 320 us
  matrix products: 236 us -> 183 us
  Pallas kernels: 0 us -> 35.4 us
  starting transfers between devices: 79.6 us -> 93.3 us
  other arithmetic: 123 us -> 135 us
    dot_general x9 -> x6, matrix products: 54.7 us -> 15.4 us  [dot_left_t(): lax.dot_general(left_side, right_side, (((0,), (0,)), ((), ())), preferre...]
    pallas_call x0 -> x3, Pallas kernels: none -> 35.4 us  [gradient_terms(): pl.pallas_call(terms_kernel, grid=(columns // step,), in_specs=[pl.BlockS...]
    ppermute x63 -> x67, waiting for transfers between devices: 257 us -> 225 us  [swap(): return lax.ppermute(value, axis, [(0, 1), (1, 0)])]
    ppermute x63 -> x67, starting transfers between devices: 57.1 us -> 81.9 us  [swap(): return lax.ppermute(value, axis, [(0, 1), (1, 0)])]
    dynamic_update_slice x0 -> x12, other arithmetic: none -> 23.7 us  [place(): lax.dynamic_update_slice(whole, block.astype(F32), (0, start + rep_of(k)...]
    unnamed x15 -> x6, other arithmetic: 20.4 us -> 5.12 us
    all_gather x1, waiting for transfers between devices: 71.4 us -> 58.4 us  [body(): lax.all_gather(attention_rows, shard_axes, axis=0, tiled=True)]
    broadcast_in_dim x0 -> x2, local copies, waits for them, and re-layouts: none -> 12.5 us  [the longest x1 8.12 us: body(): grad_gate_up = jnp.zeros((weight_rows, 2 * ffn_units), F32)]
  transfers between devices with their start and end apart: 77 -> 81, of which waited for: 44 -> 37; matrix products, arithmetic and copies ran while one was open for 37% -> 38% of each run, Pallas kernels for 0% -> 4%
where the time goes in v3:
time: 913 us; the launch traced here: 903 us
  waiting for transfers between devices  320 us (35%)
  matrix products  183 us (20%)
  other arithmetic  135 us (15%)
  local copies, waits for them, and re-layouts  119 us (13%)
  starting transfers between devices  93.3 us (10%)
  Pallas kernels  35.4 us (4%)
  between operations  16.8 us (2%)
    ppermute x67, waiting for transfers between devices, swap(): return lax.ppermute(value, axis, [(0, 1), (1, 0)])  225 us
    dot_general x10, matrix products, dot_right_t(): lax.dot_general(left_side, right_side, (((1,), (1,)), ((), ())), preferre...  82.3 us
    ppermute x67, starting transfers between devices, swap(): return lax.ppermute(value, axis, [(0, 1), (1, 0)])  81.9 us
    dot_general x10, matrix products, dot_plain(): return jnp.dot(left_side, right_side, preferred_element_type=jnp.float32)  62.1 us
    all_gather x1, waiting for transfers between devices, body(): lax.all_gather(attention_rows, shard_axes, axis=0, tiled=True)  58.4 us
    unnamed x324, local copies, waits for them, and re-layouts  46.1 us
    pallas_call x3, Pallas kernels, gradient_terms(): pl.pallas_call(terms_kernel, grid=(columns // step,), in_specs=[pl.BlockS...  35.4 us
    dynamic_update_slice x12, other arithmetic, place(): lax.dynamic_update_slice(whole, block.astype(F32), (0, start + rep_of(k)...  23.7 us
  transfers between devices with their start and end apart: 81, of which 37 were waited for; matrix products, arithmetic and copies ran while one was open for 38% of the time, Pallas kernels for 4%

profile of v3, /device:TPU:0, one launch (start us, length us, event | category | flops | bytes accessed | tf_op | source)
XLA Modules:
  0.0 903.3 jit_solution(7412244534785659065)
XLA Ops:
  22.4 58.4 %all-gather.3.cloned.1.call-done = bf16[2048,1536]{1,0:T(8,128)(2,1)} async-done(((bf16[256,1536]{1,0:T(8,128)(2,1)}), bf16[2048,1536]{1,0:T(8,128)(2,1)}) %all-gather.3.cloned.1.call-update) | async-done | bytes 6291472 | tf_op jit(solution)/shard_map/all_gather | solution.py:313
  98.2 24.4 %collective-permute-done.2 = bf16[2048,384]{1,0:T(8,128)(2,1)S(1)} collective-permute-done((bf16[2048,384]{1,0:T(8,128)(2,1)S(1)}, bf16[2048,384]{1,0:T(8,128)(2,1)S(1)}, u32[]{:S(2)}, u32[]{:S(2)}) %collective-permute-start.2) | collective-permute-done | bytes 1572896 | tf_op jit(solution)/shard_map/ppermute | solution.py:104
  126.2 16.3 %collective-permute-done.4 = bf16[1024,384]{1,0:T(8,128)(2,1)S(1)} collective-permute-done((bf16[1024,384]{1,0:T(8,128)(2,1)S(1)}, bf16[1024,384]{1,0:T(8,128)(2,1)S(1)}, u32[]{:S(2)}, u32[]{:S(2)}) %collective-permute-start.4) | collective-permute-done | bytes 786464 | tf_op jit(solution)/shard_map/ppermute | solution.py:104
  167.8 12.8 %collective-permute-done.6 = bf16[512,512]{1,0:T(8,128)(2,1)} collective-permute-done((bf16[512,512]{1,0:T(8,128)(2,1)}, bf16[512,512]{1,0:T(8,128)(2,1)}, u32[]{:S(2)}, u32[]{:S(2)}) %collective-permute-start.6) | collective-permute-done | bytes 524320 | tf_op jit(solution)/shard_map/ppermute | solution.py:391
  194.3 15.1 %fusion.131 = f32[512,2048]{1,0:T(8,128)S(1)} fusion(bf16[512,1024]{0,1:T(8,128)(2,1)S(1)} %bitcast.189, bf16[1024,256]{1,0:T(8,128)(2,1)S(1)} %collective-permute-done.9, bf16[1024,256]{1,0:T(8,128)(2,1)S(1)} %collective-permute-done.10, bf16[2048,256]{1,0:T(8,128)(2,1)} %collective-permute-done.7, bf16[2048,256]{1,0:T(8,128)(2,1)} %collective-permute-done.8, ...), kind=kOutput, calls=%fused_computation.415 | convolution fusion | flops 2168455168 | bytes 9437184 | tf_op jit(solution)/shard_map/dot_general | solution.py:53
  219.7 22.3 %collective-permute-done.12 = bf16[256,2048]{1,0:T(8,128)(2,1)S(1)} collective-permute-done((bf16[256,2048]{1,0:T(8,128)(2,1)S(1)}, bf16[256,2048]{1,0:T(8,128)(2,1)S(1)}, u32[]{:S(2)}, u32[]{:S(2)}) %collective-permute-start.12) | collective-permute-done | bytes 1048608 | tf_op jit(solution)/shard_map/ppermute | solution.py:104
  262.0 29.0 %collective-permute-done.18 = bf16[2048,128]{1,0:T(8,128)(2,1)S(1)} collective-permute-done((bf16[2048,128]{1,0:T(8,128)(2,1)S(1)}, bf16[2048,128]{1,0:T(8,128)(2,1)S(1)}, u32[]{:S(2)}, u32[]{:S(2)}) %collective-permute-start.18) | collective-permute-done | bytes 524320 | tf_op jit(solution)/shard_map/ppermute | solution.py:104
  297.8 10.8 %collective-permute-done.22 = bf16[1024,128]{1,0:T(8,128)(2,1)S(1)} collective-permute-done((bf16[1024,128]{1,0:T(8,128)(2,1)S(1)}, bf16[1024,128]{1,0:T(8,128)(2,1)S(1)}, u32[]{:S(2)}, u32[]{:S(2)}) %collective-permute-start.22) | collective-permute-done | bytes 262176 | tf_op jit(solution)/shard_map/ppermute | solution.py:104
  325.5 21.5 %fusion.7 = f32[1024,4096]{1,0:T(8,128)S(1)} fusion(bf16[1024,2048]{1,0:T(8,128)(2,1)} %constant_dynamic-update-slice_fusion.10.left_ref, bf16[2048,6144]{1,0:T(8,128)(2,1)} %all-gather.5.cloned.1.call-done), kind=kOutput, calls=%fused_computation.8 | convolution fusion | flops 17179869184 | bytes 37748736 | tf_op jit(solution)/shard_map/dot_general | solution.py:49
  349.9 14.1 %fusion.33 = bf16[1024,2048]{1,0:T(8,128)(2,1)} fusion(bf16[1024,2048]{1,0:T(8,128)(2,1)S(1)} %fusion.17.right_ref, bf16[2048,6144]{1,0:T(8,128)(2,1)} %all-gather.5.cloned.1.call-done), kind=kOutput, calls=%fused_computation.60 | convolution fusion | flops 8592031744 | bytes 16777216 | tf_op jit(solution)/shard_map/dot_general | solution.py:53
  368.8 11.1 %collective-permute-done.25 = bf16[128,2048]{1,0:T(8,128)(2,1)S(1)} collective-permute-done((bf16[128,2048]{1,0:T(8,128)(2,1)S(1)}, bf16[128,2048]{1,0:T(8,128)(2,1)S(1)}, u32[]{:S(2)}, u32[]{:S(2)}) %collective-permute-start.25) | collective-permute-done | bytes 524320 | tf_op jit(solution)/shard_map/ppermute | solution.py:104
  391.1 14.5 %collective-permute-done.28 = bf16[256,2048]{1,0:T(8,128)(2,1)S(1)} collective-permute-done((bf16[256,2048]{1,0:T(8,128)(2,1)S(1)}, bf16[256,2048]{1,0:T(8,128)(2,1)S(1)}, u32[]{:S(2)}, u32[]{:S(2)}) %collective-permute-start.28) | collective-permute-done | bytes 1048608 | tf_op jit(solution)/shard_map/ppermute | solution.py:104
  423.1 19.8 %collective-permute-done.29 = bf16[256,2048]{1,0:T(8,128)(2,1)S(1)} collective-permute-done((bf16[256,2048]{1,0:T(8,128)(2,1)}, bf16[256,2048]{1,0:T(8,128)(2,1)S(1)}, u32[]{:S(2)}, u32[]{:S(2)}) %collective-permute-start.29) | collective-permute-done | bytes 1048608 | tf_op jit(solution)/shard_map/ppermute | solution.py:104
  456.3 12.1 %fusion.39 = bf16[256,2048]{1,0:T(8,128)(2,1)} fusion(bf16[2048,6144]{1,0:T(8,128)(2,1)} %all-gather.5.cloned.1.call-done, bf16[256,2048]{1,0:T(8,128)(2,1)} %get-tuple-element.391, bf16[256,2048]{1,0:T(8,128)(2,1)} %get-tuple-element.390), kind=kOutput, calls=%fused_computation.81 | convolution fusion | flops 4299685888 | bytes 19922944 | tf_op jit(solution)/shard_map/dot_general | solution.py:53
  473.8 11.2 %shard_map.237 = bf16[2048,2048]{1,0:T(8,128)(2,1)} custom-call(bf16[1024,2048]{1,0:T(8,128)(2,1)S(1)} %pad_maximum_fusion.left_ref, bf16[1024,2048]{1,0:T(8,128)(2,1)S(1)} %copy-done.3), custom_call_target="tpu_custom_call" | custom-call | flops 1 | bytes 1 | tf_op jit(solution)/shard_map/pallas_call | solution.py:71
  500.1 15.0 %fusion.36 = bf16[512,2048]{1,0:T(8,128)(2,1)} fusion(bf16[2048,6144]{1,0:T(8,128)(2,1)} %all-gather.5.cloned.1.call-done, bf16[512,2048]{1,0:T(8,128)(2,1)} %get-tuple-element.365, bf16[512,2048]{1,0:T(8,128)(2,1)} %get-tuple-element.364), kind=kOutput, calls=%fused_computation.74 | convolution fusion | flops 8599371776 | bytes 23068672 | tf_op jit(solution)/shard_map/dot_general | solution.py:53
  522.8 11.1 %fusion.42 = bf16[256,2048]{1,0:T(8,128)(2,1)S(1)} fusion(bf16[2048,6144]{1,0:T(8,128)(2,1)} %all-gather.5.cloned.1.call-done, bf16[256,2048]{1,0:T(8,128)(2,1)} %get-tuple-element.389, bf16[256,2048]{1,0:T(8,128)(2,1)} %get-tuple-element.388), kind=kOutput, calls=%fused_computation.82 | convolution fusion | flops 4299685888 | bytes 19922944 | tf_op jit(solution)/shard_map/dot_general | solution.py:53
  548.6 12.1 %shard_map.238 = bf16[2048,2048]{1,0:T(8,128)(2,1)S(1)} custom-call(bf16[1024,2048]{1,0:T(8,128)(2,1)} %constant_dynamic-update-slice_fusion.10.left_ref, bf16[1024,4096]{1,0:T(8,128)(2,1)} %copy-done.6), custom_call_target="tpu_custom_call" | custom-call | flops 1 | bytes 1 | tf_op jit(solution)/shard_map/pallas_call | solution.py:71
  571.5 12.1 %shard_map.239 = bf16[2048,2048]{1,0:T(8,128)(2,1)S(1)} custom-call(bf16[1024,2048]{1,0:T(8,128)(2,1)} %constant_dynamic-update-slice_fusion.10.left_ref, bf16[1024,4096]{1,0:T(8,128)(2,1)} %copy-done.6), custom_call_target="tpu_custom_call" | custom-call | flops 1 | bytes 1 | tf_op jit(solution)/shard_map/pallas_call | solution.py:71
  623.6 11.7 %fusion.19 = bf16[4,512,1024]{1,2,0:T(8,128)(2,1)} fusion(f32[1024,512,4]{1,0,2:T(8,128)} %copy-done.9, f32[4,512]{1,0:T(4,128)S(1)} %log_add_fusion, pred[512,1024]{0,1:T(8,128)(4,1)S(1)} %copy-done.27, bf16[512,4,256]{0,2,1:T(8,128)(2,1)} %copy.157, bf16[1024,512]{1,0:T(8,128)(2,1)} %copy-done.57), kind=kOutput, calls=%fused_computation.22 | convolution fusion | flops 2168458240 | bytes 25182208 | tf_op jit(solution)/shard_map/sub | solution.py:616
  661.6 15.5 %collective-permute-done.42 = bf16[256,512]{0,1:T(8,128)(2,1)} collective-permute-done((bf16[256,512]{0,1:T(8,128)(2,1)S(1)}, bf16[256,512]{0,1:T(8,128)(2,1)}, u32[]{:S(2)}, u32[]{:S(2)}) %collective-permute-start.42) | collective-permute-done | bytes 262176 | tf_op jit(solution)/shard_map/ppermute | solution.py:104
  682.8 22.3 %collective-permute-done.41 = bf16[512,512]{1,0:T(8,128)(2,1)} collective-permute-done((bf16[512,512]{1,0:T(8,128)(2,1)}, bf16[512,512]{1,0:T(8,128)(2,1)}, u32[]{:S(2)}, u32[]{:S(2)}) %collective-permute-start.41) | collective-permute-done | bytes 524320 | tf_op jit(solution)/shard_map/ppermute | solution.py:631
  800.4 16.4 %collective-permute-start.58 = (f32[50,256]{1,0:T(8,128)S(1)}, f32[50,256]{1,0:T(8,128)S(1)}, u32[]{:S(2)}, u32[]{:S(2)}) collective-permute-start(f32[50,256]{1,0:T(8,128)S(1)} %add_add_fusion.9), channel_id=1, source_target_pairs={{0,4},{4,0},{1,5},{5,1},{2,6},{6,2},{3,7},{7,3},{8,12},{12,8},{9,1... | collective-permute-start | bytes 153608 | tf_op jit(solution)/shard_map/ppermute | solution.py:104
  869.1 10.8 %collective-permute-done.68 = bf16[256,128]{0,1:T(8,128)(2,1)S(1)} collective-permute-done((bf16[256,128]{0,1:T(8,128)(2,1)S(1)}, bf16[256,128]{0,1:T(8,128)(2,1)S(1)}, u32[]{:S(2)}, u32[]{:S(2)}) %collective-permute-start.68) | collective-permute-done | bytes 65568 | tf_op jit(solution)/shard_map/ppermute | solution.py:104
  (709 shorter events, 466.0 us)
Async XLA Ops:
  7.2 73.7 %all-gather.3.cloned.1.call-start = ((), (), s32[]{:S(2)}) async-start(), calls=%async_computation.5 | async-start | bytes 7077888 | tf_op jit(solution)/shard_map/all_gather | solution.py:313
  13.2 312.2 %all-gather.5.cloned.1.call-start = ((), (), s32[]{:S(2)}) async-start(), calls=%async_computation.6 | async-start | bytes 28311552 | tf_op jit(solution)/shard_map/all_gather | solution.py:346
  84.8 400.2 %reduce-scatter.6.cloned.1.call-start = ((), (), s32[]{:S(2)}) async-start(), calls=%async_computation.7 | async-start | bytes 2359296 | tf_op jit(solution)/shard_map/reduce_scatter | solution.py:515
  86.0 36.5 %collective-permute-start.2 = (bf16[2048,384]{1,0:T(8,128)(2,1)S(1)}, bf16[2048,384]{1,0:T(8,128)(2,1)S(1)}, u32[]{:S(2)}, u32[]{:S(2)}) collective-permute-start(bf16[2048,384]{1,0:T(8,128)(2,1)S(1)} %constant_dynamic-slice_fusion.1), channel_id=1, source_target_pairs={{0,16},{16,0},{1,17},{17,1},{2,18},{18,2},{3,19},{19,3},{4,20},{20... | collective-permute-start | bytes 4718600 | tf_op jit(solution)/shard_map/ppermute | solution.py:104
  87.5 36.3 %collective-permute-start.3 = (bf16[2048,384]{1,0:T(8,128)(2,1)S(1)}, bf16[2048,384]{1,0:T(8,128)(2,1)S(1)}, u32[]{:S(2)}, u32[]{:S(2)}) collective-permute-start(bf16[2048,384]{1,0:T(8,128)(2,1)S(1)} %constant_dynamic-slice_fusion.1), channel_id=1, source_target_pairs={{0,8},{8,0},{1,9},{9,1},{2,10},{10,2},{3,11},{11,3},{4,12},{12,4},... | collective-permute-start | bytes 4718600 | tf_op jit(solution)/shard_map/ppermute | solution.py:104
  143.0 37.6 %collective-permute-start.7 = (bf16[2048,256]{1,0:T(8,128)(2,1)}, bf16[2048,256]{1,0:T(8,128)(2,1)}, u32[]{:S(2)}, u32[]{:S(2)}) collective-permute-start(bf16[2048,256]{1,0:T(8,128)(2,1)} %constant_dynamic-slice_fusion), channel_id=1, source_target_pairs={{0,16},{16,0},{1,17},{17,1},{2,18},{18,2},{3,19},{19,3},{4,20},{20... | collective-permute-start | bytes 3145736 | tf_op jit(solution)/shard_map/ppermute | solution.py:104
  144.4 36.2 %collective-permute-start.8 = (bf16[2048,256]{1,0:T(8,128)(2,1)}, bf16[2048,256]{1,0:T(8,128)(2,1)}, u32[]{:S(2)}, u32[]{:S(2)}) collective-permute-start(bf16[2048,256]{1,0:T(8,128)(2,1)} %constant_dynamic-slice_fusion), channel_id=1, source_target_pairs={{0,8},{8,0},{1,9},{9,1},{2,10},{10,2},{3,11},{11,3},{4,12},{12,4},... | collective-permute-start | bytes 3145736 | tf_op jit(solution)/shard_map/ppermute | solution.py:104
  256.7 35.4 %collective-permute-start.16 = (bf16[256,2048]{1,0:T(8,128)(2,1)S(1)}, bf16[256,2048]{1,0:T(8,128)(2,1)S(1)}, u32[]{:S(2)}, u32[]{:S(2)}) collective-permute-start(bf16[256,2048]{1,0:T(8,128)(2,1)S(1)} %slice.561), channel_id=1, source_target_pairs={{0,16},{16,0},{1,17},{17,1},{2,18},{18,2},{3,19},{19,3},{4,20},{20... | collective-permute-start | bytes 3145736 | tf_op jit(solution)/shard_map/ppermute | solution.py:104
  258.1 34.0 %collective-permute-start.17 = (bf16[256,2048]{1,0:T(8,128)(2,1)S(1)}, bf16[256,2048]{1,0:T(8,128)(2,1)S(1)}, u32[]{:S(2)}, u32[]{:S(2)}) collective-permute-start(bf16[256,2048]{1,0:T(8,128)(2,1)S(1)} %slice.561), channel_id=1, source_target_pairs={{0,8},{8,0},{1,9},{9,1},{2,10},{10,2},{3,11},{11,3},{4,12},{12,4},... | collective-permute-start | bytes 3145736 | tf_op jit(solution)/shard_map/ppermute | solution.py:104
  260.6 30.4 %collective-permute-start.18 = (bf16[2048,128]{1,0:T(8,128)(2,1)S(1)}, bf16[2048,128]{1,0:T(8,128)(2,1)S(1)}, u32[]{:S(2)}, u32[]{:S(2)}) collective-permute-start(bf16[2048,128]{1,0:T(8,128)(2,1)S(1)} %slice.467), channel_id=1, source_target_pairs={{0,16},{16,0},{1,17},{17,1},{2,18},{18,2},{3,19},{19,3},{4,20},{20... | collective-permute-start | bytes 1572872 | tf_op jit(solution)/shard_map/ppermute | solution.py:104
  261.3 30.8 %collective-permute-start.19 = (bf16[2048,128]{1,0:T(8,128)(2,1)S(1)}, bf16[2048,128]{1,0:T(8,128)(2,1)S(1)}, u32[]{:S(2)}, u32[]{:S(2)}) collective-permute-start(bf16[2048,128]{1,0:T(8,128)(2,1)S(1)} %slice.467), channel_id=1, source_target_pairs={{0,8},{8,0},{1,9},{9,1},{2,10},{10,2},{3,11},{11,3},{4,12},{12,4},... | collective-permute-start | bytes 1572872 | tf_op jit(solution)/shard_map/ppermute | solution.py:104
  422.6 232.2 %reduce-scatter.8.cloned.1.call-start = ((), (), s32[]{:S(2)}) async-start(), calls=%async_computation.8 | async-start | bytes 9437184 | tf_op jit(solution)/shard_map/reduce_scatter | solution.py:564
  485.0 281.0 %reduce-scatter.10.cloned.1.call-start = ((), (), s32[]{:S(2)}) async-start(), calls=%async_computation.9 | async-start | bytes 9437184 | tf_op jit(solution)/shard_map/reduce_scatter | solution.py:564
  564.0 261.2 %reduce-scatter.12.cloned.1.call-start = ((), (), s32[]{:S(2)}) async-start(), calls=%async_computation.10 | async-start | bytes 9437184 | tf_op jit(solution)/shard_map/reduce_scatter | solution.py:564
  587.0 275.4 %reduce-scatter.14.cloned.1.call-start = ((), (), s32[]{:S(2)}) async-start(), calls=%async_computation.11 | async-start | bytes 6488064 | tf_op jit(solution)/shard_map/reduce_scatter | solution.py:682
  645.2 60.0 %collective-permute-start.44 = (bf16[2048,256]{1,0:T(8,128)(2,1)}, bf16[2048,256]{1,0:T(8,128)(2,1)}, u32[]{:S(2)}, u32[]{:S(2)}) collective-permute-start(bf16[2048,256]{1,0:T(8,128)(2,1)} %pad_maximum_fusion.22), channel_id=1, source_target_pairs={{0,8},{8,0},{1,9},{9,1},{2,10},{10,2},{3,11},{11,3},{4,12},{12,4},... | collective-permute-start | bytes 3145736 | tf_op jit(solution)/shard_map/ppermute | solution.py:104
  647.8 57.4 %collective-permute-start.43 = (bf16[2048,256]{1,0:T(8,128)(2,1)}, bf16[2048,256]{1,0:T(8,128)(2,1)}, u32[]{:S(2)}, u32[]{:S(2)}) collective-permute-start(bf16[2048,256]{1,0:T(8,128)(2,1)} %pad_maximum_fusion.21), channel_id=1, source_target_pairs={{0,16},{16,0},{1,17},{17,1},{2,18},{18,2},{3,19},{19,3},{4,20},{20... | collective-permute-start | bytes 3145736 | tf_op jit(solution)/shard_map/ppermute | solution.py:104
  648.2 28.9 %collective-permute-start.42 = (bf16[256,512]{0,1:T(8,128)(2,1)S(1)}, bf16[256,512]{0,1:T(8,128)(2,1)}, u32[]{:S(2)}, u32[]{:S(2)}) collective-permute-start(bf16[256,512]{0,1:T(8,128)(2,1)S(1)} %add_convert_fusion.9), channel_id=1, source_target_pairs={{0,8},{8,0},{1,9},{9,1},{2,10},{10,2},{3,11},{11,3},{4,12},{12,4},... | collective-permute-start | bytes 786440 | tf_op jit(solution)/shard_map/ppermute | solution.py:104
  654.8 50.3 %collective-permute-start.45 = (bf16[256,2048]{1,0:T(8,128)(2,1)}, bf16[256,2048]{1,0:T(8,128)(2,1)}, u32[]{:S(2)}, u32[]{:S(2)}) collective-permute-start(bf16[256,2048]{1,0:T(8,128)(2,1)} %reduce-scatter.8.cloned.1.call-done), channel_id=1, source_target_pairs={{0,16},{16,0},{1,17},{17,1},{2,18},{18,2},{3,19},{19,3},{4,20},{20... | collective-permute-start | bytes 3145736 | tf_op jit(solution)/shard_map/ppermute | solution.py:104
  656.2 48.9 %collective-permute-start.46 = (bf16[256,2048]{1,0:T(8,128)(2,1)}, bf16[256,2048]{1,0:T(8,128)(2,1)}, u32[]{:S(2)}, u32[]{:S(2)}) collective-permute-start(bf16[256,2048]{1,0:T(8,128)(2,1)} %reduce-scatter.8.cloned.1.call-done), channel_id=1, source_target_pairs={{0,8},{8,0},{1,9},{9,1},{2,10},{10,2},{3,11},{11,3},{4,12},{12,4},... | collective-permute-start | bytes 3145736 | tf_op jit(solution)/shard_map/ppermute | solution.py:104
  677.2 27.9 %collective-permute-start.41 = (bf16[512,512]{1,0:T(8,128)(2,1)}, bf16[512,512]{1,0:T(8,128)(2,1)}, u32[]{:S(2)}, u32[]{:S(2)}) collective-permute-start(bf16[512,512]{1,0:T(8,128)(2,1)} %fusion.75), channel_id=1, source_target_pairs={{2,0},{4,2},{6,4},{3,1},{5,3},{7,5},{10,8},{12,10},{14,12},{11,9},... | collective-permute-start | bytes 1572872 | tf_op jit(solution)/shard_map/ppermute | solution.py:631
  766.0 29.7 %collective-permute-start.56 = (bf16[256,2048]{1,0:T(8,128)(2,1)}, bf16[256,2048]{1,0:T(8,128)(2,1)}, u32[]{:S(2)}, u32[]{:S(2)}) collective-permute-start(bf16[256,2048]{1,0:T(8,128)(2,1)} %reduce-scatter.10.cloned.1.call-done), channel_id=1, source_target_pairs={{0,16},{16,0},{1,17},{17,1},{2,18},{18,2},{3,19},{19,3},{4,20},{20... | collective-permute-start | bytes 3145736 | tf_op jit(solution)/shard_map/ppermute | solution.py:104
  768.1 27.7 %collective-permute-start.57 = (bf16[256,2048]{1,0:T(8,128)(2,1)}, bf16[256,2048]{1,0:T(8,128)(2,1)}, u32[]{:S(2)}, u32[]{:S(2)}) collective-permute-start(bf16[256,2048]{1,0:T(8,128)(2,1)} %reduce-scatter.10.cloned.1.call-done), channel_id=1, source_target_pairs={{0,8},{8,0},{1,9},{9,1},{2,10},{10,2},{3,11},{11,3},{4,12},{12,4},... | collective-permute-start | bytes 3145736 | tf_op jit(solution)/shard_map/ppermute | solution.py:104
  796.9 28.3 %collective-permute-start.61 = (bf16[128,2048]{1,0:T(8,128)(2,1)S(1)}, bf16[128,2048]{1,0:T(8,128)(2,1)S(1)}, u32[]{:S(2)}, u32[]{:S(2)}) collective-permute-start(bf16[128,2048]{1,0:T(8,128)(2,1)S(1)} %slice.523), channel_id=1, source_target_pairs={{0,16},{16,0},{1,17},{17,1},{2,18},{18,2},{3,19},{19,3},{4,20},{20... | collective-permute-start | bytes 1572872 | tf_op jit(solution)/shard_map/ppermute | solution.py:104
  (198 other events, 2380.7 us)
Sparse Core Ops, SparseCore 0:
  13.4 67.4 all-gather.2
  84.9 223.8 all-gather.4
  422.7 53.7 reduce-scatter.5
  485.1 107.3 reduce-scatter.7
  594.7 87.9 reduce-scatter.9
  684.8 99.1 reduce-scatter.11
  786.3 66.7 reduce-scatter.13

commit v4 on v3

--- a/solution.py
+++ b/solution.py
@@ -457,13 +457,25 @@
     first_gather.next()
     ple_gather.next()
     waits(*first_gather.sent, *ple_gather.sent)
-    ple_blocks = reorder(ple_gather.blocks(), rep_axes)
+    (second_all,) = mark(jnp.concatenate(go(*second_gather.blocks()), axis=0))
+    gate_up = dot_plain(second_all, gate_up_cols)
+    hidden_all = (gelu_tanh(gate_up[:, :units]) * gate_up[:, units:]).astype(BF)
+    gate_up, hidden_all = mark(gate_up, hidden_all)
+    (norm_all,) = mark(dot_right_t(hidden_all, down_cols).astype(BF))
+    ffn_scatter = Scatter(
+        [norm_all[k * tokens : (k + 1) * tokens] for k in range(team)], team_axes, order
+    )
+    ple_blocks = reorder(go(*ple_gather.blocks()), rep_axes)
     gate_layer_full, project_full = mark(
         jnp.concatenate([block[:, :ple_part] for block in ple_blocks], axis=1),
         jnp.concatenate([block[:, ple_part:] for block in ple_blocks], axis=1),
     )
-    first_others = jnp.stack(first_gather.blocks()[1:])
+    first_others = jnp.stack(go(*first_gather.blocks()[1:]))
     first_sent = put(first_others, "core")
+    waits(*ffn_scatter.sent)
+    ffn_scatter.next()
+    (gate_up,) = go(gate_up)
+    ffn_value, ffn_slope = mark(*gelu_terms(gate_up[:, :units], gate_up[:, units:]))
     wait(first_sent)
     (first_all,) = mark(
         jnp.concatenate(
@@ -472,18 +484,6 @@
             axis=0,
         )
     )
-    (second_all,) = mark(jnp.concatenate(go(*second_gather.blocks()), axis=0))
-    gate_up = dot_plain(second_all, gate_up_cols)
-    hidden_all = (gelu_tanh(gate_up[:, :units]) * gate_up[:, units:]).astype(BF)
-    gate_up, hidden_all = mark(gate_up, hidden_all)
-    (norm_all,) = mark(dot_right_t(hidden_all, down_cols).astype(BF))
-    ffn_scatter = Scatter(
-        [norm_all[k * tokens : (k + 1) * tokens] for k in range(team)], team_axes, order
-    )
-    waits(*ffn_scatter.sent)
-    ffn_scatter.next()
-    (gate_up,) = go(gate_up)
-    ffn_value, ffn_slope = mark(*gelu_terms(gate_up[:, :units], gate_up[:, units:]))
     waits(*ffn_scatter.sent)
     (ffn_pre,) = mark(ffn_scatter.total())
     ffn_out, ffn_pull = jax.vjp(scaled_norm, ffn_pre, model_gains[4])
@@ -685,7 +685,8 @@
     gate_grad.spread()
     (norm_sum,) = mark(dot_right_t(go(d_proj)[0], qkv_part))
     norm_sent = put(norm_sum[tokens:], "core")
-    wait(norm_sent)
+    waits(norm_sent, *gate_grad.gather.sent)
+    gate_grad.gather.next()
     d_first_norm = (
         norm_sum[:tokens]
         + norm_sent.value
@@ -725,25 +726,23 @@
     grad_down = jnp.zeros((weight_rows, ffn_units), F32)
     grad_down = down_grad.place(grad_down, down_grad.gather.blocks(), 0)
     waits(*gain_sent, *gate_grad.gather.sent)
-    gate_grad.gather.next()
-    gains = gain_sum(gain_sent)
-    gain_sent = gain_put(gain_steps[1])
-    waits(*gain_sent, *gate_grad.gather.sent)
     up_grad.spread()
     gains = gain_sum(gain_sent)
-    for step in gain_steps[2:-1]:
+    for step in gain_steps[1:-2]:
         gain_sent = gain_put(step)
         waits(*gain_sent)
         gains = gain_sum(gain_sent)
-    gain_sent = gain_put(gain_steps[-1])
+    gain_sent = gain_put(gain_steps[-2])
     grad_gate_up = jnp.zeros((weight_rows, 2 * ffn_units), F32)
     grad_gate_up = gate_grad.place(grad_gate_up, gate_grad.gather.blocks(), 0)
     waits(*gain_sent, *up_grad.gather.sent)
     up_grad.gather.next()
     gains = gain_sum(gain_sent)
+    gain_sent = gain_put(gain_steps[-1])
     if staged:
         grad_gate_up = up_grad.place(grad_gate_up, up_grad.gather.near_blocks(), 0, ffn_units)
-    waits(*up_grad.gather.sent)
+    waits(*gain_sent, *up_grad.gather.sent)
+    gains = gain_sum(gain_sent)
     if staged:
         far_block = [up_grad.gather.far_block()]
         grad_gate_up = up_grad.place(grad_gate_up, far_block, 3, ffn_units)

time: 913 us -> 911 us (level)
    unnamed x324 -> x334, local copies, waits for them, and re-layouts: 46.1 us -> 50.4 us
  transfers between devices with their start and end apart: 81 -> 81, of which waited for: 37 -> 33; matrix products, arithmetic and copies ran while one was open for 38% -> 38% of each run, Pallas kernels for 4% -> 4%
where the time goes in v4:
time: 911 us; the launch traced here: 901 us
  waiting for transfers between devices  311 us (34%)
  matrix products  182 us (20%)
  other arithmetic  137 us (15%)
  local copies, waits for them, and re-layouts  123 us (14%)
  starting transfers between devices  94.7 us (10%)
  Pallas kernels  35.4 us (4%)
  between operations  17.1 us (2%)
    ppermute x67, waiting for transfers between devices, swap(): return lax.ppermute(value, axis, [(0, 1), (1, 0)])  219 us
    ppermute x67, starting transfers between devices, swap(): return lax.ppermute(value, axis, [(0, 1), (1, 0)])  83.2 us
    dot_general x10, matrix products, dot_right_t(): lax.dot_general(left_side, right_side, (((1,), (1,)), ((), ())), preferre...  81.1 us
    dot_general x10, matrix products, dot_plain(): return jnp.dot(left_side, right_side, preferred_element_type=jnp.float32)  62.4 us
    all_gather x1, waiting for transfers between devices, body(): lax.all_gather(attention_rows, shard_axes, axis=0, tiled=True)  58.4 us
    unnamed x334, local copies, waits for them, and re-layouts  50.4 us
    pallas_call x3, Pallas kernels, gradient_terms(): pl.pallas_call(terms_kernel, grid=(columns // step,), in_specs=[pl.BlockS...  35.4 us
    dynamic_update_slice x12, other arithmetic, place(): lax.dynamic_update_slice(whole, block.astype(F32), (0, start + rep_of(k)...  23.8 us
  transfers between devices with their start and end apart: 81, of which 33 were waited for; matrix products, arithmetic and copies ran while one was open for 38% of the time, Pallas kernels for 4%

profile of v4, /device:TPU:0, one launch (start us, length us, event | category | flops | bytes accessed | tf_op | source)
XLA Modules:
  0.0 900.8 jit_solution(11339945227261168134)
XLA Ops:
  22.4 58.4 %all-gather.3.cloned.1.call-done = bf16[2048,1536]{1,0:T(8,128)(2,1)} async-done(((bf16[256,1536]{1,0:T(8,128)(2,1)}), bf16[2048,1536]{1,0:T(8,128)(2,1)}) %all-gather.3.cloned.1.call-update) | async-done | bytes 6291472 | tf_op jit(solution)/shard_map/all_gather | solution.py:313
  98.2 24.4 %collective-permute-done.2 = bf16[2048,384]{1,0:T(8,128)(2,1)S(1)} collective-permute-done((bf16[2048,384]{1,0:T(8,128)(2,1)S(1)}, bf16[2048,384]{1,0:T(8,128)(2,1)S(1)}, u32[]{:S(2)}, u32[]{:S(2)}) %collective-permute-start.2) | collective-permute-done | bytes 1572896 | tf_op jit(solution)/shard_map/ppermute | solution.py:104
  126.2 16.3 %collective-permute-done.4 = bf16[1024,384]{1,0:T(8,128)(2,1)S(1)} collective-permute-done((bf16[1024,384]{1,0:T(8,128)(2,1)S(1)}, bf16[1024,384]{1,0:T(8,128)(2,1)S(1)}, u32[]{:S(2)}, u32[]{:S(2)}) %collective-permute-start.4) | collective-permute-done | bytes 786464 | tf_op jit(solution)/shard_map/ppermute | solution.py:104
  167.9 12.8 %collective-permute-done.6 = bf16[512,512]{1,0:T(8,128)(2,1)} collective-permute-done((bf16[512,512]{1,0:T(8,128)(2,1)}, bf16[512,512]{1,0:T(8,128)(2,1)}, u32[]{:S(2)}, u32[]{:S(2)}) %collective-permute-start.6) | collective-permute-done | bytes 524320 | tf_op jit(solution)/shard_map/ppermute | solution.py:391
  194.3 14.9 %fusion.131 = f32[512,2048]{1,0:T(8,128)S(1)} fusion(bf16[512,1024]{0,1:T(8,128)(2,1)S(1)} %bitcast.189, bf16[1024,256]{1,0:T(8,128)(2,1)S(1)} %collective-permute-done.9, bf16[1024,256]{1,0:T(8,128)(2,1)S(1)} %collective-permute-done.10, bf16[2048,256]{1,0:T(8,128)(2,1)} %collective-permute-done.7, bf16[2048,256]{1,0:T(8,128)(2,1)} %collective-permute-done.8, ...), kind=kOutput, calls=%fused_computation.413 | convolution fusion | flops 2168455168 | bytes 9437184 | tf_op jit(solution)/shard_map/dot_general | solution.py:53
  219.6 22.3 %collective-permute-done.12 = bf16[256,2048]{1,0:T(8,128)(2,1)S(1)} collective-permute-done((bf16[256,2048]{1,0:T(8,128)(2,1)S(1)}, bf16[256,2048]{1,0:T(8,128)(2,1)S(1)}, u32[]{:S(2)}, u32[]{:S(2)}) %collective-permute-start.12) | collective-permute-done | bytes 1048608 | tf_op jit(solution)/shard_map/ppermute | solution.py:104
  245.4 10.7 %collective-permute-done.14 = bf16[128,2048]{1,0:T(8,128)(2,1)S(1)} collective-permute-done((bf16[128,2048]{1,0:T(8,128)(2,1)S(1)}, bf16[128,2048]{1,0:T(8,128)(2,1)S(1)}, u32[]{:S(2)}, u32[]{:S(2)}) %collective-permute-start.14) | collective-permute-done | bytes 524320 | tf_op jit(solution)/shard_map/ppermute | solution.py:104
  261.7 29.1 %collective-permute-done.18 = bf16[2048,128]{1,0:T(8,128)(2,1)S(1)} collective-permute-done((bf16[2048,128]{1,0:T(8,128)(2,1)S(1)}, bf16[2048,128]{1,0:T(8,128)(2,1)S(1)}, u32[]{:S(2)}, u32[]{:S(2)}) %collective-permute-start.18) | collective-permute-done | bytes 524320 | tf_op jit(solution)/shard_map/ppermute | solution.py:104
  296.5 11.9 %collective-permute-done.22 = bf16[1024,128]{1,0:T(8,128)(2,1)S(1)} collective-permute-done((bf16[1024,128]{1,0:T(8,128)(2,1)S(1)}, bf16[1024,128]{1,0:T(8,128)(2,1)S(1)}, u32[]{:S(2)}, u32[]{:S(2)}) %collective-permute-start.22) | collective-permute-done | bytes 262176 | tf_op jit(solution)/shard_map/ppermute | solution.py:104
  314.8 21.7 %fusion.7 = f32[1024,4096]{1,0:T(8,128)S(1)} fusion(bf16[1024,2048]{1,0:T(8,128)(2,1)} %constant_dynamic-update-slice_fusion.3.left_ref, bf16[2048,6144]{1,0:T(8,128)(2,1)} %all-gather.5.cloned.1.call-done), kind=kOutput, calls=%fused_computation.8 | convolution fusion | flops 17179869184 | bytes 37748736 | tf_op jit(solution)/shard_map/dot_general | solution.py:49
  339.5 14.4 %fusion.33 = bf16[1024,2048]{1,0:T(8,128)(2,1)} fusion(bf16[1024,2048]{1,0:T(8,128)(2,1)S(1)} %fusion.17.right_ref, bf16[2048,6144]{1,0:T(8,128)(2,1)} %all-gather.5.cloned.1.call-done), kind=kOutput, calls=%fused_computation.60 | convolution fusion | flops 8592031744 | bytes 16777216 | tf_op jit(solution)/shard_map/dot_general | solution.py:53
  415.7 17.9 %collective-permute-done.29 = bf16[256,2048]{1,0:T(8,128)(2,1)S(1)} collective-permute-done((bf16[256,2048]{1,0:T(8,128)(2,1)}, bf16[256,2048]{1,0:T(8,128)(2,1)S(1)}, u32[]{:S(2)}, u32[]{:S(2)}) %collective-permute-start.29) | collective-permute-done | bytes 1048608 | tf_op jit(solution)/shard_map/ppermute | solution.py:104
  447.1 12.1 %fusion.39 = bf16[256,2048]{1,0:T(8,128)(2,1)} fusion(bf16[2048,6144]{1,0:T(8,128)(2,1)} %all-gather.5.cloned.1.call-done, bf16[256,2048]{1,0:T(8,128)(2,1)} %get-tuple-element.405, bf16[256,2048]{1,0:T(8,128)(2,1)} %get-tuple-element.404), kind=kOutput, calls=%fused_computation.81 | convolution fusion | flops 4299685888 | bytes 19922944 | tf_op jit(solution)/shard_map/dot_general | solution.py:53
  464.7 11.1 %shard_map.237 = bf16[2048,2048]{1,0:T(8,128)(2,1)} custom-call(bf16[1024,2048]{1,0:T(8,128)(2,1)S(1)} %pad_maximum_fusion.left_ref, bf16[1024,2048]{1,0:T(8,128)(2,1)S(1)} %copy-done.3), custom_call_target="tpu_custom_call" | custom-call | flops 1 | bytes 1 | tf_op jit(solution)/shard_map/pallas_call | solution.py:71
  491.0 15.0 %fusion.36 = bf16[512,2048]{1,0:T(8,128)(2,1)} fusion(bf16[2048,6144]{1,0:T(8,128)(2,1)} %all-gather.5.cloned.1.call-done, bf16[512,2048]{1,0:T(8,128)(2,1)} %get-tuple-element.379, bf16[512,2048]{1,0:T(8,128)(2,1)} %get-tuple-element.378), kind=kOutput, calls=%fused_computation.74 | convolution fusion | flops 8599371776 | bytes 23068672 | tf_op jit(solution)/shard_map/dot_general | solution.py:53
  513.7 11.1 %fusion.42 = bf16[256,2048]{1,0:T(8,128)(2,1)S(1)} fusion(bf16[2048,6144]{1,0:T(8,128)(2,1)} %all-gather.5.cloned.1.call-done, bf16[256,2048]{1,0:T(8,128)(2,1)} %get-tuple-element.403, bf16[256,2048]{1,0:T(8,128)(2,1)} %get-tuple-element.402), kind=kOutput, calls=%fused_computation.82 | convolution fusion | flops 4299685888 | bytes 19922944 | tf_op jit(solution)/shard_map/dot_general | solution.py:53
  539.8 12.1 %shard_map.238 = bf16[2048,2048]{1,0:T(8,128)(2,1)S(1)} custom-call(bf16[1024,2048]{1,0:T(8,128)(2,1)} %constant_dynamic-update-slice_fusion.3.left_ref, bf16[1024,4096]{1,0:T(8,128)(2,1)} %copy-done.6), custom_call_target="tpu_custom_call" | custom-call | flops 1 | bytes 1 | tf_op jit(solution)/shard_map/pallas_call | solution.py:71
  561.9 12.1 %shard_map.239 = bf16[2048,2048]{1,0:T(8,128)(2,1)S(1)} custom-call(bf16[1024,2048]{1,0:T(8,128)(2,1)} %constant_dynamic-update-slice_fusion.3.left_ref, bf16[1024,4096]{1,0:T(8,128)(2,1)} %copy-done.6), custom_call_target="tpu_custom_call" | custom-call | flops 1 | bytes 1 | tf_op jit(solution)/shard_map/pallas_call | solution.py:71
  612.0 11.7 %fusion.19 = bf16[4,512,1024]{1,2,0:T(8,128)(2,1)} fusion(f32[1024,512,4]{1,0,2:T(8,128)} %copy-done.9, f32[4,512]{1,0:T(4,128)S(1)} %log_add_fusion, pred[512,1024]{0,1:T(8,128)(4,1)S(1)} %copy-done.31, bf16[512,4,256]{0,2,1:T(8,128)(2,1)} %copy.157, bf16[1024,512]{1,0:T(8,128)(2,1)} %copy-done.63), kind=kOutput, calls=%fused_computation.22 | convolution fusion | flops 2168458240 | bytes 25182208 | tf_op jit(solution)/shard_map/sub | solution.py:616
  650.4 15.4 %collective-permute-done.42 = bf16[256,512]{0,1:T(8,128)(2,1)} collective-permute-done((bf16[256,512]{0,1:T(8,128)(2,1)S(1)}, bf16[256,512]{0,1:T(8,128)(2,1)}, u32[]{:S(2)}, u32[]{:S(2)}) %collective-permute-start.42) | collective-permute-done | bytes 262176 | tf_op jit(solution)/shard_map/ppermute | solution.py:104
  671.6 21.1 %collective-permute-done.41 = bf16[512,512]{1,0:T(8,128)(2,1)} collective-permute-done((bf16[512,512]{1,0:T(8,128)(2,1)}, bf16[512,512]{1,0:T(8,128)(2,1)}, u32[]{:S(2)}, u32[]{:S(2)}) %collective-permute-start.41) | collective-permute-done | bytes 524320 | tf_op jit(solution)/shard_map/ppermute | solution.py:631
  756.4 18.4 %collective-permute-done.53 = bf16[256,2048]{1,0:T(8,128)(2,1)} collective-permute-done((bf16[256,2048]{1,0:T(8,128)(2,1)}, bf16[256,2048]{1,0:T(8,128)(2,1)}, u32[]{:S(2)}, u32[]{:S(2)}) %collective-permute-start.53) | collective-permute-done | bytes 1048608 | tf_op jit(solution)/shard_map/ppermute | solution.py:104
  807.7 20.4 %collective-permute-start.60 = (f32[50,256]{1,0:T(8,128)S(1)}, f32[50,256]{1,0:T(8,128)S(1)}, u32[]{:S(2)}, u32[]{:S(2)}) collective-permute-start(f32[50,256]{1,0:T(8,128)S(1)} %add_add_fusion.9), channel_id=1, source_target_pairs={{0,4},{4,0},{1,5},{5,1},{2,6},{6,2},{3,7},{7,3},{8,12},{12,8},{9,1... | collective-permute-start | bytes 153608 | tf_op jit(solution)/shard_map/ppermute | solution.py:104
  865.6 11.5 %collective-permute-done.68 = bf16[256,128]{0,1:T(8,128)(2,1)S(1)} collective-permute-done((bf16[256,128]{0,1:T(8,128)(2,1)S(1)}, bf16[256,128]{0,1:T(8,128)(2,1)S(1)}, u32[]{:S(2)}, u32[]{:S(2)}) %collective-permute-start.68) | collective-permute-done | bytes 65568 | tf_op jit(solution)/shard_map/ppermute | solution.py:104
  (719 shorter events, 456.9 us)
Async XLA Ops:
  7.2 73.7 %all-gather.3.cloned.1.call-start = ((), (), s32[]{:S(2)}) async-start(), calls=%async_computation.5 | async-start | bytes 7077888 | tf_op jit(solution)/shard_map/all_gather | solution.py:313
  13.2 301.6 %all-gather.5.cloned.1.call-start = ((), (), s32[]{:S(2)}) async-start(), calls=%async_computation.6 | async-start | bytes 28311552 | tf_op jit(solution)/shard_map/all_gather | solution.py:346
  84.8 391.0 %reduce-scatter.6.cloned.1.call-start = ((), (), s32[]{:S(2)}) async-start(), calls=%async_computation.7 | async-start | bytes 2359296 | tf_op jit(solution)/shard_map/reduce_scatter | solution.py:515
  86.0 36.5 %collective-permute-start.2 = (bf16[2048,384]{1,0:T(8,128)(2,1)S(1)}, bf16[2048,384]{1,0:T(8,128)(2,1)S(1)}, u32[]{:S(2)}, u32[]{:S(2)}) collective-permute-start(bf16[2048,384]{1,0:T(8,128)(2,1)S(1)} %constant_dynamic-slice_fusion.1), channel_id=1, source_target_pairs={{0,16},{16,0},{1,17},{17,1},{2,18},{18,2},{3,19},{19,3},{4,20},{20... | collective-permute-start | bytes 4718600 | tf_op jit(solution)/shard_map/ppermute | solution.py:104
  87.5 36.3 %collective-permute-start.3 = (bf16[2048,384]{1,0:T(8,128)(2,1)S(1)}, bf16[2048,384]{1,0:T(8,128)(2,1)S(1)}, u32[]{:S(2)}, u32[]{:S(2)}) collective-permute-start(bf16[2048,384]{1,0:T(8,128)(2,1)S(1)} %constant_dynamic-slice_fusion.1), channel_id=1, source_target_pairs={{0,8},{8,0},{1,9},{9,1},{2,10},{10,2},{3,11},{11,3},{4,12},{12,4},... | collective-permute-start | bytes 4718600 | tf_op jit(solution)/shard_map/ppermute | solution.py:104
  143.0 37.6 %collective-permute-start.7 = (bf16[2048,256]{1,0:T(8,128)(2,1)}, bf16[2048,256]{1,0:T(8,128)(2,1)}, u32[]{:S(2)}, u32[]{:S(2)}) collective-permute-start(bf16[2048,256]{1,0:T(8,128)(2,1)} %constant_dynamic-slice_fusion), channel_id=1, source_target_pairs={{0,16},{16,0},{1,17},{17,1},{2,18},{18,2},{3,19},{19,3},{4,20},{20... | collective-permute-start | bytes 3145736 | tf_op jit(solution)/shard_map/ppermute | solution.py:104
  144.5 36.2 %collective-permute-start.8 = (bf16[2048,256]{1,0:T(8,128)(2,1)}, bf16[2048,256]{1,0:T(8,128)(2,1)}, u32[]{:S(2)}, u32[]{:S(2)}) collective-permute-start(bf16[2048,256]{1,0:T(8,128)(2,1)} %constant_dynamic-slice_fusion), channel_id=1, source_target_pairs={{0,8},{8,0},{1,9},{9,1},{2,10},{10,2},{3,11},{11,3},{4,12},{12,4},... | collective-permute-start | bytes 3145736 | tf_op jit(solution)/shard_map/ppermute | solution.py:104
  256.5 35.4 %collective-permute-start.16 = (bf16[256,2048]{1,0:T(8,128)(2,1)S(1)}, bf16[256,2048]{1,0:T(8,128)(2,1)S(1)}, u32[]{:S(2)}, u32[]{:S(2)}) collective-permute-start(bf16[256,2048]{1,0:T(8,128)(2,1)S(1)} %slice.561), channel_id=1, source_target_pairs={{0,16},{16,0},{1,17},{17,1},{2,18},{18,2},{3,19},{19,3},{4,20},{20... | collective-permute-start | bytes 3145736 | tf_op jit(solution)/shard_map/ppermute | solution.py:104
  257.9 34.0 %collective-permute-start.17 = (bf16[256,2048]{1,0:T(8,128)(2,1)S(1)}, bf16[256,2048]{1,0:T(8,128)(2,1)S(1)}, u32[]{:S(2)}, u32[]{:S(2)}) collective-permute-start(bf16[256,2048]{1,0:T(8,128)(2,1)S(1)} %slice.561), channel_id=1, source_target_pairs={{0,8},{8,0},{1,9},{9,1},{2,10},{10,2},{3,11},{11,3},{4,12},{12,4},... | collective-permute-start | bytes 3145736 | tf_op jit(solution)/shard_map/ppermute | solution.py:104
  260.5 30.3 %collective-permute-start.18 = (bf16[2048,128]{1,0:T(8,128)(2,1)S(1)}, bf16[2048,128]{1,0:T(8,128)(2,1)S(1)}, u32[]{:S(2)}, u32[]{:S(2)}) collective-permute-start(bf16[2048,128]{1,0:T(8,128)(2,1)S(1)} %slice.467), channel_id=1, source_target_pairs={{0,16},{16,0},{1,17},{17,1},{2,18},{18,2},{3,19},{19,3},{4,20},{20... | collective-permute-start | bytes 1572872 | tf_op jit(solution)/shard_map/ppermute | solution.py:104
  261.2 30.8 %collective-permute-start.19 = (bf16[2048,128]{1,0:T(8,128)(2,1)S(1)}, bf16[2048,128]{1,0:T(8,128)(2,1)S(1)}, u32[]{:S(2)}, u32[]{:S(2)}) collective-permute-start(bf16[2048,128]{1,0:T(8,128)(2,1)S(1)} %slice.467), channel_id=1, source_target_pairs={{0,8},{8,0},{1,9},{9,1},{2,10},{10,2},{3,11},{11,3},{4,12},{12,4},... | collective-permute-start | bytes 1572872 | tf_op jit(solution)/shard_map/ppermute | solution.py:104
  415.5 228.7 %reduce-scatter.8.cloned.1.call-start = ((), (), s32[]{:S(2)}) async-start(), calls=%async_computation.8 | async-start | bytes 9437184 | tf_op jit(solution)/shard_map/reduce_scatter | solution.py:564
  475.8 273.2 %reduce-scatter.10.cloned.1.call-start = ((), (), s32[]{:S(2)}) async-start(), calls=%async_computation.9 | async-start | bytes 9437184 | tf_op jit(solution)/shard_map/reduce_scatter | solution.py:564
  555.2 250.3 %reduce-scatter.12.cloned.1.call-start = ((), (), s32[]{:S(2)}) async-start(), calls=%async_computation.10 | async-start | bytes 9437184 | tf_op jit(solution)/shard_map/reduce_scatter | solution.py:564
  577.4 282.2 %reduce-scatter.14.cloned.1.call-start = ((), (), s32[]{:S(2)}) async-start(), calls=%async_computation.11 | async-start | bytes 6488064 | tf_op jit(solution)/shard_map/reduce_scatter | solution.py:682
  633.8 58.8 %collective-permute-start.44 = (bf16[2048,256]{1,0:T(8,128)(2,1)}, bf16[2048,256]{1,0:T(8,128)(2,1)}, u32[]{:S(2)}, u32[]{:S(2)}) collective-permute-start(bf16[2048,256]{1,0:T(8,128)(2,1)} %pad_maximum_fusion.23), channel_id=1, source_target_pairs={{0,8},{8,0},{1,9},{9,1},{2,10},{10,2},{3,11},{11,3},{4,12},{12,4},... | collective-permute-start | bytes 3145736 | tf_op jit(solution)/shard_map/ppermute | solution.py:104
  636.5 56.2 %collective-permute-start.43 = (bf16[2048,256]{1,0:T(8,128)(2,1)}, bf16[2048,256]{1,0:T(8,128)(2,1)}, u32[]{:S(2)}, u32[]{:S(2)}) collective-permute-start(bf16[2048,256]{1,0:T(8,128)(2,1)} %pad_maximum_fusion.22), channel_id=1, source_target_pairs={{0,16},{16,0},{1,17},{17,1},{2,18},{18,2},{3,19},{19,3},{4,20},{20... | collective-permute-start | bytes 3145736 | tf_op jit(solution)/shard_map/ppermute | solution.py:104
  637.9 27.9 %collective-permute-start.42 = (bf16[256,512]{0,1:T(8,128)(2,1)S(1)}, bf16[256,512]{0,1:T(8,128)(2,1)}, u32[]{:S(2)}, u32[]{:S(2)}) collective-permute-start(bf16[256,512]{0,1:T(8,128)(2,1)S(1)} %add_convert_fusion.9), channel_id=1, source_target_pairs={{0,8},{8,0},{1,9},{9,1},{2,10},{10,2},{3,11},{11,3},{4,12},{12,4},... | collective-permute-start | bytes 786440 | tf_op jit(solution)/shard_map/ppermute | solution.py:104
  644.1 48.5 %collective-permute-start.45 = (bf16[256,2048]{1,0:T(8,128)(2,1)}, bf16[256,2048]{1,0:T(8,128)(2,1)}, u32[]{:S(2)}, u32[]{:S(2)}) collective-permute-start(bf16[256,2048]{1,0:T(8,128)(2,1)} %reduce-scatter.8.cloned.1.call-done), channel_id=1, source_target_pairs={{0,16},{16,0},{1,17},{17,1},{2,18},{18,2},{3,19},{19,3},{4,20},{20... | collective-permute-start | bytes 3145736 | tf_op jit(solution)/shard_map/ppermute | solution.py:104
  644.9 47.7 %collective-permute-start.46 = (bf16[256,2048]{1,0:T(8,128)(2,1)}, bf16[256,2048]{1,0:T(8,128)(2,1)}, u32[]{:S(2)}, u32[]{:S(2)}) collective-permute-start(bf16[256,2048]{1,0:T(8,128)(2,1)} %reduce-scatter.8.cloned.1.call-done), channel_id=1, source_target_pairs={{0,8},{8,0},{1,9},{9,1},{2,10},{10,2},{3,11},{11,3},{4,12},{12,4},... | collective-permute-start | bytes 3145736 | tf_op jit(solution)/shard_map/ppermute | solution.py:104
  749.0 27.3 %collective-permute-start.52 = (f32[256,2048]{1,0:T(8,128)}, f32[256,2048]{1,0:T(8,128)}, u32[]{:S(2)}, u32[]{:S(2)}) collective-permute-start(f32[256,2048]{1,0:T(8,128)} %slice.613), channel_id=1, source_target_pairs={{0,1},{1,0},{2,3},{3,2},{4,5},{5,4},{6,7},{7,6},{8,9},{9,8},{10,11... | collective-permute-start | bytes 6291464 | tf_op jit(solution)/shard_map/ppermute | solution.py:104
  805.5 41.1 %collective-permute-start.63 = (bf16[256,2048]{1,0:T(8,128)(2,1)}, bf16[256,2048]{1,0:T(8,128)(2,1)S(1)}, u32[]{:S(2)}, u32[]{:S(2)}) collective-permute-start(bf16[256,2048]{1,0:T(8,128)(2,1)} %reduce-scatter.12.cloned.1.call-done), channel_id=1, source_target_pairs={{0,16},{16,0},{1,17},{17,1},{2,18},{18,2},{3,19},{19,3},{4,20},{20... | collective-permute-start | bytes 3145736 | tf_op jit(solution)/shard_map/ppermute | solution.py:104
  807.3 39.3 %collective-permute-start.64 = (bf16[256,2048]{1,0:T(8,128)(2,1)}, bf16[256,2048]{1,0:T(8,128)(2,1)S(1)}, u32[]{:S(2)}, u32[]{:S(2)}) collective-permute-start(bf16[256,2048]{1,0:T(8,128)(2,1)} %reduce-scatter.12.cloned.1.call-done), channel_id=1, source_target_pairs={{0,8},{8,0},{1,9},{9,1},{2,10},{10,2},{3,11},{11,3},{4,12},{12,4},... | collective-permute-start | bytes 3145736 | tf_op jit(solution)/shard_map/ppermute | solution.py:104
  807.7 38.9 %collective-permute-start.60 = (f32[50,256]{1,0:T(8,128)S(1)}, f32[50,256]{1,0:T(8,128)S(1)}, u32[]{:S(2)}, u32[]{:S(2)}) collective-permute-start(f32[50,256]{1,0:T(8,128)S(1)} %add_add_fusion.9), channel_id=1, source_target_pairs={{0,4},{4,0},{1,5},{5,1},{2,6},{6,2},{3,7},{7,3},{8,12},{12,8},{9,1... | collective-permute-start | bytes 153608 | tf_op jit(solution)/shard_map/ppermute | solution.py:104
  (204 other events, 2560.3 us)
Sparse Core Ops, SparseCore 0:
  13.4 67.4 all-gather.2
  84.9 223.8 all-gather.4
  415.6 52.8 reduce-scatter.5
  476.0 107.2 reduce-scatter.7
  585.3 87.9 reduce-scatter.9
  675.5 99.1 reduce-scatter.11
  777.0 65.9 reduce-scatter.13

commit v5 on v4

--- a/solution.py
+++ b/solution.py
@@ -732,17 +732,13 @@
         gain_sent = gain_put(step)
         waits(*gain_sent)
         gains = gain_sum(gain_sent)
-    gain_sent = gain_put(gain_steps[-2])
     grad_gate_up = jnp.zeros((weight_rows, 2 * ffn_units), F32)
     grad_gate_up = gate_grad.place(grad_gate_up, gate_grad.gather.blocks(), 0)
-    waits(*gain_sent, *up_grad.gather.sent)
+    waits(*up_grad.gather.sent)
     up_grad.gather.next()
-    gains = gain_sum(gain_sent)
-    gain_sent = gain_put(gain_steps[-1])
     if staged:
         grad_gate_up = up_grad.place(grad_gate_up, up_grad.gather.near_blocks(), 0, ffn_units)
-    waits(*gain_sent, *up_grad.gather.sent)
-    gains = gain_sum(gain_sent)
+    waits(*up_grad.gather.sent)
     if staged:
         far_block = [up_grad.gather.far_block()]
         grad_gate_up = up_grad.place(grad_gate_up, far_block, 3, ffn_units)
@@ -753,12 +749,16 @@
     attention_gather = Gather(attention_sum[:, :attention_width], rep_axes, order)
     laurel_sum = attention_sum[:, attention_width:]
     laurel_sent = put(laurel_sum, rep_axes[0])
-    waits(laurel_sent, *attention_gather.sent)
+    gain_sent = gain_put(gain_steps[-2])
+    waits(laurel_sent, *gain_sent, *attention_gather.sent)
+    gains = gain_sum(gain_sent)
+    gain_sent = gain_put(gain_steps[-1])
     attention_gather.next()
     for axis in rep_axes[1:]:
         laurel_sum = combine(laurel_sum, laurel_sent.value)
         laurel_sent = put(laurel_sum, axis)
-    waits(laurel_sent, *attention_gather.sent)
+    waits(laurel_sent, *gain_sent, *attention_gather.sent)
+    gains = gain_sum(gain_sent)
     attention_blocks = reorder(attention_gather.blocks(), rep_axes)
     grad_qkv = jnp.concatenate(
         [

time: 911 us -> 917 us (level)
    unnamed x334 -> x330, local copies, waits for them, and re-layouts: 50.4 us -> 50 us
  transfers between devices with their start and end apart: 81 -> 81, of which waited for: 33 -> 37; matrix products, arithmetic and copies ran while one was open for 38% -> 38% of each run, Pallas kernels for 4% -> 4%
where the time goes in v5:
time: 917 us; the launch traced here: 904 us
  waiting for transfers between devices  312 us (34%)
  matrix products  182 us (20%)
  other arithmetic  140 us (15%)
  local copies, waits for them, and re-layouts  122 us (13%)
  starting transfers between devices  94.7 us (10%)
  Pallas kernels  35.4 us (4%)
  between operations  17 us (2%)
    ppermute x67, waiting for transfers between devices, swap(): return lax.ppermute(value, axis, [(0, 1), (1, 0)])  218 us
    ppermute x67, starting transfers between devices, swap(): return lax.ppermute(value, axis, [(0, 1), (1, 0)])  83 us
    dot_general x10, matrix products, dot_right_t(): lax.dot_general(left_side, right_side, (((1,), (1,)), ((), ())), preferre...  81.1 us
    dot_general x10, matrix products, dot_plain(): return jnp.dot(left_side, right_side, preferred_element_type=jnp.float32)  62.4 us
    all_gather x1, waiting for transfers between devices, body(): lax.all_gather(attention_rows, shard_axes, axis=0, tiled=True)  58.4 us
    unnamed x330, local copies, waits for them, and re-layouts  50 us
    pallas_call x3, Pallas kernels, gradient_terms(): pl.pallas_call(terms_kernel, grid=(columns // step,), in_specs=[pl.BlockS...  35.4 us
    dynamic_update_slice x12, other arithmetic, place(): lax.dynamic_update_slice(whole, block.astype(F32), (0, start + rep_of(k)...  23.8 us
  transfers between devices with their start and end apart: 81, of which 37 were waited for; matrix products, arithmetic and copies ran while one was open for 38% of the time, Pallas kernels for 4%

profile of v5, /device:TPU:0, one launch (start us, length us, event | category | flops | bytes accessed | tf_op | source)
XLA Modules:
  0.0 903.6 jit_solution(2206958416338671683)
XLA Ops:
  22.4 58.4 %all-gather.3.cloned.1.call-done = bf16[2048,1536]{1,0:T(8,128)(2,1)} async-done(((bf16[256,1536]{1,0:T(8,128)(2,1)}), bf16[2048,1536]{1,0:T(8,128)(2,1)}) %all-gather.3.cloned.1.call-update) | async-done | bytes 6291472 | tf_op jit(solution)/shard_map/all_gather | solution.py:313
  98.2 24.4 %collective-permute-done.2 = bf16[2048,384]{1,0:T(8,128)(2,1)S(1)} collective-permute-done((bf16[2048,384]{1,0:T(8,128)(2,1)S(1)}, bf16[2048,384]{1,0:T(8,128)(2,1)S(1)}, u32[]{:S(2)}, u32[]{:S(2)}) %collective-permute-start.2) | collective-permute-done | bytes 1572896 | tf_op jit(solution)/shard_map/ppermute | solution.py:104
  126.2 16.3 %collective-permute-done.4 = bf16[1024,384]{1,0:T(8,128)(2,1)S(1)} collective-permute-done((bf16[1024,384]{1,0:T(8,128)(2,1)S(1)}, bf16[1024,384]{1,0:T(8,128)(2,1)S(1)}, u32[]{:S(2)}, u32[]{:S(2)}) %collective-permute-start.4) | collective-permute-done | bytes 786464 | tf_op jit(solution)/shard_map/ppermute | solution.py:104
  167.9 12.8 %collective-permute-done.6 = bf16[512,512]{1,0:T(8,128)(2,1)} collective-permute-done((bf16[512,512]{1,0:T(8,128)(2,1)}, bf16[512,512]{1,0:T(8,128)(2,1)}, u32[]{:S(2)}, u32[]{:S(2)}) %collective-permute-start.6) | collective-permute-done | bytes 524320 | tf_op jit(solution)/shard_map/ppermute | solution.py:391
  194.3 14.9 %fusion.131 = f32[512,2048]{1,0:T(8,128)S(1)} fusion(bf16[512,1024]{0,1:T(8,128)(2,1)S(1)} %bitcast.189, bf16[1024,256]{1,0:T(8,128)(2,1)S(1)} %collective-permute-done.9, bf16[1024,256]{1,0:T(8,128)(2,1)S(1)} %collective-permute-done.10, bf16[2048,256]{1,0:T(8,128)(2,1)} %collective-permute-done.7, bf16[2048,256]{1,0:T(8,128)(2,1)} %collective-permute-done.8, ...), kind=kOutput, calls=%fused_computation.413 | convolution fusion | flops 2168455168 | bytes 9437184 | tf_op jit(solution)/shard_map/dot_general | solution.py:53
  219.6 22.3 %collective-permute-done.12 = bf16[256,2048]{1,0:T(8,128)(2,1)S(1)} collective-permute-done((bf16[256,2048]{1,0:T(8,128)(2,1)S(1)}, bf16[256,2048]{1,0:T(8,128)(2,1)S(1)}, u32[]{:S(2)}, u32[]{:S(2)}) %collective-permute-start.12) | collective-permute-done | bytes 1048608 | tf_op jit(solution)/shard_map/ppermute | solution.py:104
  245.4 10.7 %collective-permute-done.14 = bf16[128,2048]{1,0:T(8,128)(2,1)S(1)} collective-permute-done((bf16[128,2048]{1,0:T(8,128)(2,1)S(1)}, bf16[128,2048]{1,0:T(8,128)(2,1)S(1)}, u32[]{:S(2)}, u32[]{:S(2)}) %collective-permute-start.14) | collective-permute-done | bytes 524320 | tf_op jit(solution)/shard_map/ppermute | solution.py:104
  261.7 29.1 %collective-permute-done.18 = bf16[2048,128]{1,0:T(8,128)(2,1)S(1)} collective-permute-done((bf16[2048,128]{1,0:T(8,128)(2,1)S(1)}, bf16[2048,128]{1,0:T(8,128)(2,1)S(1)}, u32[]{:S(2)}, u32[]{:S(2)}) %collective-permute-start.18) | collective-permute-done | bytes 524320 | tf_op jit(solution)/shard_map/ppermute | solution.py:104
  296.5 11.9 %collective-permute-done.22 = bf16[1024,128]{1,0:T(8,128)(2,1)S(1)} collective-permute-done((bf16[1024,128]{1,0:T(8,128)(2,1)S(1)}, bf16[1024,128]{1,0:T(8,128)(2,1)S(1)}, u32[]{:S(2)}, u32[]{:S(2)}) %collective-permute-start.22) | collective-permute-done | bytes 262176 | tf_op jit(solution)/shard_map/ppermute | solution.py:104
  314.8 21.7 %fusion.7 = f32[1024,4096]{1,0:T(8,128)S(1)} fusion(bf16[1024,2048]{1,0:T(8,128)(2,1)} %constant_dynamic-update-slice_fusion.3.left_ref, bf16[2048,6144]{1,0:T(8,128)(2,1)} %all-gather.5.cloned.1.call-done), kind=kOutput, calls=%fused_computation.8 | convolution fusion | flops 17179869184 | bytes 37748736 | tf_op jit(solution)/shard_map/dot_general | solution.py:49
  339.5 14.4 %fusion.33 = bf16[1024,2048]{1,0:T(8,128)(2,1)} fusion(bf16[1024,2048]{1,0:T(8,128)(2,1)S(1)} %fusion.17.right_ref, bf16[2048,6144]{1,0:T(8,128)(2,1)} %all-gather.5.cloned.1.call-done), kind=kOutput, calls=%fused_computation.60 | convolution fusion | flops 8592031744 | bytes 16777216 | tf_op jit(solution)/shard_map/dot_general | solution.py:53
  415.7 17.9 %collective-permute-done.29 = bf16[256,2048]{1,0:T(8,128)(2,1)S(1)} collective-permute-done((bf16[256,2048]{1,0:T(8,128)(2,1)}, bf16[256,2048]{1,0:T(8,128)(2,1)S(1)}, u32[]{:S(2)}, u32[]{:S(2)}) %collective-permute-start.29) | collective-permute-done | bytes 1048608 | tf_op jit(solution)/shard_map/ppermute | solution.py:104
  447.1 12.1 %fusion.39 = bf16[256,2048]{1,0:T(8,128)(2,1)} fusion(bf16[2048,6144]{1,0:T(8,128)(2,1)} %all-gather.5.cloned.1.call-done, bf16[256,2048]{1,0:T(8,128)(2,1)} %get-tuple-element.405, bf16[256,2048]{1,0:T(8,128)(2,1)} %get-tuple-element.404), kind=kOutput, calls=%fused_computation.81 | convolution fusion | flops 4299685888 | bytes 19922944 | tf_op jit(solution)/shard_map/dot_general | solution.py:53
  464.7 11.1 %shard_map.237 = bf16[2048,2048]{1,0:T(8,128)(2,1)} custom-call(bf16[1024,2048]{1,0:T(8,128)(2,1)S(1)} %pad_maximum_fusion.left_ref, bf16[1024,2048]{1,0:T(8,128)(2,1)S(1)} %copy-done.3), custom_call_target="tpu_custom_call" | custom-call | flops 1 | bytes 1 | tf_op jit(solution)/shard_map/pallas_call | solution.py:71
  480.9 10.0 %multiply_convert_fusion.3 = (bf16[512,2048]{1,0:T(8,128)(2,1)}, bf16[512,2048]{1,0:T(8,128)(2,1)}) fusion(bf16[1024,2048]{1,0:T(8,128)(2,1)S(1)} %copy-done.43, bf16[1024,2048]{1,0:T(8,128)(2,1)S(1)} %copy-done.44, bf16[512,2048]{1,0:T(8,128)(2,1)S(1)} %pad_maximum_fusion.7, bf16[2048,6144]{1,0:T(8,128)(2,1)} %all-gather.5.cloned.1.call-done), kind=kOutput, calls=%fused_computation.51 | convolution fusion | flops 4301258752 | bytes 18874368 | tf_op jit(solution)/shard_map/dot_general | solution.py:49
  491.0 15.0 %fusion.36 = bf16[512,2048]{1,0:T(8,128)(2,1)} fusion(bf16[2048,6144]{1,0:T(8,128)(2,1)} %all-gather.5.cloned.1.call-done, bf16[512,2048]{1,0:T(8,128)(2,1)} %get-tuple-element.379, bf16[512,2048]{1,0:T(8,128)(2,1)} %get-tuple-element.378), kind=kOutput, calls=%fused_computation.74 | convolution fusion | flops 8599371776 | bytes 23068672 | tf_op jit(solution)/shard_map/dot_general | solution.py:53
  513.7 11.1 %fusion.42 = bf16[256,2048]{1,0:T(8,128)(2,1)S(1)} fusion(bf16[2048,6144]{1,0:T(8,128)(2,1)} %all-gather.5.cloned.1.call-done, bf16[256,2048]{1,0:T(8,128)(2,1)} %get-tuple-element.403, bf16[256,2048]{1,0:T(8,128)(2,1)} %get-tuple-element.402), kind=kOutput, calls=%fused_computation.82 | convolution fusion | flops 4299685888 | bytes 19922944 | tf_op jit(solution)/shard_map/dot_general | solution.py:53
  539.8 12.1 %shard_map.238 = bf16[2048,2048]{1,0:T(8,128)(2,1)S(1)} custom-call(bf16[1024,2048]{1,0:T(8,128)(2,1)} %constant_dynamic-update-slice_fusion.3.left_ref, bf16[1024,4096]{1,0:T(8,128)(2,1)} %copy-done.6), custom_call_target="tpu_custom_call" | custom-call | flops 1 | bytes 1 | tf_op jit(solution)/shard_map/pallas_call | solution.py:71
  561.9 12.1 %shard_map.239 = bf16[2048,2048]{1,0:T(8,128)(2,1)S(1)} custom-call(bf16[1024,2048]{1,0:T(8,128)(2,1)} %constant_dynamic-update-slice_fusion.3.left_ref, bf16[1024,4096]{1,0:T(8,128)(2,1)} %copy-done.6), custom_call_target="tpu_custom_call" | custom-call | flops 1 | bytes 1 | tf_op jit(solution)/shard_map/pallas_call | solution.py:71
  612.0 11.7 %fusion.19 = bf16[4,512,1024]{1,2,0:T(8,128)(2,1)} fusion(f32[1024,512,4]{1,0,2:T(8,128)} %copy-done.9, f32[4,512]{1,0:T(4,128)S(1)} %log_add_fusion, pred[512,1024]{0,1:T(8,128)(4,1)S(1)} %copy-done.31, bf16[512,4,256]{0,2,1:T(8,128)(2,1)} %copy.157, bf16[1024,512]{1,0:T(8,128)(2,1)} %copy-done.62), kind=kOutput, calls=%fused_computation.22 | convolution fusion | flops 2168458240 | bytes 25182208 | tf_op jit(solution)/shard_map/sub | solution.py:616
  650.4 15.4 %collective-permute-done.42 = bf16[256,512]{0,1:T(8,128)(2,1)} collective-permute-done((bf16[256,512]{0,1:T(8,128)(2,1)S(1)}, bf16[256,512]{0,1:T(8,128)(2,1)}, u32[]{:S(2)}, u32[]{:S(2)}) %collective-permute-start.42) | collective-permute-done | bytes 262176 | tf_op jit(solution)/shard_map/ppermute | solution.py:104
  671.5 21.1 %collective-permute-done.41 = bf16[512,512]{1,0:T(8,128)(2,1)} collective-permute-done((bf16[512,512]{1,0:T(8,128)(2,1)}, bf16[512,512]{1,0:T(8,128)(2,1)}, u32[]{:S(2)}, u32[]{:S(2)}) %collective-permute-start.41) | collective-permute-done | bytes 524320 | tf_op jit(solution)/shard_map/ppermute | solution.py:631
  759.2 18.9 %collective-permute-done.53 = bf16[256,2048]{1,0:T(8,128)(2,1)} collective-permute-done((bf16[256,2048]{1,0:T(8,128)(2,1)}, bf16[256,2048]{1,0:T(8,128)(2,1)}, u32[]{:S(2)}, u32[]{:S(2)}) %collective-permute-start.53) | collective-permute-done | bytes 1048608 | tf_op jit(solution)/shard_map/ppermute | solution.py:104
  848.7 22.6 %collective-permute-start.65 = (f32[50,256]{1,0:T(8,128)S(1)}, f32[50,256]{1,0:T(8,128)S(1)}, u32[]{:S(2)}, u32[]{:S(2)}) collective-permute-start(f32[50,256]{1,0:T(8,128)S(1)} %add_add_fusion.9), channel_id=1, source_target_pairs={{0,4},{4,0},{1,5},{5,1},{2,6},{6,2},{3,7},{7,3},{8,12},{12,8},{9,1... | collective-permute-start | bytes 153608 | tf_op jit(solution)/shard_map/ppermute | solution.py:104
  (716 shorter events, 458.5 us)
Async XLA Ops:
  7.2 73.7 %all-gather.3.cloned.1.call-start = ((), (), s32[]{:S(2)}) async-start(), calls=%async_computation.5 | async-start | bytes 7077888 | tf_op jit(solution)/shard_map/all_gather | solution.py:313
  13.2 301.6 %all-gather.5.cloned.1.call-start = ((), (), s32[]{:S(2)}) async-start(), calls=%async_computation.6 | async-start | bytes 28311552 | tf_op jit(solution)/shard_map/all_gather | solution.py:346
  84.8 391.0 %reduce-scatter.6.cloned.1.call-start = ((), (), s32[]{:S(2)}) async-start(), calls=%async_computation.7 | async-start | bytes 2359296 | tf_op jit(solution)/shard_map/reduce_scatter | solution.py:515
  86.0 36.5 %collective-permute-start.2 = (bf16[2048,384]{1,0:T(8,128)(2,1)S(1)}, bf16[2048,384]{1,0:T(8,128)(2,1)S(1)}, u32[]{:S(2)}, u32[]{:S(2)}) collective-permute-start(bf16[2048,384]{1,0:T(8,128)(2,1)S(1)} %constant_dynamic-slice_fusion.1), channel_id=1, source_target_pairs={{0,16},{16,0},{1,17},{17,1},{2,18},{18,2},{3,19},{19,3},{4,20},{20... | collective-permute-start | bytes 4718600 | tf_op jit(solution)/shard_map/ppermute | solution.py:104
  87.5 36.3 %collective-permute-start.3 = (bf16[2048,384]{1,0:T(8,128)(2,1)S(1)}, bf16[2048,384]{1,0:T(8,128)(2,1)S(1)}, u32[]{:S(2)}, u32[]{:S(2)}) collective-permute-start(bf16[2048,384]{1,0:T(8,128)(2,1)S(1)} %constant_dynamic-slice_fusion.1), channel_id=1, source_target_pairs={{0,8},{8,0},{1,9},{9,1},{2,10},{10,2},{3,11},{11,3},{4,12},{12,4},... | collective-permute-start | bytes 4718600 | tf_op jit(solution)/shard_map/ppermute | solution.py:104
  143.0 37.6 %collective-permute-start.7 = (bf16[2048,256]{1,0:T(8,128)(2,1)}, bf16[2048,256]{1,0:T(8,128)(2,1)}, u32[]{:S(2)}, u32[]{:S(2)}) collective-permute-start(bf16[2048,256]{1,0:T(8,128)(2,1)} %constant_dynamic-slice_fusion), channel_id=1, source_target_pairs={{0,16},{16,0},{1,17},{17,1},{2,18},{18,2},{3,19},{19,3},{4,20},{20... | collective-permute-start | bytes 3145736 | tf_op jit(solution)/shard_map/ppermute | solution.py:104
  144.5 36.2 %collective-permute-start.8 = (bf16[2048,256]{1,0:T(8,128)(2,1)}, bf16[2048,256]{1,0:T(8,128)(2,1)}, u32[]{:S(2)}, u32[]{:S(2)}) collective-permute-start(bf16[2048,256]{1,0:T(8,128)(2,1)} %constant_dynamic-slice_fusion), channel_id=1, source_target_pairs={{0,8},{8,0},{1,9},{9,1},{2,10},{10,2},{3,11},{11,3},{4,12},{12,4},... | collective-permute-start | bytes 3145736 | tf_op jit(solution)/shard_map/ppermute | solution.py:104
  256.5 35.4 %collective-permute-start.16 = (bf16[256,2048]{1,0:T(8,128)(2,1)S(1)}, bf16[256,2048]{1,0:T(8,128)(2,1)S(1)}, u32[]{:S(2)}, u32[]{:S(2)}) collective-permute-start(bf16[256,2048]{1,0:T(8,128)(2,1)S(1)} %slice.561), channel_id=1, source_target_pairs={{0,16},{16,0},{1,17},{17,1},{2,18},{18,2},{3,19},{19,3},{4,20},{20... | collective-permute-start | bytes 3145736 | tf_op jit(solution)/shard_map/ppermute | solution.py:104
  257.9 34.0 %collective-permute-start.17 = (bf16[256,2048]{1,0:T(8,128)(2,1)S(1)}, bf16[256,2048]{1,0:T(8,128)(2,1)S(1)}, u32[]{:S(2)}, u32[]{:S(2)}) collective-permute-start(bf16[256,2048]{1,0:T(8,128)(2,1)S(1)} %slice.561), channel_id=1, source_target_pairs={{0,8},{8,0},{1,9},{9,1},{2,10},{10,2},{3,11},{11,3},{4,12},{12,4},... | collective-permute-start | bytes 3145736 | tf_op jit(solution)/shard_map/ppermute | solution.py:104
  260.5 30.3 %collective-permute-start.18 = (bf16[2048,128]{1,0:T(8,128)(2,1)S(1)}, bf16[2048,128]{1,0:T(8,128)(2,1)S(1)}, u32[]{:S(2)}, u32[]{:S(2)}) collective-permute-start(bf16[2048,128]{1,0:T(8,128)(2,1)S(1)} %slice.467), channel_id=1, source_target_pairs={{0,16},{16,0},{1,17},{17,1},{2,18},{18,2},{3,19},{19,3},{4,20},{20... | collective-permute-start | bytes 1572872 | tf_op jit(solution)/shard_map/ppermute | solution.py:104
  261.2 30.8 %collective-permute-start.19 = (bf16[2048,128]{1,0:T(8,128)(2,1)S(1)}, bf16[2048,128]{1,0:T(8,128)(2,1)S(1)}, u32[]{:S(2)}, u32[]{:S(2)}) collective-permute-start(bf16[2048,128]{1,0:T(8,128)(2,1)S(1)} %slice.467), channel_id=1, source_target_pairs={{0,8},{8,0},{1,9},{9,1},{2,10},{10,2},{3,11},{11,3},{4,12},{12,4},... | collective-permute-start | bytes 1572872 | tf_op jit(solution)/shard_map/ppermute | solution.py:104
  359.0 27.0 %collective-permute-start.28 = (bf16[3,256,2048]{2,1,0:T(8,128)(2,1)S(1)}, bf16[3,256,2048]{2,1,0:T(8,128)(2,1)}, u32[]{:S(2)}, u32[]{:S(2)}) collective-permute-start(bf16[3,256,2048]{2,1,0:T(8,128)(2,1)S(1)} %pad_maximum_fusion.3), channel_id=1, source_target_pairs={{0,1},{1,0},{2,3},{3,2},{4,5},{5,4},{6,7},{7,6},{8,9},{9,8},{10,11... | collective-permute-start | bytes 9437192 | tf_op jit(solution)/shard_map/ppermute | solution.py:104
  415.5 228.7 %reduce-scatter.8.cloned.1.call-start = ((), (), s32[]{:S(2)}) async-start(), calls=%async_computation.8 | async-start | bytes 9437184 | tf_op jit(solution)/shard_map/reduce_scatter | solution.py:564
  475.8 276.4 %reduce-scatter.10.cloned.1.call-start = ((), (), s32[]{:S(2)}) async-start(), calls=%async_computation.9 | async-start | bytes 9437184 | tf_op jit(solution)/shard_map/reduce_scatter | solution.py:564
  555.2 253.4 %reduce-scatter.14.cloned.1.call-start = ((), (), s32[]{:S(2)}) async-start(), calls=%async_computation.11 | async-start | bytes 9437184 | tf_op jit(solution)/shard_map/reduce_scatter | solution.py:564
  577.4 268.7 %reduce-scatter.12.cloned.1.call-start = ((), (), s32[]{:S(2)}) async-start(), calls=%async_computation.10 | async-start | bytes 6488064 | tf_op jit(solution)/shard_map/reduce_scatter | solution.py:682
  633.8 58.8 %collective-permute-start.44 = (bf16[2048,256]{1,0:T(8,128)(2,1)}, bf16[2048,256]{1,0:T(8,128)(2,1)}, u32[]{:S(2)}, u32[]{:S(2)}) collective-permute-start(bf16[2048,256]{1,0:T(8,128)(2,1)} %pad_maximum_fusion.23), channel_id=1, source_target_pairs={{0,8},{8,0},{1,9},{9,1},{2,10},{10,2},{3,11},{11,3},{4,12},{12,4},... | collective-permute-start | bytes 3145736 | tf_op jit(solution)/shard_map/ppermute | solution.py:104
  636.5 56.2 %collective-permute-start.43 = (bf16[2048,256]{1,0:T(8,128)(2,1)}, bf16[2048,256]{1,0:T(8,128)(2,1)}, u32[]{:S(2)}, u32[]{:S(2)}) collective-permute-start(bf16[2048,256]{1,0:T(8,128)(2,1)} %pad_maximum_fusion.22), channel_id=1, source_target_pairs={{0,16},{16,0},{1,17},{17,1},{2,18},{18,2},{3,19},{19,3},{4,20},{20... | collective-permute-start | bytes 3145736 | tf_op jit(solution)/shard_map/ppermute | solution.py:104
  637.9 27.9 %collective-permute-start.42 = (bf16[256,512]{0,1:T(8,128)(2,1)S(1)}, bf16[256,512]{0,1:T(8,128)(2,1)}, u32[]{:S(2)}, u32[]{:S(2)}) collective-permute-start(bf16[256,512]{0,1:T(8,128)(2,1)S(1)} %add_convert_fusion.9), channel_id=1, source_target_pairs={{0,8},{8,0},{1,9},{9,1},{2,10},{10,2},{3,11},{11,3},{4,12},{12,4},... | collective-permute-start | bytes 786440 | tf_op jit(solution)/shard_map/ppermute | solution.py:104
  644.2 48.5 %collective-permute-start.45 = (bf16[256,2048]{1,0:T(8,128)(2,1)}, bf16[256,2048]{1,0:T(8,128)(2,1)}, u32[]{:S(2)}, u32[]{:S(2)}) collective-permute-start(bf16[256,2048]{1,0:T(8,128)(2,1)} %reduce-scatter.8.cloned.1.call-done), channel_id=1, source_target_pairs={{0,16},{16,0},{1,17},{17,1},{2,18},{18,2},{3,19},{19,3},{4,20},{20... | collective-permute-start | bytes 3145736 | tf_op jit(solution)/shard_map/ppermute | solution.py:104
  644.9 47.8 %collective-permute-start.46 = (bf16[256,2048]{1,0:T(8,128)(2,1)}, bf16[256,2048]{1,0:T(8,128)(2,1)}, u32[]{:S(2)}, u32[]{:S(2)}) collective-permute-start(bf16[256,2048]{1,0:T(8,128)(2,1)} %reduce-scatter.8.cloned.1.call-done), channel_id=1, source_target_pairs={{0,8},{8,0},{1,9},{9,1},{2,10},{10,2},{3,11},{11,3},{4,12},{12,4},... | collective-permute-start | bytes 3145736 | tf_op jit(solution)/shard_map/ppermute | solution.py:104
  752.2 26.9 %collective-permute-start.52 = (f32[256,2048]{1,0:T(8,128)}, f32[256,2048]{1,0:T(8,128)}, u32[]{:S(2)}, u32[]{:S(2)}) collective-permute-start(f32[256,2048]{1,0:T(8,128)} %slice.613), channel_id=1, source_target_pairs={{0,1},{1,0},{2,3},{3,2},{4,5},{5,4},{6,7},{7,6},{8,9},{9,8},{10,11... | collective-permute-start | bytes 6291464 | tf_op jit(solution)/shard_map/ppermute | solution.py:104
  847.3 31.0 %collective-permute-start.68 = (bf16[256,1280]{0,1:T(8,128)(2,1)S(1)}, bf16[256,1280]{0,1:T(8,128)(2,1)S(1)}, u32[]{:S(2)}, u32[]{:S(2)}) collective-permute-start(bf16[256,1280]{0,1:T(8,128)(2,1)S(1)} %slice.528), channel_id=1, source_target_pairs={{0,16},{16,0},{1,17},{17,1},{2,18},{18,2},{3,19},{19,3},{4,20},{20... | collective-permute-start | bytes 1966088 | tf_op jit(solution)/shard_map/ppermute | solution.py:104
  848.3 30.0 %collective-permute-start.69 = (bf16[256,1280]{0,1:T(8,128)(2,1)S(1)}, bf16[256,1280]{0,1:T(8,128)(2,1)S(1)}, u32[]{:S(2)}, u32[]{:S(2)}) collective-permute-start(bf16[256,1280]{0,1:T(8,128)(2,1)S(1)} %slice.528), channel_id=1, source_target_pairs={{0,8},{8,0},{1,9},{9,1},{2,10},{10,2},{3,11},{11,3},{4,12},{12,4},... | collective-permute-start | bytes 1966088 | tf_op jit(solution)/shard_map/ppermute | solution.py:104
  (203 other events, 2562.5 us)
Sparse Core Ops, SparseCore 0:
  13.4 67.4 all-gather.2
  84.9 223.8 all-gather.4
  415.6 52.8 reduce-scatter.5
  476.0 107.2 reduce-scatter.7
  585.3 87.9 reduce-scatter.9
  675.5 99.1 reduce-scatter.13
  777.0 62.3 reduce-scatter.11
